TPU v7x, 32 devices: a whole 2x2x4 slice. The times are simulated.
32 devices in a mesh: row: 16 (over z, y, x), mem: 2 (over core).
Axes of the slice: x: 2, y: 2, z: 4, core: 2. Of those that a mesh axis runs over, the one named last changes fastest.
Arguments:
- inputs: bfloat16 [16384, 1024], P(('row', 'mem')), may hold values from -6 to 6
- memory: bfloat16 [8192, 1024], P(('row', 'mem')), may hold values from -6 to 6
- target_seg: int32 [16384], P(('row', 'mem')), may hold values from 0 to 7, as said below
- memory_seg: int32 [8192], P(('row', 'mem')), may hold values from 0 to 7, as said below
- self_query: bfloat16 [1024, 1024], replicated, may hold values from -0.1875 to 0.1875
- self_key: bfloat16 [1024, 1024], replicated, may hold values from -0.1875 to 0.1875
- self_value: bfloat16 [1024, 1024], replicated, may hold values from -0.1875 to 0.1875
- self_out: bfloat16 [1024, 1024], replicated, may hold values from -1.5 to 1.5
- cross_query: bfloat16 [1024, 1024], replicated, may hold values from -0.1875 to 0.1875
- cross_key: bfloat16 [1024, 1024], replicated, may hold values from -0.1875 to 0.1875
- cross_value: bfloat16 [1024, 1024], replicated, may hold values from -0.1875 to 0.1875
- cross_out: bfloat16 [1024, 1024], replicated, may hold values from -3 to 3
- expand_weight: bfloat16 [1024, 4096], replicated, may hold values from -0.1875 to 0.1875
- contract_weight: bfloat16 [4096, 1024], replicated, may hold values from -0.5 to 0.5
- norm_params: float32 [6, 1024], replicated, may hold values from -3 to 3, as said below
- out_grad: bfloat16 [16384, 1024], P(('row', 'mem')), may hold values from -6 to 6
Outputs:
- layer_out: bfloat16 [16384, 1024], P(('row', 'mem'))
- input_grad: bfloat16 [16384, 1024], P(('row', 'mem'))
- memory_grad: bfloat16 [8192, 1024], P(('row', 'mem'))
- self_query_grad: float32 [1024, 1024], P('row', 'mem')
- self_key_grad: float32 [1024, 1024], P('row', 'mem')
- self_value_grad: float32 [1024, 1024], P('row', 'mem')
- self_out_grad: float32 [1024, 1024], P('row', 'mem')
- cross_query_grad: float32 [1024, 1024], P('row', 'mem')
- cross_key_grad: float32 [1024, 1024], P('row', 'mem')
- cross_value_grad: float32 [1024, 1024], P('row', 'mem')
- cross_out_grad: float32 [1024, 1024], P('row', 'mem')
- expand_weight_grad: float32 [1024, 4096], P('row', 'mem')
- contract_weight_grad: float32 [4096, 1024], P('row', 'mem')
- norm_grad: float32 [6, 1024], P('mem', 'row')
Inputs may be any that keep to these rules, and one draw needn't show every extreme that they name: `target_seg`: the rows of each device hold 4 whole target sequences one after another; ids count the sequences of the devices of one index of row from 0 upward in row order. `memory_seg`: within one index of row, memory ids never fall and every target sequence of that index has one memory row or more with its id; no memory sequence but the first of an index begins at a device's first memory row. `norm_params`: rows 0, 2, 4 are positive gains, rows 1, 3, 5 biases.
All inputs are finite; a program needn't handle non-finite values.
Results may differ from a plain program's by a relative error of at most 0.025.
Values may be sent and summed in bfloat16 or wider, within the bound.
No kernel may reach another device: no remote copies, remote signals or barrier semaphores. Data moves between devices by JAX's collectives and lax.ppermute only.
A program may use at most 256 MiB of HBM per device.

v0:
```python
from functools import partial

import jax
import jax.numpy as jnp
from jax import lax
from jax.sharding import PartitionSpec as P

HEADS = 16
HEAD_DIM = 64


ALPHA = 300.0**0.25
SCALE = 0.125
NEG = -1e30
EPS = 1e-05


def layer_norm(tensor, gain_row, bias_row):
    middle = jnp.mean(tensor, -1, keepdims=True)
    centred = tensor - middle
    spread = jnp.mean(centred * centred, -1, keepdims=True)
    return centred * lax.rsqrt(spread + EPS) * gain_row + bias_row


def gelu_exact(tensor):
    return jax.nn.gelu(tensor, approximate=False)


def project(left_side, right_side):
    return jnp.dot(left_side, right_side, preferred_element_type=jnp.float32)


def weight_grad(left_side, right_side):
    return jnp.einsum("rd,re->de", left_side, right_side, preferred_element_type=jnp.float32)


def back_project(grad_rows, weight):
    return jnp.einsum("re,de->rd", grad_rows, weight, preferred_element_type=jnp.float32)


def split_heads(tensor):
    return tensor.reshape(tensor.shape[0], HEADS, HEAD_DIM)


def join_heads(tensor):
    return tensor.reshape(tensor.shape[0], HEADS * HEAD_DIM)


def to_blocks(tensor, block_rows):
    return tensor.reshape((tensor.shape[0] // block_rows, block_rows) + tensor.shape[1:])


def masked_scores(query_block, key_heads, row_seg, key_seg, row_pos, key_pos):
    raw_scores = (
        jnp.einsum("qhd,khd->hqk", query_block, key_heads, preferred_element_type=jnp.float32)
        * SCALE
    )
    allowed = row_seg[:, None] == key_seg[None, :]
    if row_pos is not None:
        allowed = allowed & (row_pos[:, None] >= key_pos[None, :])
    return jnp.where(allowed[None], raw_scores, NEG)


def self_forward(queries, key_heads, value_heads, segments):
    row_count = queries.shape[0]
    positions = jnp.arange(row_count, dtype=jnp.int32)
    scores = masked_scores(queries, key_heads, segments, segments, positions, positions)
    row_top = jnp.max(scores, -1, keepdims=True)
    log_total = row_top + jnp.log(jnp.sum(jnp.exp(scores - row_top), -1, keepdims=True))
    prob_block = jnp.exp(scores - log_total).astype(jnp.bfloat16)
    outputs = jnp.einsum(
        "hqk,khd->qhd", prob_block, value_heads, preferred_element_type=jnp.float32
    )
    return (outputs, log_total)


def self_backward(queries, key_heads, value_heads, segments, log_totals, grad_heads):
    row_count = queries.shape[0]
    block_rows = min(512, row_count)
    positions = jnp.arange(row_count, dtype=jnp.int32)
    key_sum = jnp.zeros(key_heads.shape, jnp.float32)
    value_sum = jnp.zeros(value_heads.shape, jnp.float32)
    scores = masked_scores(queries, key_heads, segments, segments, positions, positions)
    prob_block = jnp.exp(scores - log_totals)
    grad_probs = jnp.einsum(
        "qhd,khd->hqk", grad_heads, value_heads, preferred_element_type=jnp.float32
    )
    row_delta = jnp.sum(prob_block * grad_probs, -1, keepdims=True)
    grad_scores = (prob_block * (grad_probs - row_delta)).astype(jnp.bfloat16)
    query_parts = (
        jnp.einsum("hqk,khd->qhd", grad_scores, key_heads, preferred_element_type=jnp.float32)
        * SCALE
    )
    key_sum = key_sum.at[:block_rows].add(
        jnp.einsum("hqk,qhd->khd", grad_scores, queries, preferred_element_type=jnp.float32) * SCALE
    )
    value_sum = value_sum.at[:block_rows].add(
        jnp.einsum(
            "hqk,qhd->khd",
            prob_block.astype(jnp.bfloat16),
            grad_heads,
            preferred_element_type=jnp.float32,
        )
    )
    return (query_parts, key_sum, value_sum)


def block_top(block_items, key_heads, key_seg):
    query_block, seg_block = block_items
    return jnp.max(masked_scores(query_block, key_heads, seg_block, key_seg, None, None), -1)


def block_total(block_items, key_heads, key_seg):
    query_block, seg_block, row_top = block_items
    scores = masked_scores(query_block, key_heads, seg_block, key_seg, None, None)
    return jnp.sum(jnp.exp(scores - row_top[..., None]), -1)


def block_output(block_items, key_heads, value_heads, key_seg):
    query_block, seg_block, log_total = block_items
    scores = masked_scores(query_block, key_heads, seg_block, key_seg, None, None)
    prob_block = jnp.exp(scores - log_total[..., None]).astype(jnp.bfloat16)
    return jnp.einsum("hqk,khd->qhd", prob_block, value_heads, preferred_element_type=jnp.float32)


def block_delta(block_items, key_heads, value_heads, key_seg):
    query_block, seg_block, log_total, grad_block = block_items
    scores = masked_scores(query_block, key_heads, seg_block, key_seg, None, None)
    prob_block = jnp.exp(scores - log_total[..., None])
    grad_probs = jnp.einsum(
        "qhd,khd->hqk", grad_block, value_heads, preferred_element_type=jnp.float32
    )
    return jnp.sum(prob_block * grad_probs, -1)


def block_grads(carry, block_items, key_heads, value_heads, key_seg):
    key_sum, value_sum = carry
    query_block, seg_block, log_total, grad_block, row_delta = block_items
    scores = masked_scores(query_block, key_heads, seg_block, key_seg, None, None)
    prob_block = jnp.exp(scores - log_total[..., None])
    grad_probs = jnp.einsum(
        "qhd,khd->hqk", grad_block, value_heads, preferred_element_type=jnp.float32
    )
    grad_scores = (prob_block * (grad_probs - row_delta[..., None])).astype(jnp.bfloat16)
    query_part = (
        jnp.einsum("hqk,khd->qhd", grad_scores, key_heads, preferred_element_type=jnp.float32)
        * SCALE
    )
    key_sum = (
        key_sum
        + jnp.einsum("hqk,qhd->khd", grad_scores, query_block, preferred_element_type=jnp.float32)
        * SCALE
    )
    value_sum = value_sum + jnp.einsum(
        "hqk,qhd->khd",
        prob_block.astype(jnp.bfloat16),
        grad_block,
        preferred_element_type=jnp.float32,
    )
    return ((key_sum, value_sum), query_part)


def shards(
    inputs,
    memory,
    target_seg,
    memory_seg,
    self_query,
    self_key,
    self_value,
    self_out,
    cross_query,
    cross_key,
    cross_value,
    cross_out,
    expand_weight,
    contract_weight,
    norm_params,
    out_grad,
):
    inputs_wide = inputs.astype(jnp.float32)
    queries = split_heads(project(inputs, self_query).astype(jnp.bfloat16))
    key_rows = split_heads(project(inputs, self_key).astype(jnp.bfloat16))
    value_rows = split_heads(project(inputs, self_value).astype(jnp.bfloat16))
    attended, self_totals = self_forward(queries, key_rows, value_rows, target_seg)
    attended_low = join_heads(attended).astype(jnp.bfloat16)
    first_sum = ALPHA * inputs_wide + project(attended_low, self_out)
    hidden_one, norm_back_one = jax.vjp(layer_norm, first_sum, norm_params[0], norm_params[1])
    hidden_one_low = hidden_one.astype(jnp.bfloat16)
    cross_queries = project(hidden_one_low, cross_query).astype(jnp.bfloat16)
    memory_keys = project(memory, cross_key).astype(jnp.bfloat16)
    memory_values = project(memory, cross_value).astype(jnp.bfloat16)
    pair_queries, pair_seg = (
        lax.all_gather(cross_queries, "mem", axis=0, tiled=True),
        lax.all_gather(target_seg.astype(jnp.bfloat16), "mem", axis=0, tiled=True),
    )
    key_heads = split_heads(memory_keys)
    value_heads = split_heads(memory_values)
    pair_rows = pair_queries.shape[0]
    block_rows = min(512, pair_rows)
    query_blocks = to_blocks(split_heads(pair_queries), block_rows)
    seg_blocks = to_blocks(pair_seg.astype(jnp.int32), block_rows)
    local_top = lax.map(
        partial(block_top, key_heads=key_heads, key_seg=memory_seg), (query_blocks, seg_blocks)
    )
    row_top = lax.pmax(local_top.astype(jnp.bfloat16), "mem").astype(local_top.dtype)
    local_total = lax.map(
        partial(block_total, key_heads=key_heads, key_seg=memory_seg),
        (query_blocks, seg_blocks, row_top),
    )
    row_total = lax.psum(local_total.astype(jnp.bfloat16), "mem").astype(jnp.float32)
    log_total = row_top + jnp.log(row_total)
    partial_out = lax.map(
        partial(block_output, key_heads=key_heads, value_heads=value_heads, key_seg=memory_seg),
        (query_blocks, seg_blocks, log_total),
    )
    cross_values = lax.psum_scatter(
        partial_out.reshape(pair_rows, HEADS * HEAD_DIM).astype(jnp.bfloat16),
        "mem",
        scatter_dimension=0,
        tiled=True,
    )
    second_sum = ALPHA * hidden_one + project(cross_values, cross_out)
    hidden_two, norm_back_two = jax.vjp(layer_norm, second_sum, norm_params[2], norm_params[3])
    hidden_two_low = hidden_two.astype(jnp.bfloat16)
    pre_active = project(hidden_two_low, expand_weight)
    activated, gelu_back = jax.vjp(gelu_exact, pre_active)
    activated_low = activated.astype(jnp.bfloat16)
    third_sum = ALPHA * hidden_two + project(activated_low, contract_weight)
    layer_value, norm_back_three = jax.vjp(layer_norm, third_sum, norm_params[4], norm_params[5])
    layer_out = layer_value.astype(jnp.bfloat16)
    third_grad, gain_three, bias_three = norm_back_three(out_grad.astype(jnp.float32))
    branch_three = third_grad.astype(jnp.bfloat16)
    contract_back = weight_grad(activated_low, branch_three)
    (active_grad,) = gelu_back(back_project(branch_three, contract_weight))
    active_low = active_grad.astype(jnp.bfloat16)
    expand_back = weight_grad(hidden_two_low, active_low)
    hidden_two_grad = ALPHA * third_grad + back_project(active_low, expand_weight)
    second_grad, gain_two, bias_two = norm_back_two(hidden_two_grad)
    branch_two = second_grad.astype(jnp.bfloat16)
    cross_out_back = weight_grad(cross_values, branch_two)
    cross_grad = back_project(branch_two, cross_out).astype(jnp.bfloat16)
    zero_heads = jnp.zeros(key_heads.shape, jnp.float32)
    grad_pair = lax.all_gather(cross_grad, "mem", axis=0, tiled=True)
    grad_blocks = to_blocks(split_heads(grad_pair), block_rows)
    local_delta = lax.map(
        partial(block_delta, key_heads=key_heads, value_heads=value_heads, key_seg=memory_seg),
        (query_blocks, seg_blocks, log_total, grad_blocks),
    )
    row_delta = lax.psum(local_delta.astype(jnp.bfloat16), "mem").astype(jnp.float32)
    (key_sum, value_sum), query_parts = lax.scan(
        partial(block_grads, key_heads=key_heads, value_heads=value_heads, key_seg=memory_seg),
        (zero_heads, zero_heads),
        (query_blocks, seg_blocks, log_total, grad_blocks, row_delta),
    )
    query_sum = lax.psum_scatter(
        query_parts.reshape(pair_rows, HEADS * HEAD_DIM).astype(jnp.bfloat16),
        "mem",
        scatter_dimension=0,
        tiled=True,
    )
    memory_key_back = join_heads(key_sum).astype(jnp.bfloat16)
    memory_value_back = join_heads(value_sum).astype(jnp.bfloat16)
    cross_query_wgrad = weight_grad(hidden_one_low, query_sum)
    cross_key_wgrad = weight_grad(memory, memory_key_back)
    cross_value_wgrad = weight_grad(memory, memory_value_back)
    memory_grad = (
        back_project(memory_key_back, cross_key) + back_project(memory_value_back, cross_value)
    ).astype(jnp.bfloat16)
    hidden_one_grad = ALPHA * second_grad + back_project(query_sum, cross_query)
    first_grad, gain_one, bias_one = norm_back_one(hidden_one_grad)
    branch_one = first_grad.astype(jnp.bfloat16)
    self_out_wgrad = weight_grad(attended_low, branch_one)
    attended_grad = split_heads(back_project(branch_one, self_out).astype(jnp.bfloat16))
    query_heads_back, key_heads_back, value_heads_back = self_backward(
        queries, key_rows, value_rows, target_seg, self_totals, attended_grad
    )
    self_query_back = join_heads(query_heads_back).astype(jnp.bfloat16)
    self_key_back = join_heads(key_heads_back).astype(jnp.bfloat16)
    self_value_back = join_heads(value_heads_back).astype(jnp.bfloat16)
    self_query_wgrad = weight_grad(inputs, self_query_back)
    self_key_wgrad = weight_grad(inputs, self_key_back)
    self_value_wgrad = weight_grad(inputs, self_value_back)
    input_grad = (
        ALPHA * first_grad
        + back_project(self_query_back, self_query)
        + back_project(self_key_back, self_key)
        + back_project(self_value_back, self_value)
    ).astype(jnp.bfloat16)
    norm_wgrad = jnp.stack([gain_one, bias_one, gain_two, bias_two, gain_three, bias_three])
    row_parts = (
        lax.psum_scatter(self_query_wgrad, "row", scatter_dimension=0, tiled=True),
        lax.psum_scatter(self_key_wgrad, "row", scatter_dimension=0, tiled=True),
        lax.psum_scatter(self_value_wgrad, "row", scatter_dimension=0, tiled=True),
        lax.psum_scatter(self_out_wgrad, "row", scatter_dimension=0, tiled=True),
        lax.psum_scatter(cross_query_wgrad, "row", scatter_dimension=0, tiled=True),
        lax.psum_scatter(cross_key_wgrad, "row", scatter_dimension=0, tiled=True),
        lax.psum_scatter(cross_value_wgrad, "row", scatter_dimension=0, tiled=True),
        lax.psum_scatter(cross_out_back, "row", scatter_dimension=0, tiled=True),
        lax.psum_scatter(expand_back, "row", scatter_dimension=0, tiled=True),
        lax.psum_scatter(contract_back, "row", scatter_dimension=0, tiled=True),
        lax.psum_scatter(norm_wgrad, "row", scatter_dimension=1, tiled=True),
    )
    summed = (
        lax.psum_scatter(
            row_parts[0].astype(jnp.bfloat16), "mem", scatter_dimension=1, tiled=True
        ).astype(jnp.float32),
        lax.psum_scatter(
            row_parts[1].astype(jnp.bfloat16), "mem", scatter_dimension=1, tiled=True
        ).astype(jnp.float32),
        lax.psum_scatter(
            row_parts[2].astype(jnp.bfloat16), "mem", scatter_dimension=1, tiled=True
        ).astype(jnp.float32),
        lax.psum_scatter(
            row_parts[3].astype(jnp.bfloat16), "mem", scatter_dimension=1, tiled=True
        ).astype(jnp.float32),
        lax.psum_scatter(
            row_parts[4].astype(jnp.bfloat16), "mem", scatter_dimension=1, tiled=True
        ).astype(jnp.float32),
        lax.psum_scatter(
            row_parts[5].astype(jnp.bfloat16), "mem", scatter_dimension=1, tiled=True
        ).astype(jnp.float32),
        lax.psum_scatter(
            row_parts[6].astype(jnp.bfloat16), "mem", scatter_dimension=1, tiled=True
        ).astype(jnp.float32),
        lax.psum_scatter(
            row_parts[7].astype(jnp.bfloat16), "mem", scatter_dimension=1, tiled=True
        ).astype(jnp.float32),
        lax.psum_scatter(
            row_parts[8].astype(jnp.bfloat16), "mem", scatter_dimension=1, tiled=True
        ).astype(jnp.float32),
        lax.psum_scatter(
            row_parts[9].astype(jnp.bfloat16), "mem", scatter_dimension=1, tiled=True
        ).astype(jnp.float32),
        lax.psum_scatter(
            row_parts[10].astype(jnp.bfloat16), "mem", scatter_dimension=0, tiled=True
        ).astype(jnp.float32),
    )
    return (
        layer_out,
        input_grad,
        memory_grad,
        summed[0],
        summed[1],
        summed[2],
        summed[3],
        summed[4],
        summed[5],
        summed[6],
        summed[7],
        summed[8],
        summed[9],
        summed[10],
    )


def solution(mesh):
    in_specs = (
        P(("row", "mem"), None),
        P(("row", "mem"), None),
        P(("row", "mem")),
        P(("row", "mem")),
        P(),
        P(),
        P(),
        P(),
        P(),
        P(),
        P(),
        P(),
        P(),
        P(),
        P(),
        P(("row", "mem"), None),
    )
    out_specs = (
        P(("row", "mem"), None),
        P(("row", "mem"), None),
        P(("row", "mem"), None),
        P("row", "mem"),
        P("row", "mem"),
        P("row", "mem"),
        P("row", "mem"),
        P("row", "mem"),
        P("row", "mem"),
        P("row", "mem"),
        P("row", "mem"),
        P("row", "mem"),
        P("row", "mem"),
        P("mem", "row"),
    )
    return jax.shard_map(shards, mesh=mesh, in_specs=in_specs, out_specs=out_specs, check_vma=False)
```

profile of v0, /device:TPU:0, one launch (start us, length us, event | category | flops | bytes accessed | tf_op | source)
XLA Modules:
  0.0 1972.8 jit_solution(5078901319239515922)
XLA Ops:
  35.3 9.3 exponential_reduce_fusion.1
  106.2 12.2 while.61
  124.2 10.9 reduce-scatter.36.cloned.1.call-done
  139.7 27.7 %multiply_convert_fusion.2 = (bf16[512,4096]{1,0:T(8,128)(2,1)S(1)}, f32[512,4096]{1,0:T(8,128)}, f32[512,4096]{1,0:T(8,128)}) fusion(bf16[1024,4096]{1,0:T(8,128)(2,1)} %param.46, f32[512,1024]{1,0:T(8,128)S(1)} %get-tuple-element.605, f32[1024]{0:T(1024)S(1)} %bitcast.320, f32[1024]{0:T(1024)S(1)} %bitcast.306, f32[512]{0:T(512)S(1)} %fusion.74, ...), kind=kOutput, calls=%fused_computation.83 | convolution fusion | flops 4433903616 | bytes 31469568 | tf_op jit(solution)/shard_map/dot_general | solution.py:30
  178.7 15.2 add_convert_fusion
  193.9 9.6 multiply_reduce_fusion.2
  208.0 11.9 all-gather.6.cloned.1.call-done
  231.8 11.3 while.62
  248.6 26.7 %while.63 = (s32[]{:T(128)}, f32[256,16,64]{0,2,1:T(8,128)}, f32[256,16,64]{0,2,1:T(8,128)}, bf16[2,512,16,64]{1,3,2,0:T(8,128)(2,1)}, bf16[2,512,16,64]{1,3,2,0...) while((s32[]{:T(128)}, f32[256,16,64]{0,2,1:T(8,128)}, ...), condition=%wide.region_28.29_spmd.clone, body=%wide.region_27.28_spmd.clone.sunk | while | flops 1365114880 | bytes 102866352 | solution.py:251
  350.7 12.5 multiply_reduce_fusion.1
  363.2 12.4 multiply_convert_fusion.1
  406.3 13.4 fusion.84
  420.3 13.3 fusion.80
  437.2 50.1 %reduce-scatter.78.cloned.1.call-done = f32[64,1024]{1,0:T(8,128)} async-done(((f32[1024,1024]{1,0:T(8,128)}), f32[64,1024]{1,0:T(8,128)}) %reduce-scatter.78.cloned.1.call-update) | async-done | bytes 262160
  489.2 95.2 %reduce-scatter.76.cloned.1.call-done = f32[64,1024]{1,0:T(8,128)} async-done(((f32[1024,1024]{1,0:T(8,128)}), f32[64,1024]{1,0:T(8,128)}) %reduce-scatter.76.cloned.1.call-update) | async-done | bytes 262160
  586.3 95.2 %reduce-scatter.50.cloned.1.call-done = f32[64,1024]{1,0:T(8,128)} async-done(((f32[1024,1024]{1,0:T(8,128)}), f32[64,1024]{1,0:T(8,128)}) %reduce-scatter.50.cloned.1.call-update) | async-done | bytes 262160 | tf_op jit(solution)/shard_map/reduce_scatter | solution.py:296
  683.1 95.4 %reduce-scatter.46.cloned.1.call-done = f32[64,1024]{1,0:T(8,128)} async-done(((f32[1024,1024]{1,0:T(8,128)}), f32[64,1024]{1,0:T(8,128)}) %reduce-scatter.46.cloned.1.call-update) | async-done | bytes 262160 | tf_op jit(solution)/shard_map/reduce_scatter | solution.py:295
  780.2 95.2 %reduce-scatter.74.cloned.1.call-done = f32[64,1024]{1,0:T(8,128)} async-done(((f32[1024,1024]{1,0:T(8,128)}), f32[64,1024]{1,0:T(8,128)}) %reduce-scatter.74.cloned.1.call-update) | async-done | bytes 262160
  877.3 95.2 %reduce-scatter.70.cloned.1.call-done = f32[64,1024]{1,0:T(8,128)} async-done(((f32[1024,1024]{1,0:T(8,128)}), f32[64,1024]{1,0:T(8,128)}) %reduce-scatter.70.cloned.1.call-update) | async-done | bytes 262160
  974.3 95.0 %reduce-scatter.72.cloned.1.call-done = f32[64,1024]{1,0:T(8,128)} async-done(((f32[1024,1024]{1,0:T(8,128)}), f32[64,1024]{1,0:T(8,128)}) %reduce-scatter.72.cloned.1.call-update) | async-done | bytes 262160
  1071.2 346.4 %reduce-scatter.62.cloned.1.call-done = f32[64,4096]{1,0:T(8,128)} async-done(((f32[1024,4096]{1,0:T(8,128)}), f32[64,4096]{1,0:T(8,128)}) %reduce-scatter.62.cloned.1.call-update) | async-done | bytes 1048592 | tf_op jit(solution)/shard_map/reduce_scatter | solution.py:300
  1428.8 343.0 %reduce-scatter.66.cloned.1.call-done = f32[256,1024]{1,0:T(8,128)} async-done(((f32[4096,1024]{1,0:T(8,128)}), f32[256,1024]{1,0:T(8,128)}) %reduce-scatter.66.cloned.1.call-update) | async-done | bytes 1048592 | tf_op jit(solution)/shard_map/reduce_scatter | solution.py:301
  1780.3 75.9 %reduce-scatter.80.cloned.1.call-done = f32[64,6]{1,0:T(8,128)} async-done(((f32[1024,6]{1,0:T(8,128)}), f32[64,6]{1,0:T(8,128)}) %reduce-scatter.80.cloned.1.call-update) | async-done | bytes 1552
  1864.2 9.5 reduce-scatter.56.cloned.1.call-done
  1875.4 9.3 reduce-scatter.54.cloned.1.call-done
  1886.3 9.9 reduce-scatter.52.cloned.1.call-done
  1897.7 9.9 reduce-scatter.48.cloned.1.call-done
  1909.1 9.7 reduce-scatter.44.cloned.1.call-done
  1920.5 9.4 reduce-scatter.40.cloned.1.call-done
  1931.5 9.5 reduce-scatter.42.cloned.1.call-done
  1942.7 9.6 reduce-scatter.64.cloned.1.call-done
  1954.1 10.3 reduce-scatter.68.cloned.1.call-done
  (428 shorter events, 360.1 us)
Async XLA Ops:
  7.2 64.5 %all-gather.4.cloned.1.call-start = ((), (), s32[]{:S(2)}) async-start(), calls=%async_computation.23 | async-start | bytes 3145728 | tf_op jit(solution)/shard_map/all_gather | solution.py:194
  8.8 126.2 %copy-start.65 = (f32[1,1024]{1,0:T(1,128)}, f32[1,1024]{1,0:T(1,128)S(1)}, u32[]{:S(2)}) copy-start(f32[1,1024]{1,0:T(1,128)S(1)} %get-tuple-element.598) | copy-start | bytes 12292
  8.8 126.2 %copy-start.75 = (f32[1,1024]{1,0:T(1,128)}, f32[1,1024]{1,0:T(1,128)S(1)}, u32[]{:S(2)}) copy-start(f32[1,1024]{1,0:T(1,128)S(1)} %get-tuple-element.597) | copy-start | bytes 12292
  8.8 158.5 %copy-start.73 = (f32[1,1024]{1,0:T(1,128)}, f32[1,1024]{1,0:T(1,128)S(1)}, u32[]{:S(2)}) copy-start(f32[1,1024]{1,0:T(1,128)S(1)} %get-tuple-element.595) | copy-start | bytes 12292
  8.8 194.7 %copy-start.63 = (f32[1,1024]{1,0:T(1,128)}, f32[1,1024]{1,0:T(1,128)S(1)}, u32[]{:S(2)}) copy-start(f32[1,1024]{1,0:T(1,128)S(1)} %get-tuple-element.596) | copy-start | bytes 12292
  58.3 76.7 %reduce-scatter.36.cloned.1.call-start = ((), (), s32[]{:S(2)}) async-start(), calls=%async_computation.24 | async-start | bytes 3145728 | tf_op jit(solution)/shard_map/reduce_scatter | solution.py:217
  124.1 95.8 %all-gather.6.cloned.1.call-start = ((), (), s32[]{:S(2)}) async-start(), calls=%async_computation.25 | async-start | bytes 3145728 | tf_op jit(solution)/shard_map/all_gather | solution.py:244
  208.0 100.9 %reduce-scatter.38.cloned.1.call-start = ((), (), s32[]{:S(2)}) async-start(), calls=%async_computation.26 | async-start | bytes 3145728 | tf_op jit(solution)/shard_map/reduce_scatter | solution.py:256
  281.0 154.5 %reduce-scatter.58.cloned.1.call-start = ((), (), s32[]{:S(2)}) async-start(), calls=%async_computation.36 | async-start | bytes 4456448 | tf_op jit(solution)/shard_map/reduce_scatter | solution.py:299
  287.1 200.3 %reduce-scatter.78.cloned.1.call-start = ((), (), s32[]{:S(2)}) async-start(), calls=%async_computation.46 | async-start | bytes 4456448
  297.5 286.9 %reduce-scatter.76.cloned.1.call-start = ((), (), s32[]{:S(2)}) async-start(), calls=%async_computation.45 | async-start | bytes 4456448
  308.7 372.8 %reduce-scatter.50.cloned.1.call-start = ((), (), s32[]{:S(2)}) async-start(), calls=%async_computation.32 | async-start | bytes 4456448 | tf_op jit(solution)/shard_map/reduce_scatter | solution.py:296
  314.8 463.7 %reduce-scatter.46.cloned.1.call-start = ((), (), s32[]{:S(2)}) async-start(), calls=%async_computation.30 | async-start | bytes 4456448 | tf_op jit(solution)/shard_map/reduce_scatter | solution.py:295
  325.2 550.2 %reduce-scatter.74.cloned.1.call-start = ((), (), s32[]{:S(2)}) async-start(), calls=%async_computation.44 | async-start | bytes 4456448
  349.5 622.9 %reduce-scatter.70.cloned.1.call-start = ((), (), s32[]{:S(2)}) async-start(), calls=%async_computation.42 | async-start | bytes 4456448
  388.6 680.6 %reduce-scatter.72.cloned.1.call-start = ((), (), s32[]{:S(2)}) async-start(), calls=%async_computation.43 | async-start | bytes 4456448
  405.6 1012.0 %reduce-scatter.62.cloned.1.call-start = ((), (), s32[]{:S(2)}) async-start(), calls=%async_computation.38 | async-start | bytes 17825792 | tf_op jit(solution)/shard_map/reduce_scatter | solution.py:300
  419.7 1352.1 %reduce-scatter.66.cloned.1.call-start = ((), (), s32[]{:S(2)}) async-start(), calls=%async_computation.40 | async-start | bytes 17825792 | tf_op jit(solution)/shard_map/reduce_scatter | solution.py:301
  433.6 1422.5 %reduce-scatter.80.cloned.1.call-start = ((), (), s32[]{:S(2)}) async-start(), calls=%async_computation.47 | async-start | bytes 557056
  435.5 1427.2 %reduce-scatter.60.cloned.1.call-start = ((), (), s32[]{:S(2)}) async-start(), calls=%async_computation.37 | async-start | bytes 196608 | tf_op jit(solution)/shard_map/reduce_scatter | solution.py:326
  437.2 1436.5 %reduce-scatter.56.cloned.1.call-start = ((), (), s32[]{:S(2)}) async-start(), calls=%async_computation.35 | async-start | bytes 393216 | tf_op jit(solution)/shard_map/reduce_scatter | solution.py:323
  489.2 1395.5 %reduce-scatter.54.cloned.1.call-start = ((), (), s32[]{:S(2)}) async-start(), calls=%async_computation.34 | async-start | bytes 393216 | tf_op jit(solution)/shard_map/reduce_scatter | solution.py:320
  586.2 1310.0 %reduce-scatter.52.cloned.1.call-start = ((), (), s32[]{:S(2)}) async-start(), calls=%async_computation.33 | async-start | bytes 196608 | tf_op jit(solution)/shard_map/reduce_scatter | solution.py:317
  683.1 1224.5 %reduce-scatter.48.cloned.1.call-start = ((), (), s32[]{:S(2)}) async-start(), calls=%async_computation.31 | async-start | bytes 196608 | tf_op jit(solution)/shard_map/reduce_scatter | solution.py:314
  780.1 1138.7 %reduce-scatter.44.cloned.1.call-start = ((), (), s32[]{:S(2)}) async-start(), calls=%async_computation.29 | async-start | bytes 393216 | tf_op jit(solution)/shard_map/reduce_scatter | solution.py:311
  877.2 543.0 %copy-start.84 = (u32[32]{0:T(128)S(1)}, u32[32]{0:T(128)}, u32[]{:S(2)}) copy-start(u32[32]{0:T(128)} %constant.244) | copy-start | bytes 388
  877.2 544.3 %copy-start.18 = (bf16[256,16,64]{0,2,1:T(8,128)(2,1)S(1)}, bf16[256,16,64]{0,2,1:T(8,128)(2,1)}, u32[]{:S(2)}) copy-start(bf16[256,16,64]{0,2,1:T(8,128)(2,1)} %copy-done.17) | copy-start | bytes 1572868
  877.2 1052.7 %reduce-scatter.40.cloned.1.call-start = ((), (), s32[]{:S(2)}) async-start(), calls=%async_computation.27 | async-start | bytes 393216 | tf_op jit(solution)/shard_map/reduce_scatter | solution.py:305
  974.2 966.8 %reduce-scatter.42.cloned.1.call-start = ((), (), s32[]{:S(2)}) async-start(), calls=%async_computation.28 | async-start | bytes 393216 | tf_op jit(solution)/shard_map/reduce_scatter | solution.py:308
  1071.1 881.2 %reduce-scatter.64.cloned.1.call-start = ((), (), s32[]{:S(2)}) async-start(), calls=%async_computation.39 | async-start | bytes 786432 | tf_op jit(solution)/shard_map/reduce_scatter | solution.py:329
  1419.7 544.6 %reduce-scatter.68.cloned.1.call-start = ((), (), s32[]{:S(2)}) async-start(), calls=%async_computation.41 | async-start | bytes 786432 | tf_op jit(solution)/shard_map/reduce_scatter | solution.py:332
  1428.8 345.1 %copy-start.30 = (bf16[16,64,512]{2,1,0:T(8,128)(2,1)S(1)}, bf16[16,64,512]{2,1,0:T(8,128)(2,1)}, u32[]{:S(2)}) copy-start(bf16[16,64,512]{2,1,0:T(8,128)(2,1)} %copy-done.29) | copy-start | bytes 3145732
  (93 other events, 762.5 us)
Sparse Core Ops, SparseCore 0:
  58.4 13.2 all-gather.3
  124.2 10.7 reduce-scatter.35
  208.1 11.8 all-gather.5
  281.1 10.8 reduce-scatter.37
  294.2 96.2 reduce-scatter.57
  392.6 94.6 reduce-scatter.77
  489.7 94.6 reduce-scatter.75
  586.7 94.7 reduce-scatter.49
  683.7 94.7 reduce-scatter.45
  780.6 94.7 reduce-scatter.73
  877.7 94.6 reduce-scatter.69
  974.6 94.6 reduce-scatter.71
  1071.6 345.9 reduce-scatter.61
  1419.7 352.0 reduce-scatter.65
  1773.9 82.1 reduce-scatter.79
  1858.8 3.8 reduce-scatter.59
  1864.9 8.8 reduce-scatter.55
  1875.8 8.7 reduce-scatter.53
  1887.5 8.6 reduce-scatter.51
  1898.9 8.6 reduce-scatter.47
  1909.9 8.8 reduce-scatter.43
  1921.0 8.7 reduce-scatter.39
  1932.2 8.8 reduce-scatter.41
  1943.2 9.0 reduce-scatter.63
  1955.2 9.0 reduce-scatter.67
where the time goes:
time: 1980 us; the launch traced here: 1970 us
  waiting for transfers between devices  1500 us (76%)
  matrix products  266 us (13%)
  local copies, waits for them, and re-layouts  122 us (6%)
  other arithmetic  49.1 us (2%)
    unnamed x31, waiting for transfers between devices  507 us
    reduce_scatter x1, waiting for transfers between devices, shards(): lax.psum_scatter(expand_back, 'row', scatter_dimension=0, tiled=True)  346 us
    reduce_scatter x1, waiting for transfers between devices, shards(): lax.psum_scatter(contract_back, 'row', scatter_dimension=0, tiled=True)  343 us
    reduce_scatter x1, waiting for transfers between devices, shards(): lax.psum_scatter(self_out_wgrad, 'row', scatter_dimension=0, tiled=True)  95.4 us
    reduce_scatter x1, waiting for transfers between devices, shards(): lax.psum_scatter(cross_query_wgrad, 'row', scatter_dimension=0, tiled=True)  95.2 us
    unnamed x179, local copies, waits for them, and re-layouts  76.8 us
    dot_general x10, matrix products, project(): return jnp.dot(left_side, right_side, preferred_element_type=jnp.float32)  58.4 us
    dot_general x10, matrix products, weight_grad(): jnp.einsum('rd,re->de', left_side, right_side, preferred_element_type=jnp...  56.3 us
  transfers between devices with their start and end apart: 25, of which 23 were waited for; matrix products, arithmetic and copies ran while one was open for 10% of the time, Pallas kernels for 0%

commit v1 on v0

v1 whole, which is shorter than its diff:
```python
from functools import partial

import jax
import jax.numpy as jnp
from jax import lax
from jax.sharding import PartitionSpec as P

HEADS = 16
HEAD_DIM = 64


ALPHA = 300.0**0.25
SCALE = 0.125
NEG = -1e30
EPS = 1e-05


def layer_norm(tensor, gain_row, bias_row):
    middle = jnp.mean(tensor, -1, keepdims=True)
    centred = tensor - middle
    spread = jnp.mean(centred * centred, -1, keepdims=True)
    return centred * lax.rsqrt(spread + EPS) * gain_row + bias_row


def gelu_exact(tensor):
    return jax.nn.gelu(tensor, approximate=False)


def project(left_side, right_side):
    return jnp.dot(left_side, right_side, preferred_element_type=jnp.float32)


def weight_grad(left_side, right_side):
    return jnp.einsum("rd,re->de", left_side, right_side, preferred_element_type=jnp.float32)


def back_project(grad_rows, weight):
    return jnp.einsum("re,de->rd", grad_rows, weight, preferred_element_type=jnp.float32)


def split_heads(tensor):
    return tensor.reshape(tensor.shape[0], HEADS, HEAD_DIM)


def join_heads(tensor):
    return tensor.reshape(tensor.shape[0], HEADS * HEAD_DIM)


def to_blocks(tensor, block_rows):
    return tensor.reshape((tensor.shape[0] // block_rows, block_rows) + tensor.shape[1:])


def masked_scores(query_block, key_heads, row_seg, key_seg, row_pos, key_pos):
    raw_scores = (
        jnp.einsum("qhd,khd->hqk", query_block, key_heads, preferred_element_type=jnp.float32)
        * SCALE
    )
    allowed = row_seg[:, None] == key_seg[None, :]
    if row_pos is not None:
        allowed = allowed & (row_pos[:, None] >= key_pos[None, :])
    return jnp.where(allowed[None], raw_scores, NEG)


def self_forward(queries, key_heads, value_heads, segments):
    row_count = queries.shape[0]
    positions = jnp.arange(row_count, dtype=jnp.int32)
    scores = masked_scores(queries, key_heads, segments, segments, positions, positions)
    row_top = jnp.max(scores, -1, keepdims=True)
    log_total = row_top + jnp.log(jnp.sum(jnp.exp(scores - row_top), -1, keepdims=True))
    prob_block = jnp.exp(scores - log_total).astype(jnp.bfloat16)
    outputs = jnp.einsum(
        "hqk,khd->qhd", prob_block, value_heads, preferred_element_type=jnp.float32
    )
    return (outputs, log_total)


def self_backward(queries, key_heads, value_heads, segments, log_totals, grad_heads):
    row_count = queries.shape[0]
    block_rows = min(512, row_count)
    positions = jnp.arange(row_count, dtype=jnp.int32)
    key_sum = jnp.zeros(key_heads.shape, jnp.float32)
    value_sum = jnp.zeros(value_heads.shape, jnp.float32)
    scores = masked_scores(queries, key_heads, segments, segments, positions, positions)
    prob_block = jnp.exp(scores - log_totals)
    grad_probs = jnp.einsum(
        "qhd,khd->hqk", grad_heads, value_heads, preferred_element_type=jnp.float32
    )
    row_delta = jnp.sum(prob_block * grad_probs, -1, keepdims=True)
    grad_scores = (prob_block * (grad_probs - row_delta)).astype(jnp.bfloat16)
    query_parts = (
        jnp.einsum("hqk,khd->qhd", grad_scores, key_heads, preferred_element_type=jnp.float32)
        * SCALE
    )
    key_sum = key_sum.at[:block_rows].add(
        jnp.einsum("hqk,qhd->khd", grad_scores, queries, preferred_element_type=jnp.float32) * SCALE
    )
    value_sum = value_sum.at[:block_rows].add(
        jnp.einsum(
            "hqk,qhd->khd",
            prob_block.astype(jnp.bfloat16),
            grad_heads,
            preferred_element_type=jnp.float32,
        )
    )
    return (query_parts, key_sum, value_sum)


def halving_orders(bit_count):
    plain = list(range(bit_count))
    third = max(bit_count // 3, 1)
    return [plain, plain[third:] + plain[:third], plain[2 * third :] + plain[: 2 * third]]


def swap_mem(tensor):
    return lax.ppermute(tensor, "mem", [(0, 1), (1, 0)])


def scatter_sum(blocks, order, row_count):
    bit_count = len(order)
    me = lax.axis_index("row")
    rest = blocks.shape[1:]
    current = blocks
    left = list(range(bit_count - 1, -1, -1))
    for bit in order:
        at = left.index(bit)
        high = 2**at
        low = 2 ** (len(left) - at - 1)
        view = current.reshape((high, 2, low) + rest)
        mine = (me >> bit) & 1
        keep = lax.dynamic_index_in_dim(view, mine, 1, keepdims=False).reshape((high * low,) + rest)
        send = lax.dynamic_index_in_dim(view, 1 - mine, 1, keepdims=False).reshape(
            (high * low,) + rest
        )
        pairs = [(i, i ^ (1 << bit)) for i in range(row_count)]
        got = lax.ppermute(send, "row", pairs)
        left.remove(bit)
        total = keep.astype(jnp.float32) + got.astype(jnp.float32)
        current = total.astype(jnp.bfloat16) if left else total
    return current[0]


def pair_half(wgrad):
    half = wgrad.shape[1] // 2
    core = lax.axis_index("mem")
    low = wgrad.astype(jnp.bfloat16)
    keep = lax.dynamic_slice_in_dim(low, core * half, half, 1)
    send = lax.dynamic_slice_in_dim(low, (1 - core) * half, half, 1)
    got = swap_mem(send)
    return (keep.astype(jnp.float32) + got.astype(jnp.float32)).astype(jnp.bfloat16)


def pair_norm(norm_wgrad, core):
    low = norm_wgrad.astype(jnp.bfloat16)
    keep = lax.dynamic_slice_in_dim(low, core * 3, 3, 0)
    got = swap_mem(lax.dynamic_slice_in_dim(low, (1 - core) * 3, 3, 0))
    return (keep.astype(jnp.float32) + got.astype(jnp.float32)).astype(jnp.bfloat16)


def cross_forward(queries, key_heads, value_heads, row_seg, key_seg):
    scores = masked_scores(queries, key_heads, row_seg, key_seg, None, None)
    row_top = jnp.max(scores, -1, keepdims=True)
    log_total = row_top + jnp.log(jnp.sum(jnp.exp(scores - row_top), -1, keepdims=True))
    prob_block = jnp.exp(scores - log_total).astype(jnp.bfloat16)
    outputs = jnp.einsum("hqk,khd->qhd", prob_block, value_heads, preferred_element_type=jnp.float32)
    return (outputs, log_total)


def cross_backward(queries, key_heads, value_heads, row_seg, key_seg, log_totals, grad_heads):
    scores = masked_scores(queries, key_heads, row_seg, key_seg, None, None)
    prob_block = jnp.exp(scores - log_totals)
    grad_probs = jnp.einsum("qhd,khd->hqk", grad_heads, value_heads, preferred_element_type=jnp.float32)
    row_delta = jnp.sum(prob_block * grad_probs, -1, keepdims=True)
    grad_scores = (prob_block * (grad_probs - row_delta)).astype(jnp.bfloat16)
    query_parts = jnp.einsum("hqk,khd->qhd", grad_scores, key_heads, preferred_element_type=jnp.float32) * SCALE
    key_sum = jnp.einsum("hqk,qhd->khd", grad_scores, queries, preferred_element_type=jnp.float32) * SCALE
    value_sum = jnp.einsum("hqk,qhd->khd", prob_block.astype(jnp.bfloat16), grad_heads, preferred_element_type=jnp.float32)
    return (query_parts, key_sum, value_sum)


def shards(
    row_count,
    inputs,
    memory,
    target_seg,
    memory_seg,
    self_query,
    self_key,
    self_value,
    self_out,
    cross_query,
    cross_key,
    cross_value,
    cross_out,
    expand_weight,
    contract_weight,
    norm_params,
    out_grad,
):
    inputs_wide = inputs.astype(jnp.float32)
    mem_rows = memory.shape[0]
    pair_memory = jnp.concatenate([memory, swap_mem(memory)])
    pair_seg = jnp.concatenate([memory_seg, swap_mem(memory_seg)])
    queries = split_heads(project(inputs, self_query).astype(jnp.bfloat16))
    key_rows = split_heads(project(inputs, self_key).astype(jnp.bfloat16))
    value_rows = split_heads(project(inputs, self_value).astype(jnp.bfloat16))
    attended, self_totals = self_forward(queries, key_rows, value_rows, target_seg)
    attended_low = join_heads(attended).astype(jnp.bfloat16)
    first_sum = ALPHA * inputs_wide + project(attended_low, self_out)
    hidden_one, norm_back_one = jax.vjp(layer_norm, first_sum, norm_params[0], norm_params[1])
    hidden_one_low = hidden_one.astype(jnp.bfloat16)
    cross_queries = project(hidden_one_low, cross_query).astype(jnp.bfloat16)
    key_heads = split_heads(project(pair_memory, cross_key).astype(jnp.bfloat16))
    value_heads = split_heads(project(pair_memory, cross_value).astype(jnp.bfloat16))
    query_heads = split_heads(cross_queries)
    crossed, cross_totals = cross_forward(query_heads, key_heads, value_heads, target_seg, pair_seg)
    cross_values = join_heads(crossed).astype(jnp.bfloat16)
    second_sum = ALPHA * hidden_one + project(cross_values, cross_out)
    hidden_two, norm_back_two = jax.vjp(layer_norm, second_sum, norm_params[2], norm_params[3])
    hidden_two_low = hidden_two.astype(jnp.bfloat16)
    pre_active = project(hidden_two_low, expand_weight)
    activated, gelu_back = jax.vjp(gelu_exact, pre_active)
    activated_low = activated.astype(jnp.bfloat16)
    third_sum = ALPHA * hidden_two + project(activated_low, contract_weight)
    layer_value, norm_back_three = jax.vjp(layer_norm, third_sum, norm_params[4], norm_params[5])
    layer_out = layer_value.astype(jnp.bfloat16)
    third_grad, gain_three, bias_three = norm_back_three(out_grad.astype(jnp.float32))
    branch_three = third_grad.astype(jnp.bfloat16)
    contract_back = weight_grad(activated_low, branch_three)
    (active_grad,) = gelu_back(back_project(branch_three, contract_weight))
    active_low = active_grad.astype(jnp.bfloat16)
    expand_back = weight_grad(hidden_two_low, active_low)
    hidden_two_grad = ALPHA * third_grad + back_project(active_low, expand_weight)
    second_grad, gain_two, bias_two = norm_back_two(hidden_two_grad)
    branch_two = second_grad.astype(jnp.bfloat16)
    cross_out_back = weight_grad(cross_values, branch_two)
    cross_grad = back_project(branch_two, cross_out).astype(jnp.bfloat16)
    query_parts, key_sum, value_sum = cross_backward(
        query_heads, key_heads, value_heads, target_seg, pair_seg, cross_totals, split_heads(cross_grad)
    )
    query_sum = join_heads(query_parts).astype(jnp.bfloat16)
    memory_key_back = join_heads(key_sum).astype(jnp.bfloat16)
    memory_value_back = join_heads(value_sum).astype(jnp.bfloat16)
    cross_query_wgrad = weight_grad(hidden_one_low, query_sum)
    cross_key_wgrad = weight_grad(pair_memory, memory_key_back)
    cross_value_wgrad = weight_grad(pair_memory, memory_value_back)
    memory_parts = back_project(memory_key_back, cross_key) + back_project(
        memory_value_back, cross_value
    )
    memory_grad = (
        memory_parts[:mem_rows]
        + swap_mem(memory_parts[mem_rows:].astype(jnp.bfloat16)).astype(jnp.float32)
    ).astype(jnp.bfloat16)
    hidden_one_grad = ALPHA * second_grad + back_project(query_sum, cross_query)
    first_grad, gain_one, bias_one = norm_back_one(hidden_one_grad)
    branch_one = first_grad.astype(jnp.bfloat16)
    self_out_wgrad = weight_grad(attended_low, branch_one)
    attended_grad = split_heads(back_project(branch_one, self_out).astype(jnp.bfloat16))
    query_heads_back, key_heads_back, value_heads_back = self_backward(
        queries, key_rows, value_rows, target_seg, self_totals, attended_grad
    )
    self_query_back = join_heads(query_heads_back).astype(jnp.bfloat16)
    self_key_back = join_heads(key_heads_back).astype(jnp.bfloat16)
    self_value_back = join_heads(value_heads_back).astype(jnp.bfloat16)
    self_query_wgrad = weight_grad(inputs, self_query_back)
    self_key_wgrad = weight_grad(inputs, self_key_back)
    self_value_wgrad = weight_grad(inputs, self_value_back)
    input_grad = (
        ALPHA * first_grad
        + back_project(self_query_back, self_query)
        + back_project(self_key_back, self_key)
        + back_project(self_value_back, self_value)
    ).astype(jnp.bfloat16)
    norm_wgrad = jnp.stack([gain_one, bias_one, gain_two, bias_two, gain_three, bias_three])
    orders = halving_orders(row_count.bit_length() - 1)
    small = (
        self_query_wgrad,
        self_key_wgrad,
        self_value_wgrad,
        self_out_wgrad,
        cross_query_wgrad,
        cross_key_wgrad,
        cross_value_wgrad,
        cross_out_back,
        expand_back,
        contract_back,
    )
    choice = (0, 1, 2, 0, 1, 2, 0, 1, 1, 0)
    summed = []
    for wgrad, which in zip(small, choice):
        half = pair_half(wgrad)
        blocks = half.reshape(row_count, half.shape[0] // row_count, half.shape[1])
        summed.append(scatter_sum(blocks, orders[which], row_count))
    core = lax.axis_index("mem")
    norm_half = pair_norm(norm_wgrad, core)
    norm_blocks = norm_half.reshape(3, row_count, norm_half.shape[1] // row_count).transpose(1, 0, 2)
    summed.append(scatter_sum(norm_blocks, orders[2], row_count))
    return (
        layer_out,
        input_grad,
        memory_grad,
        summed[0],
        summed[1],
        summed[2],
        summed[3],
        summed[4],
        summed[5],
        summed[6],
        summed[7],
        summed[8],
        summed[9],
        summed[10],
    )


def solution(mesh):
    in_specs = (
        P(("row", "mem"), None),
        P(("row", "mem"), None),
        P(("row", "mem")),
        P(("row", "mem")),
        P(),
        P(),
        P(),
        P(),
        P(),
        P(),
        P(),
        P(),
        P(),
        P(),
        P(),
        P(("row", "mem"), None),
    )
    out_specs = (
        P(("row", "mem"), None),
        P(("row", "mem"), None),
        P(("row", "mem"), None),
        P("row", "mem"),
        P("row", "mem"),
        P("row", "mem"),
        P("row", "mem"),
        P("row", "mem"),
        P("row", "mem"),
        P("row", "mem"),
        P("row", "mem"),
        P("row", "mem"),
        P("row", "mem"),
        P("mem", "row"),
    )
    return jax.shard_map(partial(shards, mesh.shape["row"]), mesh=mesh, in_specs=in_specs, out_specs=out_specs, check_vma=False)
```

time: 1980 us -> 585 us (0.30)
  waiting for transfers between devices: 1500 us -> 153 us
  starting transfers between devices: 2.14 us -> 74.5 us
  local copies, waits for them, and re-layouts: 122 us -> 51.1 us
  matrix products: 266 us -> 218 us
  other arithmetic: 49.1 us -> 82 us
    reduce_scatter x17 -> x0, waiting for transfers between devices: 981 us -> none  [the longest x1 346 us: shards(): lax.psum_scatter(expand_back, 'row', scatter_dimension=0, tiled=True)]
    unnamed x31 -> x0, waiting for transfers between devices: 507 us -> none
    ppermute x0 -> x58, waiting for transfers between devices: none -> 153 us  [the longest x44 151 us: scatter_sum(): got = lax.ppermute(send, 'row', pairs)]
    ppermute x0 -> x58, starting transfers between devices: none -> 74.5 us  [the longest x44 70.8 us: scatter_sum(): got = lax.ppermute(send, 'row', pairs)]
    unnamed x179 -> x183, local copies, waits for them, and re-layouts: 76.8 us -> 11.5 us
    dot_general x10, matrix products: 56.3 us -> 34.8 us  [weight_grad(): jnp.einsum('rd,re->de', left_side, right_side, preferred_element_type=jnp...]
  transfers between devices with their start and end apart: 25 -> 58, of which waited for: 23 -> 26; matrix products, arithmetic and copies ran while one was open for 10% -> 20% of each run, Pallas kernels for 0% -> 0%
where the time goes in v1:
time: 585 us; the launch traced here: 581 us
  matrix products  218 us (37%)
  waiting for transfers between devices  153 us (26%)
  other arithmetic  82 us (14%)
  starting transfers between devices  74.5 us (13%)
  local copies, waits for them, and re-layouts  51.1 us (9%)
    ppermute x44, waiting for transfers between devices, scatter_sum(): got = lax.ppermute(send, 'row', pairs)  151 us
    ppermute x44, starting transfers between devices, scatter_sum(): got = lax.ppermute(send, 'row', pairs)  70.8 us
    dot_general x10, matrix products, project(): return jnp.dot(left_side, right_side, preferred_element_type=jnp.float32)  53.8 us
    dot_general x10, matrix products, back_project(): jnp.einsum('re,de->rd', grad_rows, weight, preferred_element_type=jnp.flo...  42.9 us
    dot_general x10, matrix products, weight_grad(): jnp.einsum('rd,re->de', left_side, right_side, preferred_element_type=jnp...  34.8 us
    dot_general x2, matrix products, masked_scores(): jnp.einsum('qhd,khd->hqk', query_block, key_heads, preferred_element_type...  17 us
    convert_element_type x9, other arithmetic, pair_half(): (keep.astype(jnp.float32) + got.astype(jnp.float32)).astype(jnp.bfloat16)  14.9 us
    dynamic_slice x10, local copies, waits for them, and re-layouts, pair_half(): send = lax.dynamic_slice_in_dim(low, (1 - core) * half, half, 1)  13.5 us
  transfers between devices with their start and end apart: 58, of which 26 were waited for; matrix products, arithmetic and copies ran while one was open for 20% of the time, Pallas kernels for 0%

profile of v1, /device:TPU:0, one launch (start us, length us, event | category | flops | bytes accessed | tf_op | source)
XLA Modules:
  0.0 581.4 jit_solution(13778461265133653400)
XLA Ops:
  4.2 4.3 convolution_convert_fusion.20
  21.6 8.5 %fusion = (f32[16,512]{1,0:T(8,128)S(1)}, f32[16,512,512]{1,2,0:T(8,128)}) fusion(pred[512,512]{0,1:T(8,128)(4,1)S(1)} %get-tuple-element.102, bf16[512,16,64]{0,2,1:T(8,128)(2,1)} %bitcast.369, bf16[512,16,64]{0,2,1:T(8,128)(2,1)S(1)} %bitcast.365), kind=kOutput, calls=%fused_computation.10 | convolution fusion | flops 549445632 | bytes 19169280 | tf_op jit(solution)/shard_map/qhd,khd->hqk/dot_general | solution.py:55
  30.1 9.3 %exponential_reduce_fusion.1 = f32[16,512]{1,0:T(8,128)S(1)} fusion(f32[16,512,512]{1,2,0:T(8,128)} %get-tuple-element.104, f32[16,512]{1,0:T(8,128)S(1)} %get-tuple-element.103, pred[512,512]{0,1:T(8,128)(4,1)S(1)} %get-tuple-element.102), kind=kLoop, calls=%fused_computation.8 | loop fusion | flops 16769024 | bytes 17104896 | tf_op jit(solution)/shard_map/reduce_sum | solution.py:69
  39.4 8.2 %convolution_convert_fusion.13 = bf16[16,64,512]{2,1,0:T(8,128)(2,1)S(1)} fusion(bf16[512,16,64]{0,2,1:T(8,128)(2,1)S(1)} %bitcast.382, f32[16,512,512]{1,2,0:T(8,128)} %get-tuple-element.104, f32[16,512]{1,0:T(8,128)S(1)} %log_add_fusion.1, pred[512,512]{0,1:T(8,128)(4,1)S(1)} %get-tuple-element.102), kind=kOutput, calls=%fused_computation.101 | convolution fusion | flops 554172416 | bytes 19169280 | tf_op jit(solution)/shard_map/hqk,khd->qhd/dot_general | solution.py:71
  61.1 4.5 convolution_convert_fusion.18
  68.0 8.5 %fusion.1 = (f32[16,512]{1,0:T(8,128)S(1)}, f32[16,512,512]{1,2,0:T(8,128)}) fusion(pred[512,512]{0,1:T(8,128)(4,1)S(1)} %copy-done.14, bf16[512,16,64]{0,2,1:T(8,128)(2,1)} %bitcast.371, bf16[512,16,64]{0,2,1:T(8,128)(2,1)S(1)} %bitcast.367), kind=kOutput, calls=%fused_computation.11 | convolution fusion | flops 549445632 | bytes 19169280 | tf_op jit(solution)/shard_map/qhd,khd->hqk/dot_general | solution.py:55
  76.5 9.3 %exponential_reduce_fusion = f32[16,512]{1,0:T(8,128)S(1)} fusion(f32[16,512,512]{1,2,0:T(8,128)} %get-tuple-element.108, f32[16,512]{1,0:T(8,128)S(1)} %get-tuple-element.107, pred[512,512]{0,1:T(8,128)(4,1)S(1)} %copy-done.14), kind=kLoop, calls=%fused_computation.5 | loop fusion | flops 16769024 | bytes 17104896 | tf_op jit(solution)/shard_map/reduce_sum | solution.py:162
  85.8 8.2 %convolution_convert_fusion.12 = bf16[16,64,512]{2,1,0:T(8,128)(2,1)S(1)} fusion(bf16[512,16,64]{0,2,1:T(8,128)(2,1)S(1)} %bitcast.384, f32[16,512,512]{1,2,0:T(8,128)} %get-tuple-element.108, f32[16,512]{1,0:T(8,128)S(1)} %log_add_fusion, pred[512,512]{0,1:T(8,128)(4,1)S(1)} %copy-done.14), kind=kOutput, calls=%fused_computation.100 | convolution fusion | flops 554172416 | bytes 19169280 | tf_op jit(solution)/shard_map/hqk,khd->qhd/dot_general | solution.py:164
  96.0 27.3 %multiply_convert_fusion.2 = (bf16[512,4096]{1,0:T(8,128)(2,1)S(1)}, f32[512,4096]{1,0:T(8,128)}, f32[512,4096]{1,0:T(8,128)}) fusion(bf16[1024,4096]{1,0:T(8,128)(2,1)} %param.36, f32[512,1024]{1,0:T(8,128)S(1)} %get-tuple-element.110, f32[1024]{0:T(1024)S(1)} %bitcast.477, f32[1024]{0:T(1024)S(1)} %bitcast.467, f32[512]{0:T(512)S(1)} %fusion.61, ...), kind=kOutput, calls=%fused_computation.19 | convolution fusion | flops 4433903616 | bytes 31469568 | tf_op jit(solution)/shard_map/dot_general | solution.py:30
  123.4 4.8 fusion.86
  132.2 14.6 %add_convert_fusion.2 = bf16[512,4096]{1,0:T(8,128)(2,1)} fusion(f32[512,4096]{1,0:T(8,128)} %get-tuple-element.69, f32[512,4096]{1,0:T(8,128)} %get-tuple-element.111, bf16[4096,1024]{1,0:T(8,128)(2,1)} %param.37, f32[512,1024]{1,0:T(8,128)S(1)} %get-tuple-element.67, f32[512]{0:T(512)S(1)} %negate_multiply_fusion.3), kind=kOutput, calls=%fused_computation.18 | convolution fusion | flops 4325376000 | bytes 31459328 | tf_op jit(solution)/shard_map/re,de->rd/dot_general | solution.py:38
  146.8 9.0 %multiply_reduce_fusion.2 = (bf16[1024]{0:T(1024)(128)(2,1)S(1)}, f32[512]{0:T(512)S(1)}, bf16[1024]{0:T(1024)(128)(2,1)S(1)}, f32[512,1024]{1,0:T(8,128)S(1)}) fusion(f32[512,1024]{1,0:T(8,128)S(1)} %get-tuple-element.110, f32[512]{0:T(512)S(1)} %fusion.61, f32[512]{0:T(512)S(1)} %broadcast_multiply_fusion.1, f32[1024]{0:T(1024)S(1)} %bitcast.469, ...), kind=kOutput, calls=%fused_computation.58 | convolution fusion | flops 4300731904 | bytes 18890752 | tf_op jit(solution)/shard_map/re,de->rd/dot_general | solution.py:38
  161.5 7.5 %convolution_convert_fusion.1 = bf16[1024,4096]{1,0:T(8,128)(2,1)} fusion(bf16[512,4096]{1,0:T(8,128)(2,1)S(1)} %copy-done.81, f32[512,1024]{1,0:T(8,128)S(1)} %get-tuple-element.110, f32[1024]{0:T(1024)S(1)} %bitcast.479, f32[1024]{0:T(1024)S(1)} %bitcast.471, f32[512]{0:T(512)S(1)} %fusion.61, f32[512]{0:T(512)S(1)} %broadcast_multiply_fusion.1), kind=kOutput, calls=%fused_computation.34 | convolution fusion | flops 4301783040 | bytes 14692352 | tf_op jit(solution)/shard_map/rd,re->de/dot_general | solution.py:34
  169.0 7.5 %convolution_convert_fusion = bf16[4096,1024]{1,0:T(8,128)(2,1)} fusion(bf16[512,4096]{1,0:T(8,128)(2,1)S(1)} %copy-done.80, f32[512,1024]{1,0:T(8,128)S(1)} %get-tuple-element.67, f32[512]{0:T(512)S(1)} %negate_multiply_fusion.3), kind=kOutput, calls=%fused_computation.33 | convolution fusion | flops 4300210176 | bytes 14682112 | tf_op jit(solution)/shard_map/rd,re->de/dot_general | solution.py:34
  178.8 11.2 %convolution_convert_fusion.10 = bf16[16,64,512]{2,1,0:T(8,128)(2,1)} fusion(bf16[512,16,64]{0,2,1:T(8,128)(2,1)} %bitcast.390, f32[16,512,512]{1,2,0:T(8,128)} %get-tuple-element.108, f32[16,512]{1,0:T(8,128)S(1)} %log_add_fusion, pred[512,512]{0,1:T(8,128)(4,1)S(1)} %copy-done.14), kind=kOutput, calls=%fused_computation.98 | convolution fusion | flops 554172416 | bytes 19169280 | tf_op jit(solution)/shard_map/hqk,qhd->khd/dot_general | solution.py:176
  190.0 11.7 %multiply_reduce_fusion.1 = (f32[16,512]{1,0:T(8,128)S(1)}, f32[16,512,512]{1,2,0:T(8,128)}) fusion(f32[16,512,512]{1,2,0:T(8,128)} %get-tuple-element.108, f32[16,512]{1,0:T(8,128)S(1)} %log_add_fusion, pred[512,512]{0,1:T(8,128)(4,1)S(1)} %copy-done.14, bf16[512,16,64]{0,2,1:T(8,128)(2,1)S(1)} %bitcast.391, bf16[512,16,64]{0,2,1:T(8,128)(2,1)S(1)} %bitcast.385), kind=kOutput, calls=%fused_computation.3 | convolution fusion | flops 557834240 | bytes 35979264 | tf_op jit(solution)/shard_map/qhd,khd->hqk/dot_general | solution.py:171
  201.6 12.5 %multiply_convert_fusion.1 = bf16[16,512,512]{1,2,0:T(8,128)(2,1)S(1)} fusion(f32[16,512,512]{1,2,0:T(8,128)} %get-tuple-element.116, f32[16,512,512]{1,2,0:T(8,128)} %get-tuple-element.108, f32[16,512]{1,0:T(8,128)S(1)} %get-tuple-element.115, f32[16,512]{1,0:T(8,128)S(1)} %log_add_fusion, pred[512,512]{0,1:T(8,128)(4,1)S(1)} %copy-done.14), kind=kLoop, calls=%fused_computation.2 | loop fusion | flops 25165824 | bytes 42270720 | tf_op jit(solution)/shard_map/convert_element_type | solution.py:173
  232.7 9.0 %convolution_convert_fusion.11 = bf16[16,64,512]{2,1,0:T(8,128)(2,1)} fusion(bf16[512,16,64]{0,2,1:T(8,128)(2,1)S(1)} %bitcast.392, f32[16,512,512]{1,2,0:T(8,128)} %get-tuple-element.104, f32[16,512]{1,0:T(8,128)S(1)} %copy-done.48, pred[512,512]{0,1:T(8,128)(4,1)S(1)} %copy-done.13), kind=kOutput, calls=%fused_computation.99 | convolution fusion | flops 554172416 | bytes 19169280 | tf_op jit(solution)/shard_map/hqk,qhd->khd/dot_general | solution.py:98
  241.8 11.9 %multiply_reduce_fusion = (f32[16,512]{1,0:T(8,128)S(1)}, f32[16,512,512]{1,2,0:T(8,128)}) fusion(f32[16,512,512]{1,2,0:T(8,128)} %get-tuple-element.104, f32[16,512]{1,0:T(8,128)S(1)} %copy-done.48, pred[512,512]{0,1:T(8,128)(4,1)S(1)} %copy-done.13, bf16[512,16,64]{0,2,1:T(8,128)(2,1)S(1)} %bitcast.393, bf16[512,16,64]{0,2,1:T(8,128)(2,1)S(1)} %bitcast.383), kind=kOutput, calls=%fused_computation.1 | convolution fusion | flops 557834240 | bytes 35979264 | tf_op jit(solution)/shard_map/qhd,khd->hqk/dot_general | solution.py:85
  253.7 12.7 %multiply_convert_fusion = bf16[16,512,512]{1,2,0:T(8,128)(2,1)S(1)} fusion(f32[16,512,512]{1,2,0:T(8,128)} %get-tuple-element.119, f32[16,512,512]{1,2,0:T(8,128)} %get-tuple-element.104, f32[16,512]{1,0:T(8,128)S(1)} %get-tuple-element.118, f32[16,512]{1,0:T(8,128)S(1)} %copy-done.48, pred[512,512]{0,1:T(8,128)(4,1)S(1)} %copy-done.13), kind=kLoop, calls=%fused_computation | loop fusion | flops 25165824 | bytes 42270720 | tf_op jit(solution)/shard_map/convert_element_type | solution.py:89
  349.0 6.2 %collective-permute-done.34 = bf16[8,64,512]{2,1,0:T(8,128)(2,1)S(1)} collective-permute-done((bf16[8,64,512]{2,1,0:T(8,128)(2,1)S(1)}, bf16[8,64,512]{2,1,0:T(8,128)(2,1)S(1)}, u32[]{:S(2)}, u32[]{:S(2)}) %collective-permute-start.34) | collective-permute-done | bytes 524320 | tf_op jit(solution)/shard_map/ppermute | solution.py:135
  357.2 8.8 %collective-permute-done.19 = bf16[8,64,512]{2,1,0:T(8,128)(2,1)S(1)} collective-permute-done((bf16[8,64,512]{2,1,0:T(8,128)(2,1)S(1)}, bf16[8,64,512]{2,1,0:T(8,128)(2,1)S(1)}, u32[]{:S(2)}, u32[]{:S(2)}) %collective-permute-start.19) | collective-permute-done | bytes 524320 | tf_op jit(solution)/shard_map/ppermute | solution.py:135
  371.8 9.2 %collective-permute-done.29 = bf16[8,64,512]{2,1,0:T(8,128)(2,1)S(1)} collective-permute-done((bf16[8,64,512]{2,1,0:T(8,128)(2,1)S(1)}, bf16[8,64,512]{2,1,0:T(8,128)(2,1)S(1)}, u32[]{:S(2)}, u32[]{:S(2)}) %collective-permute-start.29) | collective-permute-done | bytes 524320 | tf_op jit(solution)/shard_map/ppermute | solution.py:135
  383.2 9.1 %collective-permute-done.4 = bf16[8,64,512]{2,1,0:T(8,128)(2,1)S(1)} collective-permute-done((bf16[8,64,512]{2,1,0:T(8,128)(2,1)S(1)}, bf16[8,64,512]{2,1,0:T(8,128)(2,1)S(1)}, u32[]{:S(2)}, u32[]{:S(2)}) %collective-permute-start.4) | collective-permute-done | bytes 524320 | tf_op jit(solution)/shard_map/ppermute | solution.py:135
  405.3 11.9 %collective-permute-done.30 = bf16[4,64,512]{2,1,0:T(8,128)(2,1)S(1)} collective-permute-done((bf16[4,64,512]{2,1,0:T(8,128)(2,1)S(1)}, bf16[4,64,512]{2,1,0:T(8,128)(2,1)S(1)}, u32[]{:S(2)}, u32[]{:S(2)}) %collective-permute-start.30) | collective-permute-done | bytes 262176 | tf_op jit(solution)/shard_map/ppermute | solution.py:135
  450.9 4.8 add_convert_fusion
  472.2 25.6 %collective-permute-done.42 = bf16[1,64,512]{2,1,0:T(8,128)(2,1)S(1)} collective-permute-done((bf16[1,64,512]{2,1,0:T(8,128)(2,1)S(1)}, bf16[1,64,512]{2,1,0:T(8,128)(2,1)S(1)}, u32[]{:S(2)}, u32[]{:S(2)}) %collective-permute-start.42) | collective-permute-done | bytes 65568 | tf_op jit(solution)/shard_map/ppermute | solution.py:135
  497.8 8.8 %collective-permute-start.32 = (bf16[1,64,512]{2,1,0:T(8,128)(2,1)S(1)}, bf16[1,64,512]{2,1,0:T(8,128)(2,1)S(1)}, u32[]{:S(2)}, u32[]{:S(2)}) collective-permute-start(bf16[1,64,512]{2,1,0:T(8,128)(2,1)S(1)} %constant_dynamic-slice_fusion.26), channel_id=1, source_target_pairs={{0,4},{2,6},{4,0},{6,2},{8,12},{10,14},{12,8},{14,10},{16,20},{18,... | collective-permute-start | bytes 196616 | tf_op jit(solution)/shard_map/ppermute | solution.py:135
  518.4 15.6 %collective-permute-done.50 = bf16[4,256,512]{2,1,0:T(8,128)(2,1)S(1)} collective-permute-done((bf16[4,256,512]{2,1,0:T(8,128)(2,1)S(1)}, bf16[4,256,512]{2,1,0:T(8,128)(2,1)S(1)}, u32[]{:S(2)}, u32[]{:S(2)}) %collective-permute-start.50) | collective-permute-done | bytes 1048608 | tf_op jit(solution)/shard_map/ppermute | solution.py:135
  534.5 9.7 %collective-permute-done.45 = bf16[4,64,2048]{2,1,0:T(8,128)(2,1)S(1)} collective-permute-done((bf16[4,64,2048]{2,1,0:T(8,128)(2,1)S(1)}, bf16[4,64,2048]{2,1,0:T(8,128)(2,1)S(1)}, u32[]{:S(2)}, u32[]{:S(2)}) %collective-permute-start.45) | collective-permute-done | bytes 1048608 | tf_op jit(solution)/shard_map/ppermute | solution.py:135
  545.7 9.2 %collective-permute-done.51 = bf16[2,256,512]{2,1,0:T(8,128)(2,1)S(1)} collective-permute-done((bf16[2,256,512]{2,1,0:T(8,128)(2,1)S(1)}, bf16[2,256,512]{2,1,0:T(8,128)(2,1)S(1)}, u32[]{:S(2)}, u32[]{:S(2)}) %collective-permute-start.51) | collective-permute-done | bytes 524320 | tf_op jit(solution)/shard_map/ppermute | solution.py:135
  555.1 18.6 %collective-permute-done.46 = bf16[2,64,2048]{2,1,0:T(8,128)(2,1)S(1)} collective-permute-done((bf16[2,64,2048]{2,1,0:T(8,128)(2,1)S(1)}, bf16[2,64,2048]{2,1,0:T(8,128)(2,1)S(1)}, u32[]{:S(2)}, u32[]{:S(2)}) %collective-permute-start.46) | collective-permute-done | bytes 524320 | tf_op jit(solution)/shard_map/ppermute | solution.py:135
  (469 shorter events, 241.1 us)
Async XLA Ops:
  0.7 19.9 %collective-permute-start.1 = (s32[256]{0:T(256)}, s32[256]{0:T(256)S(1)}, u32[]{:S(2)}, u32[]{:S(2)}) collective-permute-start(s32[256]{0:T(256)} %param.27), channel_id=1, source_target_pairs={{0,1},{1,0},{2,3},{3,2},{4,5},{5,4},{6,7},{7,6},{8,9},{9,8},{10,11... | collective-permute-start | bytes 3080 | tf_op jit(solution)/shard_map/ppermute | solution.py:115
  1.2 52.0 %collective-permute-start = (bf16[256,1024]{1,0:T(8,128)(2,1)}, bf16[256,1024]{1,0:T(8,128)(2,1)}, u32[]{:S(2)}, u32[]{:S(2)}) collective-permute-start(bf16[256,1024]{1,0:T(8,128)(2,1)} %param.25), channel_id=1, source_target_pairs={{0,1},{1,0},{2,3},{3,2},{4,5},{5,4},{6,7},{7,6},{8,9},{9,8},{10,11... | collective-permute-start | bytes 1572872 | tf_op jit(solution)/shard_map/ppermute | solution.py:115
  282.1 49.7 %collective-permute-start.38 = (bf16[1024,512]{1,0:T(8,128)(2,1)}, bf16[1024,512]{1,0:T(8,128)(2,1)S(1)}, u32[]{:S(2)}, u32[]{:S(2)}) collective-permute-start(bf16[1024,512]{1,0:T(8,128)(2,1)} %constant_dynamic-slice_fusion.23), channel_id=1, source_target_pairs={{0,1},{1,0},{2,3},{3,2},{4,5},{5,4},{6,7},{7,6},{8,9},{9,8},{10,11... | collective-permute-start | bytes 3145736 | tf_op jit(solution)/shard_map/ppermute | solution.py:115
  286.6 48.0 %collective-permute-start.33 = (bf16[1024,512]{1,0:T(8,128)(2,1)}, bf16[1024,512]{1,0:T(8,128)(2,1)}, u32[]{:S(2)}, u32[]{:S(2)}) collective-permute-start(bf16[1024,512]{1,0:T(8,128)(2,1)} %constant_dynamic-slice_fusion.25), channel_id=1, source_target_pairs={{0,1},{1,0},{2,3},{3,2},{4,5},{5,4},{6,7},{7,6},{8,9},{9,8},{10,11... | collective-permute-start | bytes 3145736 | tf_op jit(solution)/shard_map/ppermute | solution.py:115
  289.6 21.8 %collective-permute-start.53 = (bf16[3,1024]{1,0:T(4,128)(2,1)S(1)}, bf16[3,1024]{1,0:T(4,128)(2,1)S(1)}, u32[]{:S(2)}, u32[]{:S(2)}) collective-permute-start(bf16[3,1024]{1,0:T(4,128)(2,1)S(1)} %constant_dynamic-slice_fusion.8), channel_id=1, source_target_pairs={{0,1},{1,0},{2,3},{3,2},{4,5},{5,4},{6,7},{7,6},{8,9},{9,8},{10,11... | collective-permute-start | bytes 18440 | tf_op jit(solution)/shard_map/ppermute | solution.py:115
  295.6 33.4 %collective-permute-start.2 = (bf16[256,1024]{1,0:T(8,128)(2,1)}, bf16[256,1024]{1,0:T(8,128)(2,1)}, u32[]{:S(2)}, u32[]{:S(2)}) collective-permute-start(bf16[256,1024]{1,0:T(8,128)(2,1)} %slice.77), channel_id=1, source_target_pairs={{0,1},{1,0},{2,3},{3,2},{4,5},{5,4},{6,7},{7,6},{8,9},{9,8},{10,11... | collective-permute-start | bytes 1572872 | tf_op jit(solution)/shard_map/ppermute | solution.py:115
  298.3 33.6 %collective-permute-start.23 = (bf16[1024,512]{1,0:T(8,128)(2,1)}, bf16[1024,512]{1,0:T(8,128)(2,1)}, u32[]{:S(2)}, u32[]{:S(2)}) collective-permute-start(bf16[1024,512]{1,0:T(8,128)(2,1)} %constant_dynamic-slice_fusion.35), channel_id=1, source_target_pairs={{0,1},{1,0},{2,3},{3,2},{4,5},{5,4},{6,7},{7,6},{8,9},{9,8},{10,11... | collective-permute-start | bytes 3145736 | tf_op jit(solution)/shard_map/ppermute | solution.py:115
  329.0 121.9 %collective-permute-start.48 = (bf16[4096,512]{1,0:T(8,128)(2,1)S(1)}, bf16[4096,512]{1,0:T(8,128)(2,1)}, u32[]{:S(2)}, u32[]{:S(2)}) collective-permute-start(bf16[4096,512]{1,0:T(8,128)(2,1)S(1)} %copy-done.19), channel_id=1, source_target_pairs={{0,1},{1,0},{2,3},{3,2},{4,5},{5,4},{6,7},{7,6},{8,9},{9,8},{10,11... | collective-permute-start | bytes 12582920 | tf_op jit(solution)/shard_map/ppermute | solution.py:115
  339.8 118.9 %collective-permute-start.43 = (bf16[1024,2048]{1,0:T(8,128)(2,1)S(1)}, bf16[1024,2048]{1,0:T(8,128)(2,1)}, u32[]{:S(2)}, u32[]{:S(2)}) collective-permute-start(bf16[1024,2048]{1,0:T(8,128)(2,1)S(1)} %copy-done.20), channel_id=1, source_target_pairs={{0,1},{1,0},{2,3},{3,2},{4,5},{5,4},{6,7},{7,6},{8,9},{9,8},{10,11... | collective-permute-start | bytes 12582920 | tf_op jit(solution)/shard_map/ppermute | solution.py:115
  344.5 23.4 %collective-permute-start.39 = (bf16[8,64,512]{2,1,0:T(8,128)(2,1)S(1)}, bf16[8,64,512]{2,1,0:T(8,128)(2,1)S(1)}, u32[]{:S(2)}, u32[]{:S(2)}) collective-permute-start(bf16[8,64,512]{2,1,0:T(8,128)(2,1)S(1)} %bitcast.450), channel_id=1, source_target_pairs={{0,4},{2,6},{4,0},{6,2},{8,12},{10,14},{12,8},{14,10},{16,20},{18,... | collective-permute-start | bytes 1572872 | tf_op jit(solution)/shard_map/ppermute | solution.py:135
  346.8 19.1 %collective-permute-start.19 = (bf16[8,64,512]{2,1,0:T(8,128)(2,1)S(1)}, bf16[8,64,512]{2,1,0:T(8,128)(2,1)S(1)}, u32[]{:S(2)}, u32[]{:S(2)}) collective-permute-start(bf16[8,64,512]{2,1,0:T(8,128)(2,1)S(1)} %dynamic-slice_bitcast_fusion.8), channel_id=1, source_target_pairs={{0,2},{2,0},{4,6},{6,4},{8,10},{10,8},{12,14},{14,12},{16,18},{18,... | collective-permute-start | bytes 1572872 | tf_op jit(solution)/shard_map/ppermute | solution.py:135
  367.9 26.1 %collective-permute-start.14 = (bf16[8,64,512]{2,1,0:T(8,128)(2,1)S(1)}, bf16[8,64,512]{2,1,0:T(8,128)(2,1)S(1)}, u32[]{:S(2)}, u32[]{:S(2)}) collective-permute-start(bf16[8,64,512]{2,1,0:T(8,128)(2,1)S(1)} %bitcast.446), channel_id=1, source_target_pairs={{0,8},{2,10},{4,12},{6,14},{8,0},{10,2},{12,4},{14,6},{16,24},{18,... | collective-permute-start | bytes 1572872 | tf_op jit(solution)/shard_map/ppermute | solution.py:135
  369.9 26.0 %collective-permute-start.9 = (bf16[8,64,512]{2,1,0:T(8,128)(2,1)S(1)}, bf16[8,64,512]{2,1,0:T(8,128)(2,1)S(1)}, u32[]{:S(2)}, u32[]{:S(2)}) collective-permute-start(bf16[8,64,512]{2,1,0:T(8,128)(2,1)S(1)} %bitcast.449), channel_id=1, source_target_pairs={{0,4},{2,6},{4,0},{6,2},{8,12},{10,14},{12,8},{14,10},{16,20},{18,... | collective-permute-start | bytes 1572872 | tf_op jit(solution)/shard_map/ppermute | solution.py:135
  394.0 26.6 %collective-permute-start.40 = (bf16[4,64,512]{2,1,0:T(8,128)(2,1)S(1)}, bf16[4,64,512]{2,1,0:T(8,128)(2,1)S(1)}, u32[]{:S(2)}, u32[]{:S(2)}) collective-permute-start(bf16[4,64,512]{2,1,0:T(8,128)(2,1)S(1)} %bitcast.452), channel_id=1, source_target_pairs={{0,8},{2,10},{4,12},{6,14},{8,0},{10,2},{12,4},{14,6},{16,24},{18,... | collective-permute-start | bytes 786440 | tf_op jit(solution)/shard_map/ppermute | solution.py:135
  399.8 17.3 %collective-permute-start.30 = (bf16[4,64,512]{2,1,0:T(8,128)(2,1)S(1)}, bf16[4,64,512]{2,1,0:T(8,128)(2,1)S(1)}, u32[]{:S(2)}, u32[]{:S(2)}) collective-permute-start(bf16[4,64,512]{2,1,0:T(8,128)(2,1)S(1)} %dynamic-slice_bitcast_fusion.11), channel_id=1, source_target_pairs={{0,16},{2,18},{4,20},{6,22},{8,24},{10,26},{12,28},{14,30},{16,0},... | collective-permute-start | bytes 786440 | tf_op jit(solution)/shard_map/ppermute | solution.py:135
  402.6 17.4 %collective-permute-start.15 = (bf16[4,64,512]{2,1,0:T(8,128)(2,1)S(1)}, bf16[4,64,512]{2,1,0:T(8,128)(2,1)S(1)}, u32[]{:S(2)}, u32[]{:S(2)}) collective-permute-start(bf16[4,64,512]{2,1,0:T(8,128)(2,1)S(1)} %dynamic-slice_bitcast_fusion.13), channel_id=1, source_target_pairs={{0,16},{2,18},{4,20},{6,22},{8,24},{10,26},{12,28},{14,30},{16,0},... | collective-permute-start | bytes 786440 | tf_op jit(solution)/shard_map/ppermute | solution.py:135
  444.9 18.5 %collective-permute-start.11 = (bf16[2,64,512]{2,1,0:T(8,128)(2,1)S(1)}, bf16[2,64,512]{2,1,0:T(8,128)(2,1)}, u32[]{:S(2)}, u32[]{:S(2)}) collective-permute-start(bf16[2,64,512]{2,1,0:T(8,128)(2,1)S(1)} %dynamic-slice_bitcast_fusion.21), channel_id=1, source_target_pairs={{0,16},{2,18},{4,20},{6,22},{8,24},{10,26},{12,28},{14,30},{16,0},... | collective-permute-start | bytes 393224 | tf_op jit(solution)/shard_map/ppermute | solution.py:135
  447.0 18.1 %collective-permute-start.6 = (bf16[2,64,512]{2,1,0:T(8,128)(2,1)S(1)}, bf16[2,64,512]{2,1,0:T(8,128)(2,1)}, u32[]{:S(2)}, u32[]{:S(2)}) collective-permute-start(bf16[2,64,512]{2,1,0:T(8,128)(2,1)S(1)} %dynamic-slice_bitcast_fusion.22), channel_id=1, source_target_pairs={{0,8},{2,10},{4,12},{6,14},{8,0},{10,2},{12,4},{14,6},{16,24},{18,... | collective-permute-start | bytes 393224 | tf_op jit(solution)/shard_map/ppermute | solution.py:135
  450.8 16.9 %collective-permute-start.37 = (bf16[1,64,512]{2,1,0:T(8,128)(2,1)}, bf16[1,64,512]{2,1,0:T(8,128)(2,1)}, u32[]{:S(2)}, u32[]{:S(2)}) collective-permute-start(bf16[1,64,512]{2,1,0:T(8,128)(2,1)} %constant_dynamic-slice_fusion.24), channel_id=1, source_target_pairs={{0,16},{2,18},{4,20},{6,22},{8,24},{10,26},{12,28},{14,30},{16,0},... | collective-permute-start | bytes 196616 | tf_op jit(solution)/shard_map/ppermute | solution.py:135
  457.2 50.8 %collective-permute-start.49 = (bf16[8,256,512]{2,1,0:T(8,128)(2,1)}, bf16[8,256,512]{2,1,0:T(8,128)(2,1)S(1)}, u32[]{:S(2)}, u32[]{:S(2)}) collective-permute-start(bf16[8,256,512]{2,1,0:T(8,128)(2,1)} %dynamic-slice_bitcast_fusion), channel_id=1, source_target_pairs={{0,2},{2,0},{4,6},{6,4},{8,10},{10,8},{12,14},{14,12},{16,18},{18,... | collective-permute-start | bytes 6291464 | tf_op jit(solution)/shard_map/ppermute | solution.py:135
  463.3 47.0 %collective-permute-start.44 = (bf16[8,64,2048]{2,1,0:T(8,128)(2,1)S(1)}, bf16[8,64,2048]{2,1,0:T(8,128)(2,1)S(1)}, u32[]{:S(2)}, u32[]{:S(2)}) collective-permute-start(bf16[8,64,2048]{2,1,0:T(8,128)(2,1)S(1)} %bitcast.409), channel_id=1, source_target_pairs={{0,4},{2,6},{4,0},{6,2},{8,12},{10,14},{12,8},{14,10},{16,20},{18,... | collective-permute-start | bytes 6291464 | tf_op jit(solution)/shard_map/ppermute | solution.py:135
  463.6 34.1 %collective-permute-start.42 = (bf16[1,64,512]{2,1,0:T(8,128)(2,1)S(1)}, bf16[1,64,512]{2,1,0:T(8,128)(2,1)S(1)}, u32[]{:S(2)}, u32[]{:S(2)}) collective-permute-start(bf16[1,64,512]{2,1,0:T(8,128)(2,1)S(1)} %copy-done.52), channel_id=1, source_target_pairs={{0,2},{2,0},{4,6},{6,4},{8,10},{10,8},{12,14},{14,12},{16,18},{18,... | collective-permute-start | bytes 196616 | tf_op jit(solution)/shard_map/ppermute | solution.py:135
  465.2 42.1 %collective-permute-start.27 = (bf16[1,64,512]{2,1,0:T(8,128)(2,1)S(1)}, bf16[1,64,512]{2,1,0:T(8,128)(2,1)S(1)}, u32[]{:S(2)}, u32[]{:S(2)}) collective-permute-start(bf16[1,64,512]{2,1,0:T(8,128)(2,1)S(1)} %copy-done.51), channel_id=1, source_target_pairs={{0,2},{2,0},{4,6},{6,4},{8,10},{10,8},{12,14},{14,12},{16,18},{18,... | collective-permute-start | bytes 196616 | tf_op jit(solution)/shard_map/ppermute | solution.py:135
  467.7 45.7 %collective-permute-start.22 = (bf16[1,64,512]{2,1,0:T(8,128)(2,1)S(1)}, bf16[1,64,512]{2,1,0:T(8,128)(2,1)S(1)}, u32[]{:S(2)}, u32[]{:S(2)}) collective-permute-start(bf16[1,64,512]{2,1,0:T(8,128)(2,1)S(1)} %constant_dynamic-slice_fusion.36), channel_id=1, source_target_pairs={{0,16},{2,18},{4,20},{6,22},{8,24},{10,26},{12,28},{14,30},{16,0},... | collective-permute-start | bytes 196616 | tf_op jit(solution)/shard_map/ppermute | solution.py:135
  497.8 16.7 %collective-permute-start.32 = (bf16[1,64,512]{2,1,0:T(8,128)(2,1)S(1)}, bf16[1,64,512]{2,1,0:T(8,128)(2,1)S(1)}, u32[]{:S(2)}, u32[]{:S(2)}) collective-permute-start(bf16[1,64,512]{2,1,0:T(8,128)(2,1)S(1)} %constant_dynamic-slice_fusion.26), channel_id=1, source_target_pairs={{0,4},{2,6},{4,0},{6,2},{8,12},{10,14},{12,8},{14,10},{16,20},{18,... | collective-permute-start | bytes 196616 | tf_op jit(solution)/shard_map/ppermute | solution.py:135
  508.0 37.0 %collective-permute-start.12 = (bf16[1,64,512]{2,1,0:T(8,128)(2,1)S(1)}, bf16[1,64,512]{2,1,0:T(8,128)(2,1)S(1)}, u32[]{:S(2)}, u32[]{:S(2)}) collective-permute-start(bf16[1,64,512]{2,1,0:T(8,128)(2,1)S(1)} %constant_dynamic-slice_fusion.41), channel_id=1, source_target_pairs={{0,2},{2,0},{4,6},{6,4},{8,10},{10,8},{12,14},{14,12},{16,18},{18,... | collective-permute-start | bytes 196616 | tf_op jit(solution)/shard_map/ppermute | solution.py:135
  510.3 23.8 %collective-permute-start.50 = (bf16[4,256,512]{2,1,0:T(8,128)(2,1)S(1)}, bf16[4,256,512]{2,1,0:T(8,128)(2,1)S(1)}, u32[]{:S(2)}, u32[]{:S(2)}) collective-permute-start(bf16[4,256,512]{2,1,0:T(8,128)(2,1)S(1)} %dynamic-slice_bitcast_fusion.1), channel_id=1, source_target_pairs={{0,4},{2,6},{4,0},{6,2},{8,12},{10,14},{12,8},{14,10},{16,20},{18,... | collective-permute-start | bytes 3145736 | tf_op jit(solution)/shard_map/ppermute | solution.py:135
  513.4 30.7 %collective-permute-start.45 = (bf16[4,64,2048]{2,1,0:T(8,128)(2,1)S(1)}, bf16[4,64,2048]{2,1,0:T(8,128)(2,1)S(1)}, u32[]{:S(2)}, u32[]{:S(2)}) collective-permute-start(bf16[4,64,2048]{2,1,0:T(8,128)(2,1)S(1)} %bitcast.425), channel_id=1, source_target_pairs={{0,8},{2,10},{4,12},{6,14},{8,0},{10,2},{12,4},{14,6},{16,24},{18,... | collective-permute-start | bytes 3145736 | tf_op jit(solution)/shard_map/ppermute | solution.py:135
  514.4 60.0 %collective-permute-start.7 = (bf16[1,64,512]{2,1,0:T(8,128)(2,1)S(1)}, bf16[1,64,512]{2,1,0:T(8,128)(2,1)S(1)}, u32[]{:S(2)}, u32[]{:S(2)}) collective-permute-start(bf16[1,64,512]{2,1,0:T(8,128)(2,1)S(1)} %constant_dynamic-slice_fusion.46), channel_id=1, source_target_pairs={{0,16},{2,18},{4,20},{6,22},{8,24},{10,26},{12,28},{14,30},{16,0},... | collective-permute-start | bytes 196616 | tf_op jit(solution)/shard_map/ppermute | solution.py:135
  534.4 20.5 %collective-permute-start.51 = (bf16[2,256,512]{2,1,0:T(8,128)(2,1)S(1)}, bf16[2,256,512]{2,1,0:T(8,128)(2,1)S(1)}, u32[]{:S(2)}, u32[]{:S(2)}) collective-permute-start(bf16[2,256,512]{2,1,0:T(8,128)(2,1)S(1)} %dynamic-slice_bitcast_fusion.5), channel_id=1, source_target_pairs={{0,8},{2,10},{4,12},{6,14},{8,0},{10,2},{12,4},{14,6},{16,24},{18,... | collective-permute-start | bytes 1572872 | tf_op jit(solution)/shard_map/ppermute | solution.py:135
  544.7 29.0 %collective-permute-start.46 = (bf16[2,64,2048]{2,1,0:T(8,128)(2,1)S(1)}, bf16[2,64,2048]{2,1,0:T(8,128)(2,1)S(1)}, u32[]{:S(2)}, u32[]{:S(2)}) collective-permute-start(bf16[2,64,2048]{2,1,0:T(8,128)(2,1)S(1)} %dynamic-slice_bitcast_fusion.6), channel_id=1, source_target_pairs={{0,16},{2,18},{4,20},{6,22},{8,24},{10,26},{12,28},{14,30},{16,0},... | collective-permute-start | bytes 1572872 | tf_op jit(solution)/shard_map/ppermute | solution.py:135
  555.1 21.4 %collective-permute-start.52 = (bf16[1,256,512]{2,1,0:T(8,128)(2,1)S(1)}, bf16[1,256,512]{2,1,0:T(8,128)(2,1)S(1)}, u32[]{:S(2)}, u32[]{:S(2)}) collective-permute-start(bf16[1,256,512]{2,1,0:T(8,128)(2,1)S(1)} %constant_dynamic-slice_fusion.10), channel_id=1, source_target_pairs={{0,16},{2,18},{4,20},{6,22},{8,24},{10,26},{12,28},{14,30},{16,0},... | collective-permute-start | bytes 786440 | tf_op jit(solution)/shard_map/ppermute | solution.py:135
  (116 other events, 1019.9 us)

commit v2 on v1

v2 whole, which is shorter than its diff:
```python
import math
from functools import partial

import jax
import jax.numpy as jnp
import numpy as np
from jax import lax
from jax.experimental import pallas as pl
from jax.experimental.pallas import tpu as pltpu
from jax.sharding import PartitionSpec as P

HEADS = 16
HEAD_DIM = 64
GROUP = 256
PAIR = 128

ALPHA = 300.0**0.25
SCALE = 0.125
NEG = -1e30
EPS = 1e-05

ERFC_SLOPE = 0.3
ERFC_TERMS = (
    0.16918800133874554,
    0.17071528857689505,
    0.14833875833407398,
    0.2149275739002705,
    -0.09465408961006916,
    0.5477246520897923,
    -0.5122819409407986,
    0.4855649934109654,
    -0.12952325668594952,
)

BF = jnp.bfloat16
F32 = jnp.float32
VMEM_LIMIT = 56 * 2**20


def mul(left, right, left_axis, right_axis):
    return lax.dot_general(
        left, right, (((left_axis,), (right_axis,)), ((), ())), preferred_element_type=F32
    )


def mul_nn(left, right):
    return mul(left, right, 1, 0)


def mul_nt(left, right):
    return mul(left, right, 1, 1)


def mul_tn(left, right):
    return mul(left, right, 0, 0)


def kernel_call(body, grid, in_specs, out_specs, out_shape, scratch, flops, moved, scalars=0):
    return pl.pallas_call(
        body,
        grid_spec=pltpu.PrefetchScalarGridSpec(
            num_scalar_prefetch=scalars,
            grid=grid,
            in_specs=in_specs,
            out_specs=out_specs,
            scratch_shapes=scratch,
        ),
        out_shape=out_shape,
        compiler_params=pltpu.CompilerParams(vmem_limit_bytes=VMEM_LIMIT),
        cost_estimate=pl.CostEstimate(
            flops=int(flops), bytes_accessed=int(moved), transcendentals=0
        ),
    )


def whole(shape):
    return pl.BlockSpec(shape, lambda *_: (0,) * len(shape))


def shape_of(shape, dtype):
    return jax.ShapeDtypeStruct(shape, dtype)


def by_rows(rows, step, body):
    def one(at, carry):
        body(pl.ds(pl.multiple_of(at * step, step), step))
        return carry

    lax.fori_loop(0, rows // step, one, 0)


def normalize(value):
    middle = jnp.mean(value, -1, keepdims=True)
    centred = value - middle
    spread = jnp.mean(centred * centred, -1, keepdims=True)
    inverse = lax.rsqrt(spread + EPS)
    return centred * inverse, inverse


def normalize_back(cotangent, normal, inverse, gain_row):
    scaled = cotangent * gain_row
    first = jnp.mean(scaled, -1, keepdims=True)
    second = jnp.mean(scaled * normal, -1, keepdims=True)
    grad = (scaled - first - normal * second) * inverse
    gain_term = jnp.sum(cotangent * normal, 0, keepdims=True)
    bias_term = jnp.sum(cotangent, 0, keepdims=True)
    return grad, gain_term, bias_term


def head_masks():
    lane = lax.broadcasted_iota(jnp.int32, (1, PAIR), 1)
    first = (lane < HEAD_DIM).astype(F32)
    return (first.astype(BF), (1.0 - first).astype(BF))


def head_masks_scaled():
    lane = lax.broadcasted_iota(jnp.int32, (1, PAIR), 1)
    first = (lane < HEAD_DIM).astype(F32)
    return ((first * SCALE).astype(BF), ((1.0 - first) * SCALE).astype(BF))


def fill_bias(bias, row_seg, key_seg, causal):
    rows, keys = bias.shape

    def block(at):
        allowed = row_seg[at, :] == key_seg[...]
        if causal:
            row_pos = at.start + lax.broadcasted_iota(jnp.int32, (64, keys), 0)
            key_pos = lax.broadcasted_iota(jnp.int32, (64, keys), 1)
            allowed = allowed & (row_pos >= key_pos)
        bias[at, :] = jnp.where(allowed, 0.0, NEG)

    by_rows(rows, 64, block)


def row_parts(rows, keys, causal):
    half = rows // 2
    if causal:
        return ((0, half, half), (half, half, rows))
    return ((0, half, keys), (half, half, keys))


def forward_body(causal, *refs):
    if causal:
        (row_seg, key_seg, source, w_query, w_key, w_value, w_out, norms) = refs[:8]
        rest = refs[8:]
        key_source = (source,)
    else:
        (row_seg, key_seg, source, normal_in, own, other) = refs[:6]
        (w_query, w_key, w_value, w_out, norms) = refs[6:11]
        rest = refs[11:]
        key_source = (own, other)
    (q_out, k_out, v_out, o_out, lse_out, normal_out, inverse_out, low_out) = rest[:8]
    bias, total = rest[8:10]
    step = pl.program_id(0)
    rows = source.shape[0]
    keys = bias.shape[1]

    @pl.when(step == 0)
    def _():
        fill_bias(bias, row_seg, key_seg, causal)
        total[...] = jnp.zeros_like(total)

    q_out[...] = mul_nn(source[...], w_query[...]).astype(BF)
    at = 0
    for part in key_source:
        size = part.shape[0]
        k_out[at : at + size, :] = mul_nn(part[...], w_key[...]).astype(BF)
        v_out[at : at + size, :] = mul_nn(part[...], w_value[...]).astype(BF)
        at += size
    scaled = head_masks_scaled()
    lane = lax.broadcasted_iota(jnp.int32, (1, PAIR), 1)
    for begin, size, seen in row_parts(rows, keys, causal):
        rows_at = slice(begin, begin + size)
        lse_block = jnp.zeros((size, PAIR), F32)
        for pair in range(GROUP // PAIR):
            lanes = slice(pair * PAIR, (pair + 1) * PAIR)
            query = q_out[rows_at, lanes]
            key = k_out[:seen, lanes]
            value = v_out[:seen, lanes]
            outs = []
            for head in range(2):
                scores = mul_nt(query * scaled[head], key) + bias[rows_at, :seen]
                top = jnp.max(scores, -1, keepdims=True)
                weights = jnp.exp(scores - top)
                weight_sum = jnp.sum(weights, -1, keepdims=True)
                outs.append(mul_nn(weights.astype(BF), value) * (1.0 / weight_sum))
                lse_block = jnp.where(
                    lane == pair * 2 + head, top + jnp.log(weight_sum), lse_block
                )
            o_out[rows_at, lanes] = jnp.where(lane < HEAD_DIM, outs[0], outs[1]).astype(BF)
        lse_out[rows_at, :] = lse_block
    total[...] += mul_nn(o_out[...], w_out[...])

    @pl.when(step == pl.num_programs(0) - 1)
    def _():
        def block(at):
            if causal:
                base = source[at, :].astype(F32)
                gain, shift = norms[0:1, :], norms[1:2, :]
            else:
                base = normal_in[at, :] * norms[0:1, :] + norms[1:2, :]
                gain, shift = norms[2:3, :], norms[3:4, :]
            normal, inverse = normalize(ALPHA * base + total[at, :])
            normal_out[at, :] = normal
            inverse_out[at, :] = inverse
            low_out[at, :] = (normal * gain + shift).astype(BF)

        by_rows(rows, 32, block)


def attention_forward(causal, row_seg, key_seg, source, extra, weights, norms):
    rows, width = source.shape
    keys = key_seg.shape[0]
    steps = width // GROUP
    columns = pl.BlockSpec((width, GROUP), lambda g: (0, g))
    in_specs = [whole((rows, 1)), whole((1, keys)), whole((rows, width))]
    operands = [row_seg.reshape(rows, 1), key_seg.reshape(1, keys), source]
    for item in extra:
        in_specs.append(whole(item.shape))
        operands.append(item)
    in_specs += [columns] * 3 + [pl.BlockSpec((GROUP, width), lambda g: (g, 0))]
    in_specs.append(whole(norms.shape))
    row_block = pl.BlockSpec((rows, GROUP), lambda g: (0, g))
    key_block = pl.BlockSpec((keys, GROUP), lambda g: (0, g))
    out_specs = [
        row_block,
        key_block,
        key_block,
        row_block,
        pl.BlockSpec((rows, PAIR), lambda g: (0, g)),
        whole((rows, width)),
        whole((rows, 1)),
        whole((rows, width)),
    ]
    out_shape = [
        shape_of((rows, width), BF),
        shape_of((keys, width), BF),
        shape_of((keys, width), BF),
        shape_of((rows, width), BF),
        shape_of((rows, PAIR * steps), F32),
        shape_of((rows, width), F32),
        shape_of((rows, 1), F32),
        shape_of((rows, width), BF),
    ]
    scratch = [pltpu.VMEM((rows, keys), F32), pltpu.VMEM((rows, width), F32)]
    flops = 2 * rows * width * width * 4 + 4 * rows * keys * width
    call = kernel_call(
        partial(forward_body, causal), (steps,), in_specs, out_specs, out_shape, scratch, flops, 20e6
    )
    return call(*operands, *weights, norms)


def gelu_parts(value):
    bell = jnp.exp(value * value * -0.5)
    short = 1.0 / (1.0 + (ERFC_SLOPE * 0.5**0.5) * jnp.abs(value))
    series = jnp.full_like(value, 0.5 * ERFC_TERMS[-1])
    for term in ERFC_TERMS[-2::-1]:
        series = series * short + 0.5 * term
    tail = bell * short * series
    share = jnp.where(value < 0, tail, 1.0 - tail)
    return value * share, share + value * (bell * (0.5 / np.pi) ** 0.5)


def expand_body(
    core, low, normal_in, w_expand, w_contract, norms, out_grad,
    active_out, slope_out, layer_out, grad_out, low_grad, send_grad, keep_grad, norm_out,
    total,
):
    step = pl.program_id(0)
    rows, width = low.shape

    @pl.when(step == 0)
    def _():
        total[...] = jnp.zeros_like(total)

    size = rows // 2
    for part in range(2):
        at = slice(part * size, (part + 1) * size)
        active, slope = gelu_parts(mul_nn(low[at, :], w_expand[...]))
        active_out[at, :] = active.astype(BF)
        slope_out[at, :] = slope.astype(BF)
    total[...] += mul_nn(active_out[...], w_contract[...])

    @pl.when(step == pl.num_programs(0) - 1)
    def _():
        norm_out[...] = jnp.zeros_like(norm_out)
        half = width // 2
        is_low = core[0] == 0

        def block(at):
            base = normal_in[at, :] * norms[2:3, :] + norms[3:4, :]
            normal, inverse = normalize(ALPHA * base + total[at, :])
            layer_out[at, :] = (normal * norms[4:5, :] + norms[5:6, :]).astype(BF)
            grad, gain_term, bias_term = normalize_back(
                out_grad[at, :].astype(F32), normal, inverse, norms[4:5, :]
            )
            norm_out[0:1, :] += gain_term
            norm_out[1:2, :] += bias_term
            grad_out[at, :] = grad
            low_grad[at, :] = grad.astype(BF)
            left, right = grad[:, :half], grad[:, half:]
            keep_grad[at, :] = jnp.where(is_low, left, right).astype(BF)
            send_grad[at, :] = jnp.where(is_low, right, left).astype(BF)

        by_rows(rows, 32, block)


def feed_forward(core, low, normal, w_expand, w_contract, norms, out_grad):
    rows, width = low.shape
    wide = w_expand.shape[1]
    chunk = 512
    steps = wide // chunk
    in_specs = [
        whole((rows, width)),
        whole((rows, width)),
        pl.BlockSpec((width, chunk), lambda c, _: (0, c)),
        pl.BlockSpec((chunk, width), lambda c, _: (c, 0)),
        whole(norms.shape),
        whole((rows, width)),
    ]
    wide_block = pl.BlockSpec((rows, chunk), lambda c, _: (0, c))
    out_specs = [wide_block, wide_block] + [whole((rows, width))] * 3
    out_specs += [whole((rows, width // 2))] * 2 + [whole((2, width))]
    out_shape = [
        shape_of((rows, wide), BF),
        shape_of((rows, wide), BF),
        shape_of((rows, width), BF),
        shape_of((rows, width), F32),
        shape_of((rows, width), BF),
        shape_of((rows, width // 2), BF),
        shape_of((rows, width // 2), BF),
        shape_of((2, width), F32),
    ]
    call = kernel_call(
        expand_body,
        (steps,),
        in_specs,
        out_specs,
        out_shape,
        [pltpu.VMEM((rows, width), F32)],
        4 * rows * width * wide,
        36e6,
        scalars=1,
    )
    return call(core, low, normal, w_expand, w_contract, norms, out_grad)


def send_first(step, steps, core):
    half = steps // 2
    later = step // half
    return jnp.where(later == 0, 1 - core[0], core[0]) * half + step % half


def contract_back_body(
    core, low_grad, w_contract, slope, w_expand, grad_in, normal_in, inverse_in, norms,
    send_wide, keep_wide, grad_out, low_out, send_low, keep_low, norm_out,
    total,
):
    step = pl.program_id(0)
    steps = pl.num_programs(0)
    rows, width = low_grad.shape

    @pl.when(step == 0)
    def _():
        total[...] = jnp.zeros_like(total)

    wide_grad = (mul_nt(low_grad[...], w_contract[...]) * slope[...].astype(F32)).astype(BF)

    @pl.when(step < steps // 2)
    def _():
        send_wide[...] = wide_grad

    @pl.when(step >= steps // 2)
    def _():
        keep_wide[...] = wide_grad

    total[...] += mul_nt(wide_grad, w_expand[...])

    @pl.when(step == steps - 1)
    def _():
        norm_out[...] = jnp.zeros_like(norm_out)
        half = width // 2
        is_low = core[0] == 0

        def block(at):
            grad, gain_term, bias_term = normalize_back(
                ALPHA * grad_in[at, :] + total[at, :],
                normal_in[at, :],
                inverse_in[at, :],
                norms[2:3, :],
            )
            norm_out[0:1, :] += gain_term
            norm_out[1:2, :] += bias_term
            grad_out[at, :] = grad
            low_out[at, :] = grad.astype(BF)
            left, right = grad[:, :half], grad[:, half:]
            keep_low[at, :] = jnp.where(is_low, left, right).astype(BF)
            send_low[at, :] = jnp.where(is_low, right, left).astype(BF)

        by_rows(rows, 32, block)


def feed_backward(core, low_grad, w_contract, slope, w_expand, grad, normal, inverse, norms):
    rows, width = low_grad.shape
    wide = w_expand.shape[1]
    chunk = 512
    steps = wide // chunk
    half = steps // 2
    in_specs = [
        whole((rows, width)),
        pl.BlockSpec((chunk, width), lambda s, core: (send_first(s, steps, core), 0)),
        pl.BlockSpec((rows, chunk), lambda s, core: (0, send_first(s, steps, core))),
        pl.BlockSpec((width, chunk), lambda s, core: (0, send_first(s, steps, core))),
        whole((rows, width)),
        whole((rows, width)),
        whole((rows, 1)),
        whole(norms.shape),
    ]
    out_specs = [
        pl.BlockSpec((rows, chunk), lambda s, _: (0, jnp.minimum(s, half - 1))),
        pl.BlockSpec((rows, chunk), lambda s, _: (0, jnp.maximum(s - half, 0))),
        whole((rows, width)),
        whole((rows, width)),
        whole((rows, width // 2)),
        whole((rows, width // 2)),
        whole((2, width)),
    ]
    out_shape = [
        shape_of((rows, wide // 2), BF),
        shape_of((rows, wide // 2), BF),
        shape_of((rows, width), F32),
        shape_of((rows, width), BF),
        shape_of((rows, width // 2), BF),
        shape_of((rows, width // 2), BF),
        shape_of((2, width), F32),
    ]
    call = kernel_call(
        contract_back_body,
        (steps,),
        in_specs,
        out_specs,
        out_shape,
        [pltpu.VMEM((rows, width), F32)],
        4 * rows * width * wide,
        32e6,
        scalars=1,
    )
    return call(core, low_grad, w_contract, slope, w_expand, grad, normal, inverse, norms)


def backward_body(causal, core, *refs):
    (row_seg, key_seg, low_grad, w_out, query_in, key_in, value_in, o_in, lse_in) = refs[:9]
    (w_query, w_key, w_value, grad_in) = refs[9:13]
    rest = refs[13:]
    if causal:
        (send_out, keep_out, input_out, bias, total) = rest
    else:
        (normal_in, inverse_in, norms) = rest[:3]
        (send_out, keep_out, grad_out, low_out, send_low, keep_low, norm_out) = rest[3:10]
        (mem_own, mem_send, bias, total, mem_total) = rest[10:]
    step = pl.program_id(0)
    steps = pl.num_programs(0)
    rows, width = low_grad.shape
    keys = bias.shape[1]

    @pl.when(step == 0)
    def _():
        fill_bias(bias, row_seg, key_seg, causal)
        total[...] = jnp.zeros_like(total)
        if not causal:
            mem_total[...] = jnp.zeros_like(mem_total)

    o_grad = mul_nt(low_grad[...], w_out[...]).astype(BF)
    plain = head_masks()
    scaled = head_masks_scaled()
    first_lanes = lax.broadcasted_iota(jnp.int32, (1, PAIR), 1) < HEAD_DIM
    query_grads, key_grads, value_grads = [], [], []
    for pair in range(GROUP // PAIR):
        lanes = slice(pair * PAIR, (pair + 1) * PAIR)
        key_all = key_in[:, lanes]
        value_all = value_in[:, lanes]
        key_grad = value_grad = None
        query_parts = []
        for begin, size, seen in row_parts(rows, keys, causal):
            rows_at = slice(begin, begin + size)
            query = query_in[rows_at, lanes]
            grad = o_grad[rows_at, lanes]
            product = grad.astype(F32) * o_in[rows_at, lanes].astype(F32)
            key = key_all[:seen]
            value = value_all[:seen]
            query_part = None
            for head in range(2):
                mine = first_lanes if head == 0 else jnp.logical_not(first_lanes)
                delta = jnp.sum(jnp.where(mine, product, 0.0), -1, keepdims=True)
                head_query = query * scaled[head]
                head_grad = grad * plain[head]
                lse = lse_in[rows_at, pair * 2 + head : pair * 2 + head + 1]
                prob = jnp.exp(mul_nt(head_query, key) + bias[rows_at, :seen] - lse)
                score_grad = (prob * (mul_nt(head_grad, value) - delta)).astype(BF)
                value_term = mul_tn(prob.astype(BF), head_grad)
                key_term = mul_tn(score_grad, head_query)
                query_term = mul_nn(score_grad, key * scaled[head])
                query_part = query_term if query_part is None else query_part + query_term
                if seen < keys:
                    zeros = jnp.zeros((keys - seen, PAIR), F32)
                    value_term = jnp.concatenate([value_term, zeros])
                    key_term = jnp.concatenate([key_term, zeros])
                value_grad = value_term if value_grad is None else value_grad + value_term
                key_grad = key_term if key_grad is None else key_grad + key_term
            query_parts.append(query_part)
        query_grads.append(jnp.concatenate(query_parts).astype(BF))
        key_grads.append(key_grad.astype(BF))
        value_grads.append(value_grad.astype(BF))
    query_grad = jnp.concatenate(query_grads, axis=1)
    key_grad = jnp.concatenate(key_grads, axis=1)
    value_grad = jnp.concatenate(value_grads, axis=1)

    @pl.when(step < steps // 2)
    def _():
        send_out[0], send_out[1], send_out[2] = query_grad, key_grad, value_grad

    @pl.when(step >= steps // 2)
    def _():
        keep_out[0], keep_out[1], keep_out[2] = query_grad, key_grad, value_grad

    if causal:
        joined = jnp.concatenate([query_grad, key_grad, value_grad], axis=1)
        weights = jnp.concatenate([w_query[...], w_key[...], w_value[...]], axis=1)
        total[...] += mul_nt(joined, weights)
    else:
        total[...] += mul_nt(query_grad, w_query[...])
        joined = jnp.concatenate([key_grad, value_grad], axis=1)
        weights = jnp.concatenate([w_key[...], w_value[...]], axis=1)
        mem_total[...] += mul_nt(joined, weights)

    @pl.when(step == steps - 1)
    def _():
        if causal:

            def block(at):
                input_out[at, :] = (ALPHA * grad_in[at, :] + total[at, :]).astype(BF)

            by_rows(rows, 64, block)
        else:
            own_rows = mem_own.shape[0]
            mem_own[...] = mem_total[:own_rows, :].astype(BF)
            mem_send[...] = mem_total[own_rows:, :].astype(BF)
            norm_out[...] = jnp.zeros_like(norm_out)
            half = width // 2
            is_low = core[0] == 0

            def block(at):
                grad, gain_term, bias_term = normalize_back(
                    ALPHA * grad_in[at, :] + total[at, :],
                    normal_in[at, :],
                    inverse_in[at, :],
                    norms[0:1, :],
                )
                norm_out[0:1, :] += gain_term
                norm_out[1:2, :] += bias_term
                grad_out[at, :] = grad
                low_out[at, :] = grad.astype(BF)
                left, right = grad[:, :half], grad[:, half:]
                keep_low[at, :] = jnp.where(is_low, left, right).astype(BF)
                send_low[at, :] = jnp.where(is_low, right, left).astype(BF)

            by_rows(rows, 32, block)


def attention_backward(causal, core, row_seg, key_seg, low_grad, w_out, saved, weights, grad, extra):
    rows, width = low_grad.shape
    keys = key_seg.shape[0]
    steps = width // GROUP
    half = steps // 2

    def block(shape, spread):
        def index(s, core):
            group = send_first(s, steps, core)
            return (group, 0) if spread == 0 else (0, group)

        return pl.BlockSpec(shape, index)

    row_block = block((rows, GROUP), 1)
    key_block = block((keys, GROUP), 1)
    columns = block((width, GROUP), 1)
    in_specs = [
        whole((rows, 1)),
        whole((1, keys)),
        whole((rows, width)),
        block((GROUP, width), 0),
        row_block,
        key_block,
        key_block,
        row_block,
        block((rows, PAIR), 1),
        columns,
        columns,
        columns,
        whole((rows, width)),
    ]
    in_specs += [whole(item.shape) for item in extra]
    out_specs = [
        pl.BlockSpec((3, rows, GROUP), lambda s, _: (0, 0, jnp.minimum(s, half - 1))),
        pl.BlockSpec((3, rows, GROUP), lambda s, _: (0, 0, jnp.maximum(s - half, 0))),
    ]
    out_shape = [shape_of((3, rows, width // 2), BF)] * 2
    scratch = [pltpu.VMEM((rows, keys), F32), pltpu.VMEM((rows, width), F32)]
    if causal:
        out_specs += [whole((rows, width))]
        out_shape += [shape_of((rows, width), BF)]
    else:
        out_specs += [whole((rows, width))] * 2 + [whole((rows, width // 2))] * 2
        out_specs += [whole((2, width))] + [whole((keys // 2, width))] * 2
        out_shape += [
            shape_of((rows, width), F32),
            shape_of((rows, width), BF),
            shape_of((rows, width // 2), BF),
            shape_of((rows, width // 2), BF),
            shape_of((2, width), F32),
            shape_of((keys // 2, width), BF),
            shape_of((keys // 2, width), BF),
        ]
        scratch += [pltpu.VMEM((keys, width), F32)]
    flops = 2 * rows * width * width * 4 + 10 * rows * keys * width
    call = kernel_call(
        partial(backward_body, causal),
        (steps,),
        in_specs,
        out_specs,
        out_shape,
        scratch,
        flops,
        24e6,
        scalars=1,
    )
    return call(
        core,
        row_seg.reshape(rows, 1),
        key_seg.reshape(1, keys),
        low_grad,
        w_out,
        *saved,
        *weights,
        grad,
        *extra,
    )


def swap_mem(tensor):
    return lax.ppermute(tensor, "mem", [(0, 1), (1, 0)])


def tie(value, *after):
    return lax.optimization_barrier((value, after))[0]


class Plan:
    def __init__(self, steps, row_count):
        self.steps = steps
        self.row_count = row_count
        bit_count = row_count.bit_length() - 1
        sizes = [2 ** (bit_count - 2) if step == "group" else 2 for step in steps]
        self.relative, self.fixed = [], []
        for k in range(row_count):
            mask = fixed = 0
            rest = row_count
            for step, size in zip(steps, sizes):
                rest //= size
                digit = k // rest % size
                if step == "group":
                    fixed = digit << 2
                else:
                    mask |= digit << step
            self.relative.append(mask)
            self.fixed.append(fixed)
        self.own_bits = sum(1 << step for step in steps if step != "group")
        self.groups = [list(range(low, row_count, 4)) for low in range(4)]

    def at_places(self, chip):
        own = chip & self.own_bits
        return (own ^ jnp.asarray(self.relative, jnp.int32)) | jnp.asarray(self.fixed, jnp.int32)

    def permute(self, tensor, bit):
        pairs = [(i, i ^ (1 << bit)) for i in range(self.row_count)]
        return lax.ppermute(tensor, "row", pairs)

    def group_sum(self, tensor):
        return lax.psum_scatter(
            tensor, "row", scatter_dimension=0, tiled=True, axis_index_groups=self.groups
        )


def group_sum_joined(plan, tensors):
    count = plan.row_count // 4
    lanes = math.gcd(*(tensor.shape[1] for tensor in tensors))
    pieces, sizes = [], []
    for tensor in tensors:
        blocks = tensor.reshape(count, -1, tensor.shape[1])
        sizes.append(blocks.shape[1:])
        pieces += [blocks[:, :, at : at + lanes] for at in range(0, blocks.shape[2], lanes)]
    joined = jnp.concatenate(pieces, axis=1)
    summed = plan.group_sum(joined)[0]
    outs, at = [], 0
    for rows, width in sizes:
        parts = []
        for _ in range(width // lanes):
            parts.append(summed[at : at + rows])
            at += rows
        outs.append(jnp.concatenate(parts, axis=1) if len(parts) > 1 else parts[0])
    return outs


class Chain:
    def __init__(self, plan, blocks):
        self.plan = plan
        self.left = list(plan.steps)
        self.got = None
        self.total = None
        if self.left[0] == "group":
            self.sent = blocks[0]
            self.left.pop(0)
            self.total = plan.group_sum(self.sent)
        else:
            self.keep, self.sent = blocks
            self.got = plan.permute(self.sent, self.left.pop(0))

    def sum_rows(self, rows):
        if self.got is None:
            return self.total[rows]
        return self.keep[rows].astype(F32) + self.got[rows].astype(F32)

    def merged(self):
        assert self.left.pop(0) == "group"
        return self.sum_rows(slice(None)).astype(BF)

    def advance(self):
        if self.left[0] == "group":
            self.sent = self.merged()
            self.total, self.got = self.plan.group_sum(self.sent), None
            return
        rows = (self.keep if self.got is not None else self.total).shape[0]
        sent = self.sum_rows(slice(rows // 2, None)).astype(BF)
        self.keep = self.sum_rows(slice(None, rows // 2)).astype(BF)
        self.sent = sent
        self.got = self.plan.permute(sent, self.left.pop(0))

    def result(self):
        assert not self.left
        return self.sum_rows(slice(None)).astype(F32)


def swap_mem(tensor):
    return lax.ppermute(tensor, "mem", [(0, 1), (1, 0)])


def weight_grads_body(spans, item_of_step, count, at_place, *refs):
    items = len(set(item_of_step))
    sources = refs[: 2 * items]
    own_grad, other_grad = refs[2 * items : 2 * items + 2]
    outs = refs[2 * items + 2 : -1]
    whole_grad = refs[-1]
    step = pl.program_id(0)
    _, block_rows, lanes = whole_grad.shape
    joined = max(16 // block_rows, 1)
    for item in range(items):
        steps = [at for at, which in enumerate(item_of_step) if which == item]

        @pl.when((step >= steps[0]) & (step <= steps[-1]))
        def _():
            own, other = sources[2 * item : 2 * item + 2]
            grad = mul_tn(own[...], own_grad[0]) + mul_tn(other[...], other_grad[0])
            whole_grad[...] = grad.reshape(count, block_rows, lanes)

    at_out = 0
    for number, (begin, chunks, halves) in enumerate(spans):
        targets = outs[at_out : at_out + (2 if halves else 1)]
        at_out += len(targets)

        @pl.when((step >= begin) & (step < begin + chunks))
        def _():
            size = count // len(targets)
            for part, out in enumerate(targets):
                for k in range(0, size, joined):
                    base = number * count + part * size + k
                    blocks = [whole_grad[at_place[base + i]] for i in range(joined)]
                    rows = slice(k * block_rows, (k + joined) * block_rows)
                    out[rows, :] = jnp.concatenate(blocks).astype(BF)


def weight_grads(chip, sources, item_of_step, own_grads, other_grads, chunk, outs):
    if own_grads.ndim == 2:
        own_grads, other_grads = own_grads[None], other_grads[None]
    tokens, width = sources[0][0].shape
    across = own_grads.shape[2] // chunk
    count = outs[0][1].row_count
    steps = len(item_of_step)
    grads_block = pl.BlockSpec((1, tokens, chunk), lambda i, _: (i // across, 0, i % across))
    in_specs = [whole((tokens, width))] * (2 * len(sources)) + [grads_block] * 2
    out_specs, out_shape, spans, parts = [], [], [], []
    begin = 0
    for chunks, plan in outs:
        halves = plan.steps[0] != "group"
        pieces = 2 if halves else 1

        def index(i, _, begin=begin, chunks=chunks):
            return (0, jnp.clip(i - begin, 0, chunks - 1))

        for _ in range(pieces):
            out_specs.append(pl.BlockSpec((width // pieces, chunk), index))
            out_shape.append(shape_of((width // pieces, chunk * chunks), BF))
        spans.append((begin, chunks, halves))
        parts.append(pieces)
        begin += chunks
    call = kernel_call(
        partial(weight_grads_body, spans, item_of_step, count),
        (steps,),
        in_specs,
        out_specs,
        out_shape,
        [pltpu.VMEM((count, width // count, chunk), F32)],
        4 * tokens * width * chunk * steps,
        4 * tokens * (width * len(sources) + chunk * steps) + 2 * width * chunk * steps,
        scalars=1,
    )
    at_place = jnp.concatenate([plan.at_places(chip) for _, plan in outs])
    flat = [item for pair in sources for item in pair]
    results = call(at_place, *flat, own_grads, other_grads)
    blocks, at = [], 0
    for pieces in parts:
        blocks.append(results[at : at + pieces])
        at += pieces
    return blocks


def shards(
    row_count,
    inputs,
    memory,
    target_seg,
    memory_seg,
    self_query,
    self_key,
    self_value,
    self_out,
    cross_query,
    cross_key,
    cross_value,
    cross_out,
    expand_weight,
    contract_weight,
    norm_params,
    out_grad,
):
    core = lax.axis_index("mem").astype(jnp.int32).reshape(1)
    chip = lax.axis_index("row").astype(jnp.int32)
    upper = list(range(2, row_count.bit_length() - 1))
    plan_x = Plan([0, 1, "group"], row_count)
    plan_y = Plan([1, 0, "group"], row_count)
    plan_z = Plan(["group", 0, 1], row_count)
    last_x = Plan([0, 1] + upper, row_count)
    last_y = Plan([1] + upper + [0], row_count)
    last_z = Plan(upper + [0, 1], row_count)

    other_inputs = swap_mem(inputs)
    other_memory = swap_mem(memory)
    pair_seg = jnp.concatenate([memory_seg, swap_mem(memory_seg)])

    self_saved = attention_forward(
        True,
        target_seg,
        target_seg,
        inputs,
        (),
        (self_query, self_key, self_value, self_out),
        norm_params,
    )
    self_o, normal_one, inverse_one, low_one = self_saved[3], *self_saved[5:]
    cross_saved = attention_forward(
        False,
        target_seg,
        pair_seg,
        low_one,
        (normal_one, memory, other_memory),
        (cross_query, cross_key, cross_value, cross_out),
        norm_params,
    )
    cross_o, normal_two, inverse_two, low_two = cross_saved[3], *cross_saved[5:]
    (active, slope, layer_out, grad_three, low_three, send_three, keep_three, norm_three) = (
        feed_forward(core, low_two, normal_two, expand_weight, contract_weight, norm_params, out_grad)
    )
    other_active = swap_mem(active)
    got_three = swap_mem(send_three)
    other_self_o = swap_mem(self_o)
    other_one = swap_mem(low_one)
    other_cross_o = swap_mem(cross_o)
    other_two = swap_mem(low_two)
    (send_wide, keep_wide, grad_two, low_grad_two, send_two, keep_two, norm_two) = feed_backward(
        core,
        low_three,
        contract_weight,
        slope,
        expand_weight,
        grad_three,
        normal_two,
        inverse_two,
        norm_params,
    )
    got_wide = swap_mem(send_wide)
    got_two = swap_mem(send_two)

    blocks = weight_grads(
        chip,
        [(tie(active, low_grad_two), other_active)],
        [0, 0],
        keep_three,
        got_three,
        256,
        [(1, plan_x), (1, plan_y)],
    )
    contract_x, contract_y = Chain(plan_x, blocks[0]), Chain(plan_y, blocks[1])
    blocks = weight_grads(
        chip,
        [(tie(low_two, contract_x.sent, contract_y.sent), other_two)],
        [0, 0, 0, 0],
        keep_wide,
        got_wide,
        512,
        [(2, plan_z), (2, plan_x)],
    )
    expand_z, expand_x = Chain(plan_z, blocks[0]), Chain(plan_x, blocks[1])
    blocks = weight_grads(
        chip,
        [(tie(cross_o, expand_z.sent, expand_x.sent), other_cross_o)],
        [0],
        keep_two,
        got_two,
        512,
        [(1, plan_y)],
    )
    cross_out_y = Chain(plan_y, blocks[0])

    (send_c, keep_c, grad_one, low_grad_one, send_one, keep_one, norm_one, mem_own, mem_send) = (
        attention_backward(
            False,
            core,
            target_seg,
            pair_seg,
            tie(low_grad_two, cross_out_y.sent),
            cross_out,
            (cross_saved[0], cross_saved[1], cross_saved[2], cross_o, cross_saved[4]),
            (cross_query, cross_key, cross_value),
            grad_two,
            (normal_one, inverse_one, norm_params),
        )
    )
    memory_grad = (mem_own.astype(F32) + swap_mem(mem_send).astype(F32)).astype(BF)
    got_c = swap_mem(send_c)
    got_one = swap_mem(send_one)

    contract_x.got, contract_y.got, expand_x.got = tie(
        (contract_x.got, contract_y.got, expand_x.got), low_grad_one
    )
    for chain in (contract_x, contract_y, expand_x):
        chain.advance()
    norm_grad = jnp.concatenate([norm_one, norm_two, norm_three])
    norm_grad = norm_grad.reshape(2, 3, norm_grad.shape[1])
    norm_half = norm_grad[core[0]] + swap_mem(norm_grad[1 - core[0]])
    pair_memory = jnp.concatenate([memory, other_memory])
    turned_memory = jnp.concatenate([other_memory, memory])
    blocks = weight_grads(
        chip,
        [
            (tie(low_one, contract_x.sent, contract_y.sent, expand_x.sent), other_one),
            (pair_memory, turned_memory),
        ],
        [0, 0, 1, 1, 1, 1],
        keep_c,
        got_c,
        256,
        [(3, plan_x), (3, plan_y)],
    )
    cross_x, cross_y = Chain(plan_x, blocks[0]), Chain(plan_y, blocks[1])
    blocks = weight_grads(
        chip,
        [(tie(self_o, cross_x.sent, cross_y.sent), other_self_o)],
        [0],
        keep_one,
        got_one,
        512,
        [(1, last_z)],
    )
    block_rows = self_o.shape[1] // row_count
    norm_blocks = norm_half.reshape(3, row_count, block_rows).transpose(1, 0, 2)
    norm_blocks = jnp.pad(norm_blocks, ((0, 0), (0, block_rows - 3), (0, PAIR - block_rows)))
    norm_blocks = jnp.take(norm_blocks, last_z.at_places(chip), axis=0).astype(BF)
    norm_blocks = norm_blocks.reshape(2, -1, PAIR)
    self_out_z = Chain(
        last_z, [jnp.concatenate([blocks[0][i], norm_blocks[i]], axis=1) for i in range(2)]
    )
    contract_x.got, contract_y.got, expand_x.got, cross_out_y.got = tie(
        (contract_x.got, contract_y.got, expand_x.got, cross_out_y.got), self_out_z.sent
    )
    cross_out_y.advance()
    merging = (contract_x, contract_y, expand_x)
    merged = [chain.merged() for chain in merging]
    merged_sums = group_sum_joined(plan_x, merged)

    send_s, keep_s, input_grad = attention_backward(
        True,
        core,
        target_seg,
        target_seg,
        tie(low_grad_one, cross_out_y.sent, merged),
        self_out,
        (self_saved[0], self_saved[1], self_saved[2], self_o, self_saved[4]),
        (self_query, self_key, self_value),
        grad_one,
        (),
    )
    got_s = swap_mem(send_s)
    cross_x.got, cross_y.got, self_out_z.got, cross_out_y.got = tie(
        (cross_x.got, cross_y.got, self_out_z.got, cross_out_y.got), input_grad
    )
    for chain in (cross_x, cross_y, self_out_z):
        chain.advance()
    blocks = weight_grads(
        chip,
        [(tie(inputs, cross_x.sent, cross_y.sent, self_out_z.sent), other_inputs)],
        [0, 0, 0],
        keep_s,
        got_s,
        512,
        [(1, last_x), (1, last_y), (1, last_z)],
    )
    self_x, self_y = Chain(last_x, blocks[0]), Chain(last_y, blocks[1])
    self_z = Chain(last_z, blocks[2])
    expand_z.total = tie(expand_z.total, self_x.sent, self_y.sent, self_z.sent)
    expand_z.advance()
    cross_out_merged = cross_out_y.merged()
    cross_merged = [cross_x.merged(), cross_y.merged(), cross_out_merged]
    cross_sums = group_sum_joined(plan_x, cross_merged)
    self_out_z.advance()
    self_x.advance(), self_y.advance(), self_z.advance()
    expand_z.advance()
    while self_x.left:
        for chain in (self_x, self_y, self_z, self_out_z):
            if chain.left:
                chain.advance()
    self_out_sum = self_out_z.result()
    own_lanes = self_out.shape[1] // 2
    cross_first, cross_second = cross_sums[0].astype(F32), cross_sums[1].astype(F32)
    chunk = 256
    return (
        layer_out,
        input_grad,
        memory_grad,
        self_x.result(),
        self_y.result(),
        self_z.result(),
        self_out_sum[:, :own_lanes],
        cross_first[:, : 2 * chunk],
        jnp.concatenate([cross_first[:, 2 * chunk :], cross_second[:, :chunk]], axis=1),
        cross_second[:, chunk:],
        cross_sums[2].astype(F32),
        jnp.concatenate([expand_z.result(), merged_sums[2].astype(F32)], axis=1),
        jnp.concatenate([merged_sums[0], merged_sums[1]], axis=1).astype(F32),
        self_out_sum[:3, own_lanes : own_lanes + block_rows],
    )


def solution(mesh):
    split_rows = P(("row", "mem"), None)
    split_ids = P(("row", "mem"))
    in_specs = (split_rows, split_rows, split_ids, split_ids) + (P(),) * 11 + (split_rows,)
    out_specs = (split_rows,) * 3 + (P("row", "mem"),) * 10 + (P("mem", "row"),)
    return jax.shard_map(
        partial(shards, mesh.shape["row"]),
        mesh=mesh,
        in_specs=in_specs,
        out_specs=out_specs,
        check_vma=False,
    )
```

time: 585 us -> 398 us (0.68)
  matrix products: 218 us -> 0 us
  Pallas kernels: 0 us -> 213 us
  waiting for transfers between devices: 153 us -> 66.3 us
  other arithmetic: 82 us -> 28.1 us
  local copies, waits for them, and re-layouts: 51.1 us -> 12.4 us
  starting transfers between devices: 74.5 us -> 59.2 us
  between operations: 2.51 us -> 14.7 us
    dot_general x42 -> x0, matrix products: 218 us -> none  [the longest x10 53.8 us: project(): return jnp.dot(left_side, right_side, preferred_element_type=jnp.float32)]
    pallas_call x0 -> x12, Pallas kernels: none -> 213 us  [the longest x2 61 us: attention_backward(): call(core, row_seg.reshape(rows, 1), key_seg.reshape(1, keys), low_grad,...]
    ppermute x44 -> x30, waiting for transfers between devices: 151 us -> 57.2 us  [permute(): return lax.ppermute(tensor, 'row', pairs)]
    convert_element_type x46 -> x31, other arithmetic: 49.1 us -> 17.5 us  [the longest x11 6.51 us: advance(): sent = self.sum_rows(slice(rows // 2, None)).astype(BF)]
    ppermute x44 -> x30, starting transfers between devices: 70.8 us -> 43.6 us  [permute(): return lax.ppermute(tensor, 'row', pairs)]
    reduce_sum x10 -> x0, other arithmetic: 23.9 us -> none  [the longest x1 9.25 us: self_forward(): jnp.sum(jnp.exp(scores - row_top), -1, keepdims=True)]
    dynamic_slice x32 -> x0, local copies, waits for them, and re-layouts: 16.8 us -> none  [the longest x10 13.5 us: pair_half(): send = lax.dynamic_slice_in_dim(low, (1 - core) * half, half, 1)]
    convert_element_type x8 -> x0, local copies, waits for them, and re-layouts: 16.2 us -> none  [the longest x1 2.66 us: shards(): value_rows = split_heads(project(inputs, self_value).astype(jnp.bfloat16))]
  transfers between devices with their start and end apart: 58 -> 49, of which waited for: 26 -> 14; matrix products, arithmetic and copies ran while one was open for 20% -> 8% of each run, Pallas kernels for 0% -> 40%
where the time goes in v2:
time: 398 us; the launch traced here: 394 us
  Pallas kernels  213 us (54%)
  waiting for transfers between devices  66.3 us (17%)
  starting transfers between devices  59.2 us (15%)
  other arithmetic  28.1 us (7%)
  between operations  14.7 us (4%)
  local copies, waits for them, and re-layouts  12.4 us (3%)
    pallas_call x2, Pallas kernels, attention_backward(): call(core, row_seg.reshape(rows, 1), key_seg.reshape(1, keys), low_grad,...  61 us
    ppermute x30, waiting for transfers between devices, permute(): return lax.ppermute(tensor, 'row', pairs)  57.2 us
    pallas_call x6, Pallas kernels, weight_grads(): results = call(at_place, *flat, own_grads, other_grads)  50.5 us
    pallas_call x2, Pallas kernels, attention_forward(): return call(*operands, *weights, norms)  49.4 us
    ppermute x30, starting transfers between devices, permute(): return lax.ppermute(tensor, 'row', pairs)  43.6 us
    pallas_call x1, Pallas kernels, feed_forward(): return call(core, low, normal, w_expand, w_contract, norms, out_grad)  29.5 us
    pallas_call x1, Pallas kernels, feed_backward(): call(core, low_grad, w_contract, slope, w_expand, grad, normal, inverse,...  22.5 us
    reduce_scatter x3, starting transfers between devices, group_sum(): lax.psum_scatter(tensor, 'row', scatter_dimension=0, tiled=True, axis_ind...  11.6 us
  transfers between devices with their start and end apart: 49, of which 14 were waited for; matrix products, arithmetic and copies ran while one was open for 8% of the time, Pallas kernels for 40%

profile of v2, /device:TPU:0, one launch (start us, length us, event | category | flops | bytes accessed | tf_op | source)
XLA Modules:
  0.0 393.7 jit_solution(6803490495901502796)
XLA Ops:
  9.3 24.0 %shard_map.479 = (bf16[512,1024]{1,0:T(8,128)(2,1)}, bf16[512,1024]{1,0:T(8,128)(2,1)}, bf16[512,1024]{1,0:T(8,128)(2,1)}, bf16[512,1024]{1,0:T(8,128)(2,1)}, f3...) custom-call(s32[512,1]{1,0:T(8,128)} %copy.59.refs_0_, ...), custom_call_target="tpu_custom_call" | custom-call | flops 5368709120 | bytes 20000000 | tf_op jit(solution)/shard_map/pallas_call | solution.py:251
  34.7 25.5 %shard_map.480 = (bf16[512,1024]{1,0:T(8,128)(2,1)}, bf16[512,1024]{1,0:T(8,128)(2,1)}, bf16[512,1024]{1,0:T(8,128)(2,1)}, bf16[512,1024]{1,0:T(8,128)(2,1)}, f3...) custom-call(s32[512,1]{1,0:T(8,128)} %copy.59.refs_0_, ...), custom_call_target="tpu_custom_call" | custom-call | flops 5368709120 | bytes 20000000 | tf_op jit(solution)/shard_map/pallas_call | solution.py:251
  60.2 29.5 %shard_map.481 = (bf16[512,4096]{1,0:T(8,128)(2,1)}, bf16[512,4096]{1,0:T(8,128)(2,1)}, bf16[512,1024]{1,0:T(8,128)(2,1)}, f32[512,1024]{1,0:T(8,128)}, bf16[512...) custom-call(s32[1]{0:T(128)} %bitcast.core, ...), custom_call_target="tpu_custom_call" | custom-call | flops 8589934592 | bytes 36000000 | tf_op jit(solution)/shard_map/pallas_call | solution.py:346
  90.3 22.5 %shard_map.482 = (bf16[512,2048]{1,0:T(8,128)(2,1)}, bf16[512,2048]{1,0:T(8,128)(2,1)}, f32[512,1024]{1,0:T(8,128)}, bf16[512,1024]{1,0:T(8,128)(2,1)}, bf16[512...) custom-call(s32[1]{0:T(128)} %bitcast.core, bf16[512,1024]{1,0:T(8,128)(2,1)} %get-tuple-element.103.low_grad, ...), custom_call_target="tpu_custom_call" | custom-call | flops 8589934592 | bytes 32000000 | tf_op jit(solution)/shard_map/pallas_call | solution.py:449
  115.3 5.8 %collective-permute-done.3 = bf16[512,512]{1,0:T(8,128)(2,1)} collective-permute-done((bf16[512,512]{1,0:T(8,128)(2,1)}, bf16[512,512]{1,0:T(8,128)(2,1)}, u32[]{:S(2)}, u32[]{:S(2)}) %collective-permute-start.3) | collective-permute-done | bytes 524320 | tf_op jit(solution)/shard_map/ppermute | solution.py:754
  121.2 12.3 %shard_map.483 = (bf16[2048,256]{1,0:T(8,128)(2,1)}, bf16[2048,256]{1,0:T(8,128)(2,1)}, bf16[2048,256]{1,0:T(8,128)(2,1)}, bf16[2048,256]{1,0:T(8,128)(2,1)}) custom-call(s32[32]{0:T(128)} %get-tuple-element.218.at_place, bf16[512,4096]{1,0:T(8,128)(2,1)} %get-tuple-element.110.refs_0_, bf16[512,4096]{1,0:T(8,128)(2,1)} %collective-permute-done.2.refs_1_, ...), custom_call_target="tpu_custom_call" | custom-call | flops 4294967296 | bytes 13631488 | tf_op jit(solution)/shard_map/pallas_call | solution.py:828
  133.5 2.9 collective-permute-start.8
  139.3 9.8 %shard_map.484 = (bf16[1024,1024]{1,0:T(8,128)(2,1)}, bf16[512,1024]{1,0:T(8,128)(2,1)}, bf16[512,1024]{1,0:T(8,128)(2,1)}) custom-call(s32[32]{0:T(128)} %get-tuple-element.219.at_place, bf16[512,1024]{1,0:T(8,128)(2,1)} %get-tuple-element.115.low.refs_0_, bf16[512,1024]{1,0:T(8,128)(2,1)} %collective-permute-done.4.refs_1_, ...), custom_call_target="tpu_custom_call" | custom-call | flops 4294967296 | bytes 10485760 | tf_op jit(solution)/shard_map/pallas_call | solution.py:828
  149.7 4.8 %shard_map.485 = (bf16[512,512]{1,0:T(8,128)(2,1)}, bf16[512,512]{1,0:T(8,128)(2,1)}) custom-call(s32[16]{0:T(128)} %copy-done.21, bf16[512,1024]{1,0:T(8,128)(2,1)} %get-tuple-element.120.refs_0_.refs_7_, bf16[512,1024]{1,0:T(8,128)(2,1)} %collective-permute-done.6.refs_1_, bf16[1,512,512]{2,1,0:T(8,128)(2,1)} %bitcast.80, bf16[1,512,512]{2,1,0:T(8,128)(2,1)} %bitcast.9.refs_3_), custom_call_target="tpu_custom_call" | custom-call | flops 1073741824 | bytes 4194304 | tf_op jit(solution)/shard_map/pallas_call | solution.py:828
  154.5 33.6 %shard_map.486 = (bf16[3,512,512]{2,1,0:T(8,128)(2,1)}, bf16[3,512,512]{2,1,0:T(8,128)(2,1)}, f32[512,1024]{1,0:T(8,128)}, bf16[512,1024]{1,0:T(8,128)(2,1)}, bf...) custom-call(s32[1]{0:T(128)} %bitcast.core, ...), custom_call_target="tpu_custom_call" | custom-call | flops 6979321856 | bytes 24000000 | tf_op jit(solution)/shard_map/pallas_call | solution.py:637
  190.6 11.6 %reduce-scatter.8.cloned.1.call-start = ((), (), s32[]{:S(2)}) async-start(), calls=%async_computation.5 | async-start | bytes 1966080 | tf_op jit(solution)/shard_map/reduce_scatter | solution.py:689
  203.6 3.2 collective-permute-done.20
  207.4 2.5 add_convert_fusion
  212.7 1.8 collective-permute-start.13
  216.6 10.3 %shard_map.487 = (bf16[512,768]{1,0:T(8,128)(2,1)}, bf16[512,768]{1,0:T(8,128)(2,1)}, bf16[512,768]{1,0:T(8,128)(2,1)}, bf16[512,768]{1,0:T(8,128)(2,1)}) custom-call(s32[32]{0:T(128)} %get-tuple-element.218.at_place, bf16[512,1024]{1,0:T(8,128)(2,1)} %get-tuple-element.140.refs_2_.refs_0_, bf16[512,1024]{1,0:T(8,128)(2,1)} %copy-done.35, ...), custom_call_target="tpu_custom_call" | custom-call | flops 3221225472 | bytes 10485760 | tf_op jit(solution)/shard_map/pallas_call | solution.py:828
  226.9 4.8 %shard_map.488 = (bf16[512,512]{1,0:T(8,128)(2,1)}, bf16[512,512]{1,0:T(8,128)(2,1)}) custom-call(s32[16]{0:T(128)} %copy-done.25, bf16[512,1024]{1,0:T(8,128)(2,1)} %get-tuple-element.145.refs_0_.refs_7_, bf16[512,1024]{1,0:T(8,128)(2,1)} %copy-done.34, bf16[1,512,512]{2,1,0:T(8,128)(2,1)} %bitcast.79, bf16[1,512,512]{2,1,0:T(8,128)(2,1)} %bitcast.11.refs_3_), custom_call_target="tpu_custom_call" | custom-call | flops 1073741824 | bytes 4194304 | tf_op jit(solution)/shard_map/pallas_call | solution.py:828
  231.7 2.0 pad_maximum_fusion.2
  236.1 2.0 collective-permute-start.23
  238.1 9.2 %collective-permute-done.11 = bf16[1024,256]{1,0:T(8,128)(2,1)S(1)} collective-permute-done((bf16[1024,256]{1,0:T(8,128)(2,1)S(1)}, bf16[1024,256]{1,0:T(8,128)(2,1)S(1)}, u32[]{:S(2)}, u32[]{:S(2)}) %collective-permute-start.11) | collective-permute-done | bytes 524320 | tf_op jit(solution)/shard_map/ppermute | solution.py:686
  252.2 27.4 %shard_map.489 = (bf16[3,512,512]{2,1,0:T(8,128)(2,1)}, bf16[3,512,512]{2,1,0:T(8,128)(2,1)}, bf16[512,1024]{1,0:T(8,128)(2,1)}) custom-call(s32[1]{0:T(128)} %bitcast.core, s32[512,1]{1,0:T(8,128)} %copy.59.refs_0_, s32[1,512]{1,0:T(1,128)} %bitcast.74, bf16[512,1024]{1,0:T(8,128)(2,1)} %get-tuple-element.156.refs_2_, bf16[1024,1024]{1,0:T(8,128)(2,1)} %refs_3_.5, ...), custom_call_target="tpu_custom_call" | custom-call | flops 6979321856 | bytes 24000000 | tf_op jit(solution)/shard_map/pallas_call | solution.py:637
  283.4 2.7 collective-permute-start.39
  287.8 13.4 %collective-permute-done.39 = bf16[256,640]{1,0:T(8,128)(2,1)S(1)} collective-permute-done((bf16[256,640]{1,0:T(8,128)(2,1)S(1)}, bf16[256,640]{1,0:T(8,128)(2,1)S(1)}, u32[]{:S(2)}, u32[]{:S(2)}) %collective-permute-start.39) | collective-permute-done | bytes 327712 | tf_op jit(solution)/shard_map/ppermute | solution.py:686
  304.7 8.5 %shard_map.490 = (bf16[512,512]{1,0:T(8,128)(2,1)}, bf16[512,512]{1,0:T(8,128)(2,1)}, bf16[512,512]{1,0:T(8,128)(2,1)}, bf16[512,512]{1,0:T(8,128)(2,1)}, bf16[5...) custom-call(s32[48]{0:T(128)} %pad_add_fusion.3.at_place, bf16[512,1024]{1,0:T(8,128)(2,1)} %refs_0_, ...), custom_call_target="tpu_custom_call" | custom-call | flops 3221225472 | bytes 8388608 | tf_op jit(solution)/shard_map/pallas_call | solution.py:828
  321.5 7.3 %collective-permute-done.35 = bf16[512,512]{1,0:T(8,128)(2,1)S(1)} collective-permute-done((bf16[512,512]{1,0:T(8,128)(2,1)}, bf16[512,512]{1,0:T(8,128)(2,1)S(1)}, u32[]{:S(2)}, u32[]{:S(2)}) %collective-permute-start.35) | collective-permute-done | bytes 524320 | tf_op jit(solution)/shard_map/ppermute | solution.py:686
  329.0 7.8 %collective-permute-start.36 = (bf16[256,512]{1,0:T(8,128)(2,1)S(1)}, bf16[256,512]{1,0:T(8,128)(2,1)S(1)}, u32[]{:S(2)}, u32[]{:S(2)}) collective-permute-start(bf16[256,512]{1,0:T(8,128)(2,1)S(1)} %get-tuple-element.187), channel_id=1, source_target_pairs={{0,16},{2,18},{4,20},{6,22},{8,24},{10,26},{12,28},{14,30},{16,0},... | collective-permute-start | bytes 786440 | tf_op jit(solution)/shard_map/ppermute | solution.py:686
  336.9 3.5 collective-permute-start.32
  340.6 14.1 %collective-permute-done.36 = bf16[256,512]{1,0:T(8,128)(2,1)S(1)} collective-permute-done((bf16[256,512]{1,0:T(8,128)(2,1)S(1)}, bf16[256,512]{1,0:T(8,128)(2,1)S(1)}, u32[]{:S(2)}, u32[]{:S(2)}) %collective-permute-start.36) | collective-permute-done | bytes 262176 | tf_op jit(solution)/shard_map/ppermute | solution.py:686
  354.7 1.8 collective-permute-start.37
  357.7 1.8 collective-permute-start.29
  361.2 2.5 collective-permute-done.33
  369.5 3.4 collective-permute-done.44
  375.6 3.3 collective-permute-done.45
  (234 shorter events, 63.7 us)
Async XLA Ops:
  7.2 358.3 %reduce-scatter.6.cloned.1.call-start = ((), (), s32[]{:S(2)}) async-start(), calls=%async_computation.4 | async-start | bytes 2621440 | tf_op jit(solution)/shard_map/reduce_scatter | solution.py:689
  7.2 26.7 %collective-permute-start.1 = (bf16[256,1024]{1,0:T(8,128)(2,1)}, bf16[256,1024]{1,0:T(8,128)(2,1)S(1)}, u32[]{:S(2)}, u32[]{:S(2)}) collective-permute-start(bf16[256,1024]{1,0:T(8,128)(2,1)} %refs_4_.3), channel_id=1, source_target_pairs={{0,1},{1,0},{2,3},{3,2},{4,5},{5,4},{6,7},{7,6},{8,9},{9,8},{10,11... | collective-permute-start | bytes 1572872 | tf_op jit(solution)/shard_map/ppermute | solution.py:754
  7.7 25.6 %collective-permute-start = (s32[256]{0:T(256)}, s32[256]{0:T(256)S(1)}, u32[]{:S(2)}, u32[]{:S(2)}) collective-permute-start(s32[256]{0:T(256)} %param.43), channel_id=1, source_target_pairs={{0,1},{1,0},{2,3},{3,2},{4,5},{5,4},{6,7},{7,6},{8,9},{9,8},{10,11... | collective-permute-start | bytes 3080 | tf_op jit(solution)/shard_map/ppermute | solution.py:754
  89.7 31.5 %collective-permute-start.2 = (bf16[512,4096]{1,0:T(8,128)(2,1)}, bf16[512,4096]{1,0:T(8,128)(2,1)}, u32[]{:S(2)}, u32[]{:S(2)}) collective-permute-start(bf16[512,4096]{1,0:T(8,128)(2,1)} %get-tuple-element.110.refs_0_), channel_id=1, source_target_pairs={{0,1},{1,0},{2,3},{3,2},{4,5},{5,4},{6,7},{7,6},{8,9},{9,8},{10,11... | collective-permute-start | bytes 12582920 | tf_op jit(solution)/shard_map/ppermute | solution.py:754
  112.7 25.2 %collective-permute-start.5 = (bf16[512,2048]{1,0:T(8,128)(2,1)}, bf16[512,2048]{1,0:T(8,128)(2,1)S(1)}, u32[]{:S(2)}, u32[]{:S(2)}) collective-permute-start(bf16[512,2048]{1,0:T(8,128)(2,1)} %get-tuple-element.117), channel_id=1, source_target_pairs={{0,1},{1,0},{2,3},{3,2},{4,5},{5,4},{6,7},{7,6},{8,9},{9,8},{10,11... | collective-permute-start | bytes 6291464 | tf_op jit(solution)/shard_map/ppermute | solution.py:754
  113.0 23.5 %collective-permute-start.4 = (bf16[512,1024]{1,0:T(8,128)(2,1)}, bf16[512,1024]{1,0:T(8,128)(2,1)}, u32[]{:S(2)}, u32[]{:S(2)}) collective-permute-start(bf16[512,1024]{1,0:T(8,128)(2,1)} %get-tuple-element.115.low.refs_0_), channel_id=1, source_target_pairs={{0,1},{1,0},{2,3},{3,2},{4,5},{5,4},{6,7},{7,6},{8,9},{9,8},{10,11... | collective-permute-start | bytes 3145736 | tf_op jit(solution)/shard_map/ppermute | solution.py:754
  113.6 36.0 %collective-permute-start.6 = (bf16[512,1024]{1,0:T(8,128)(2,1)S(1)}, bf16[512,1024]{1,0:T(8,128)(2,1)}, u32[]{:S(2)}, u32[]{:S(2)}) collective-permute-start(bf16[512,1024]{1,0:T(8,128)(2,1)S(1)} %copy-done.33), channel_id=1, source_target_pairs={{0,1},{1,0},{2,3},{3,2},{4,5},{5,4},{6,7},{7,6},{8,9},{9,8},{10,11... | collective-permute-start | bytes 3145736 | tf_op jit(solution)/shard_map/ppermute | solution.py:754
  121.1 28.6 %collective-permute-start.7 = (bf16[512,512]{1,0:T(8,128)(2,1)}, bf16[512,512]{1,0:T(8,128)(2,1)}, u32[]{:S(2)}, u32[]{:S(2)}) collective-permute-start(bf16[512,512]{1,0:T(8,128)(2,1)} %get-tuple-element.122), channel_id=1, source_target_pairs={{0,1},{1,0},{2,3},{3,2},{4,5},{5,4},{6,7},{7,6},{8,9},{9,8},{10,11... | collective-permute-start | bytes 1572872 | tf_op jit(solution)/shard_map/ppermute | solution.py:754
  133.5 76.3 %collective-permute-start.8 = (bf16[2048,256]{1,0:T(8,128)(2,1)}, bf16[2048,256]{1,0:T(8,128)(2,1)}, u32[]{:S(2)}, u32[]{:S(2)}) collective-permute-start(bf16[2048,256]{1,0:T(8,128)(2,1)} %get-tuple-element.113), channel_id=1, source_target_pairs={{0,2},{2,0},{4,6},{6,4},{8,10},{10,8},{12,14},{14,12},{16,18},{18,... | collective-permute-start | bytes 3145736 | tf_op jit(solution)/shard_map/ppermute | solution.py:686
  136.4 73.5 %collective-permute-start.9 = (bf16[2048,256]{1,0:T(8,128)(2,1)}, bf16[2048,256]{1,0:T(8,128)(2,1)}, u32[]{:S(2)}, u32[]{:S(2)}) collective-permute-start(bf16[2048,256]{1,0:T(8,128)(2,1)} %get-tuple-element.114), channel_id=1, source_target_pairs={{0,4},{2,6},{4,0},{6,2},{8,12},{10,14},{12,8},{14,10},{16,20},{18,... | collective-permute-start | bytes 3145736 | tf_op jit(solution)/shard_map/ppermute | solution.py:686
  149.1 58.1 %collective-permute-start.10 = (bf16[512,1024]{1,0:T(8,128)(2,1)}, bf16[512,1024]{1,0:T(8,128)(2,1)S(1)}, u32[]{:S(2)}, u32[]{:S(2)}) collective-permute-start(bf16[512,1024]{1,0:T(8,128)(2,1)} %get-tuple-element.119), channel_id=1, source_target_pairs={{0,2},{2,0},{4,6},{6,4},{8,10},{10,8},{12,14},{14,12},{16,18},{18,... | collective-permute-start | bytes 3145736 | tf_op jit(solution)/shard_map/ppermute | solution.py:686
  190.6 189.2 %reduce-scatter.8.cloned.1.call-start = ((), (), s32[]{:S(2)}) async-start(), calls=%async_computation.5 | async-start | bytes 1966080 | tf_op jit(solution)/shard_map/reduce_scatter | solution.py:689
  209.8 23.8 %collective-permute-start.14 = (bf16[512,512]{1,0:T(8,128)(2,1)}, bf16[512,512]{1,0:T(8,128)(2,1)S(1)}, u32[]{:S(2)}, u32[]{:S(2)}) collective-permute-start(bf16[512,512]{1,0:T(8,128)(2,1)} %get-tuple-element.123), channel_id=1, source_target_pairs={{0,4},{2,6},{4,0},{6,2},{8,12},{10,14},{12,8},{14,10},{16,20},{18,... | collective-permute-start | bytes 1572872 | tf_op jit(solution)/shard_map/ppermute | solution.py:686
  209.9 16.9 %collective-permute-start.18 = (bf16[512,512]{1,0:T(8,128)(2,1)}, bf16[512,512]{1,0:T(8,128)(2,1)}, u32[]{:S(2)}, u32[]{:S(2)}) collective-permute-start(bf16[512,512]{1,0:T(8,128)(2,1)} %get-tuple-element.147), channel_id=1, source_target_pairs={{0,1},{1,0},{2,3},{3,2},{4,5},{5,4},{6,7},{7,6},{8,9},{9,8},{10,11... | collective-permute-start | bytes 1572872 | tf_op jit(solution)/shard_map/ppermute | solution.py:754
  212.7 23.3 %collective-permute-start.13 = (bf16[256,1024]{1,0:T(8,128)(2,1)S(1)}, bf16[256,1024]{1,0:T(8,128)(2,1)S(1)}, u32[]{:S(2)}, u32[]{:S(2)}) collective-permute-start(bf16[256,1024]{1,0:T(8,128)(2,1)S(1)} %add_convert_fusion.7), channel_id=1, source_target_pairs={{0,4},{2,6},{4,0},{6,2},{8,12},{10,14},{12,8},{14,10},{16,20},{18,... | collective-permute-start | bytes 1572872 | tf_op jit(solution)/shard_map/ppermute | solution.py:686
  214.6 21.6 %collective-permute-start.12 = (bf16[1024,256]{1,0:T(8,128)(2,1)S(1)}, bf16[1024,256]{1,0:T(8,128)(2,1)S(1)}, u32[]{:S(2)}, u32[]{:S(2)}) collective-permute-start(bf16[1024,256]{1,0:T(8,128)(2,1)S(1)} %add_convert_fusion.8), channel_id=1, source_target_pairs={{0,2},{2,0},{4,6},{6,4},{8,10},{10,8},{12,14},{14,12},{16,18},{18,... | collective-permute-start | bytes 1572872 | tf_op jit(solution)/shard_map/ppermute | solution.py:686
  216.0 31.2 %collective-permute-start.11 = (bf16[1024,256]{1,0:T(8,128)(2,1)S(1)}, bf16[1024,256]{1,0:T(8,128)(2,1)S(1)}, u32[]{:S(2)}, u32[]{:S(2)}) collective-permute-start(bf16[1024,256]{1,0:T(8,128)(2,1)S(1)} %add_convert_fusion.9), channel_id=1, source_target_pairs={{0,4},{2,6},{4,0},{6,2},{8,12},{10,14},{12,8},{14,10},{16,20},{18,... | collective-permute-start | bytes 1572872 | tf_op jit(solution)/shard_map/ppermute | solution.py:686
  226.8 77.8 %collective-permute-start.25 = (bf16[512,1024]{1,0:T(8,128)(2,1)}, bf16[512,1024]{1,0:T(8,128)(2,1)}, u32[]{:S(2)}, u32[]{:S(2)}) collective-permute-start(bf16[512,1024]{1,0:T(8,128)(2,1)} %refs_0_), channel_id=1, source_target_pairs={{0,1},{1,0},{2,3},{3,2},{4,5},{5,4},{6,7},{7,6},{8,9},{9,8},{10,11... | collective-permute-start | bytes 3145736 | tf_op jit(solution)/shard_map/ppermute | solution.py:754
  233.7 46.1 %collective-permute-start.21 = (bf16[512,768]{1,0:T(8,128)(2,1)}, bf16[512,768]{1,0:T(8,128)(2,1)}, u32[]{:S(2)}, u32[]{:S(2)}) collective-permute-start(bf16[512,768]{1,0:T(8,128)(2,1)} %get-tuple-element.143), channel_id=1, source_target_pairs={{0,2},{2,0},{4,6},{6,4},{8,10},{10,8},{12,14},{14,12},{16,18},{18,... | collective-permute-start | bytes 2359304 | tf_op jit(solution)/shard_map/ppermute | solution.py:686
  236.0 43.7 %collective-permute-start.22 = (bf16[512,768]{1,0:T(8,128)(2,1)}, bf16[512,768]{1,0:T(8,128)(2,1)}, u32[]{:S(2)}, u32[]{:S(2)}) collective-permute-start(bf16[512,768]{1,0:T(8,128)(2,1)} %get-tuple-element.144), channel_id=1, source_target_pairs={{0,4},{2,6},{4,0},{6,2},{8,12},{10,14},{12,8},{14,10},{16,20},{18,... | collective-permute-start | bytes 2359304 | tf_op jit(solution)/shard_map/ppermute | solution.py:686
  236.1 43.6 %collective-permute-start.23 = (bf16[512,640]{1,0:T(8,128)(2,1)}, bf16[512,640]{1,0:T(8,128)(2,1)}, u32[]{:S(2)}, u32[]{:S(2)}) collective-permute-start(bf16[512,640]{1,0:T(8,128)(2,1)} %pad_maximum_fusion.2), channel_id=1, source_target_pairs={{0,8},{2,10},{4,12},{6,14},{8,0},{10,2},{12,4},{14,6},{16,24},{18,... | collective-permute-start | bytes 1966088 | tf_op jit(solution)/shard_map/ppermute | solution.py:686
  250.6 29.1 %collective-permute-start.24 = (bf16[256,512]{1,0:T(8,128)(2,1)S(1)}, bf16[256,512]{1,0:T(8,128)(2,1)S(1)}, u32[]{:S(2)}, u32[]{:S(2)}) collective-permute-start(bf16[256,512]{1,0:T(8,128)(2,1)S(1)} %add_convert_fusion.26), channel_id=1, source_target_pairs={{0,2},{2,0},{4,6},{6,4},{8,10},{10,8},{12,14},{14,12},{16,18},{18,... | collective-permute-start | bytes 786440 | tf_op jit(solution)/shard_map/ppermute | solution.py:686
  252.2 131.2 %reduce-scatter.4.cloned.1.call-start = ((), (), s32[]{:S(2)}) async-start(), calls=%async_computation.3 | async-start | bytes 1310720 | tf_op jit(solution)/shard_map/reduce_scatter | solution.py:689
  279.7 25.0 %collective-permute-start.26 = (bf16[3,512,512]{2,1,0:T(8,128)(2,1)}, bf16[3,512,512]{2,1,0:T(8,128)(2,1)}, u32[]{:S(2)}, u32[]{:S(2)}) collective-permute-start(bf16[3,512,512]{2,1,0:T(8,128)(2,1)} %get-tuple-element.173), channel_id=1, source_target_pairs={{0,1},{1,0},{2,3},{3,2},{4,5},{5,4},{6,7},{7,6},{8,9},{9,8},{10,11... | collective-permute-start | bytes 4718600 | tf_op jit(solution)/shard_map/ppermute | solution.py:754
  281.0 22.4 %collective-permute-start.43 = (bf16[256,768]{1,0:T(8,128)(2,1)S(1)}, bf16[256,768]{1,0:T(8,128)(2,1)S(1)}, u32[]{:S(2)}, u32[]{:S(2)}) collective-permute-start(bf16[256,768]{1,0:T(8,128)(2,1)S(1)} %add_convert_fusion.14), channel_id=1, source_target_pairs={{0,2},{2,0},{4,6},{6,4},{8,10},{10,8},{12,14},{14,12},{16,18},{18,... | collective-permute-start | bytes 1179656 | tf_op jit(solution)/shard_map/ppermute | solution.py:686
  283.4 17.8 %collective-permute-start.39 = (bf16[256,640]{1,0:T(8,128)(2,1)S(1)}, bf16[256,640]{1,0:T(8,128)(2,1)S(1)}, u32[]{:S(2)}, u32[]{:S(2)}) collective-permute-start(bf16[256,640]{1,0:T(8,128)(2,1)S(1)} %get-tuple-element.185), channel_id=1, source_target_pairs={{0,16},{2,18},{4,20},{6,22},{8,24},{10,26},{12,28},{14,30},{16,0},... | collective-permute-start | bytes 983048 | tf_op jit(solution)/shard_map/ppermute | solution.py:686
  313.2 15.6 %collective-permute-start.35 = (bf16[512,512]{1,0:T(8,128)(2,1)}, bf16[512,512]{1,0:T(8,128)(2,1)S(1)}, u32[]{:S(2)}, u32[]{:S(2)}) collective-permute-start(bf16[512,512]{1,0:T(8,128)(2,1)} %get-tuple-element.179), channel_id=1, source_target_pairs={{0,8},{2,10},{4,12},{6,14},{8,0},{10,2},{12,4},{14,6},{16,24},{18,... | collective-permute-start | bytes 1572872 | tf_op jit(solution)/shard_map/ppermute | solution.py:686
  315.3 21.5 %collective-permute-start.31 = (bf16[512,512]{1,0:T(8,128)(2,1)}, bf16[512,512]{1,0:T(8,128)(2,1)S(1)}, u32[]{:S(2)}, u32[]{:S(2)}) collective-permute-start(bf16[512,512]{1,0:T(8,128)(2,1)} %get-tuple-element.177), channel_id=1, source_target_pairs={{0,4},{2,6},{4,0},{6,2},{8,12},{10,14},{12,8},{14,10},{16,20},{18,... | collective-permute-start | bytes 1572872 | tf_op jit(solution)/shard_map/ppermute | solution.py:686
  317.7 22.7 %collective-permute-start.27 = (bf16[512,512]{1,0:T(8,128)(2,1)}, bf16[512,512]{1,0:T(8,128)(2,1)S(1)}, u32[]{:S(2)}, u32[]{:S(2)}) collective-permute-start(bf16[512,512]{1,0:T(8,128)(2,1)} %get-tuple-element.175), channel_id=1, source_target_pairs={{0,2},{2,0},{4,6},{6,4},{8,10},{10,8},{12,14},{14,12},{16,18},{18,... | collective-permute-start | bytes 1572872 | tf_op jit(solution)/shard_map/ppermute | solution.py:686
  329.0 25.7 %collective-permute-start.36 = (bf16[256,512]{1,0:T(8,128)(2,1)S(1)}, bf16[256,512]{1,0:T(8,128)(2,1)S(1)}, u32[]{:S(2)}, u32[]{:S(2)}) collective-permute-start(bf16[256,512]{1,0:T(8,128)(2,1)S(1)} %get-tuple-element.187), channel_id=1, source_target_pairs={{0,16},{2,18},{4,20},{6,22},{8,24},{10,26},{12,28},{14,30},{16,0},... | collective-permute-start | bytes 786440 | tf_op jit(solution)/shard_map/ppermute | solution.py:686
  336.9 19.7 %collective-permute-start.32 = (bf16[256,512]{1,0:T(8,128)(2,1)S(1)}, bf16[256,512]{1,0:T(8,128)(2,1)S(1)}, u32[]{:S(2)}, u32[]{:S(2)}) collective-permute-start(bf16[256,512]{1,0:T(8,128)(2,1)S(1)} %get-tuple-element.189), channel_id=1, source_target_pairs={{0,8},{2,10},{4,12},{6,14},{8,0},{10,2},{12,4},{14,6},{16,24},{18,... | collective-permute-start | bytes 786440 | tf_op jit(solution)/shard_map/ppermute | solution.py:686
  340.5 17.2 %collective-permute-start.28 = (bf16[256,512]{1,0:T(8,128)(2,1)S(1)}, bf16[256,512]{1,0:T(8,128)(2,1)S(1)}, u32[]{:S(2)}, u32[]{:S(2)}) collective-permute-start(bf16[256,512]{1,0:T(8,128)(2,1)S(1)} %get-tuple-element.191), channel_id=1, source_target_pairs={{0,4},{2,6},{4,0},{6,2},{8,12},{10,14},{12,8},{14,10},{16,20},{18,... | collective-permute-start | bytes 786440 | tf_op jit(solution)/shard_map/ppermute | solution.py:686
  (53 other events, 757.0 us)
Sparse Core Ops, SparseCore 0:
  190.7 44.2 reduce-scatter.5
  252.3 35.1 reduce-scatter.7
  317.8 36.9 reduce-scatter.3

commit v3 on v2

--- a/solution.py
+++ b/solution.py
@@ -19,19 +19,6 @@
 NEG = -1e30
 EPS = 1e-05
 
-ERFC_SLOPE = 0.3
-ERFC_TERMS = (
-    0.16918800133874554,
-    0.17071528857689505,
-    0.14833875833407398,
-    0.2149275739002705,
-    -0.09465408961006916,
-    0.5477246520897923,
-    -0.5122819409407986,
-    0.4855649934109654,
-    -0.12952325668594952,
-)
-
 BF = jnp.bfloat16
 F32 = jnp.float32
 VMEM_LIMIT = 56 * 2**20
@@ -55,7 +42,7 @@
     return mul(left, right, 0, 0)
 
 
-def kernel_call(body, grid, in_specs, out_specs, out_shape, scratch, flops, moved, scalars=0):
+def kernel_call(body, grid, in_specs, out_specs, out_shape, scratch, moved, scalars=0):
     return pl.pallas_call(
         body,
         grid_spec=pltpu.PrefetchScalarGridSpec(
@@ -68,7 +55,7 @@
         out_shape=out_shape,
         compiler_params=pltpu.CompilerParams(vmem_limit_bytes=VMEM_LIMIT),
         cost_estimate=pl.CostEstimate(
-            flops=int(flops), bytes_accessed=int(moved), transcendentals=0
+            flops=1, bytes_accessed=int(moved * 2**20), transcendentals=0
         ),
     )
 
@@ -172,17 +159,22 @@
     lane = lax.broadcasted_iota(jnp.int32, (1, PAIR), 1)
     for begin, size, seen in row_parts(rows, keys, causal):
         rows_at = slice(begin, begin + size)
-        lse_block = jnp.zeros((size, PAIR), F32)
+        scores = []
         for pair in range(GROUP // PAIR):
             lanes = slice(pair * PAIR, (pair + 1) * PAIR)
             query = q_out[rows_at, lanes]
             key = k_out[:seen, lanes]
+            for head in range(2):
+                scores.append(mul_nt(query * scaled[head], key) + bias[rows_at, :seen])
+        lse_block = jnp.zeros((size, PAIR), F32)
+        for pair in range(GROUP // PAIR):
+            lanes = slice(pair * PAIR, (pair + 1) * PAIR)
             value = v_out[:seen, lanes]
             outs = []
             for head in range(2):
-                scores = mul_nt(query * scaled[head], key) + bias[rows_at, :seen]
-                top = jnp.max(scores, -1, keepdims=True)
-                weights = jnp.exp(scores - top)
+                score = scores[pair * 2 + head]
+                top = jnp.max(score, -1, keepdims=True)
+                weights = jnp.exp(score - top)
                 weight_sum = jnp.sum(weights, -1, keepdims=True)
                 outs.append(mul_nn(weights.astype(BF), value) * (1.0 / weight_sum))
                 lse_block = jnp.where(
@@ -206,7 +198,7 @@
             inverse_out[at, :] = inverse
             low_out[at, :] = (normal * gain + shift).astype(BF)
 
-        by_rows(rows, 32, block)
+        by_rows(rows, 128, block)
 
 
 def attention_forward(causal, row_seg, key_seg, source, extra, weights, norms):
@@ -244,22 +236,16 @@
         shape_of((rows, width), BF),
     ]
     scratch = [pltpu.VMEM((rows, keys), F32), pltpu.VMEM((rows, width), F32)]
-    flops = 2 * rows * width * width * 4 + 4 * rows * keys * width
     call = kernel_call(
-        partial(forward_body, causal), (steps,), in_specs, out_specs, out_shape, scratch, flops, 20e6
+        partial(forward_body, causal), (steps,), in_specs, out_specs, out_shape, scratch, 30
     )
     return call(*operands, *weights, norms)
 
 
 def gelu_parts(value):
-    bell = jnp.exp(value * value * -0.5)
-    short = 1.0 / (1.0 + (ERFC_SLOPE * 0.5**0.5) * jnp.abs(value))
-    series = jnp.full_like(value, 0.5 * ERFC_TERMS[-1])
-    for term in ERFC_TERMS[-2::-1]:
-        series = series * short + 0.5 * term
-    tail = bell * short * series
-    share = jnp.where(value < 0, tail, 1.0 - tail)
-    return value * share, share + value * (bell * (0.5 / np.pi) ** 0.5)
+    share = 0.5 + 0.5 * lax.erf(value * 0.5**0.5)
+    bell = jnp.exp(value * value * -0.5) * (0.5 / np.pi) ** 0.5
+    return value * share, share + value * bell
 
 
 def expand_body(
@@ -275,12 +261,14 @@
         total[...] = jnp.zeros_like(total)
 
     size = rows // 2
-    for part in range(2):
-        at = slice(part * size, (part + 1) * size)
-        active, slope = gelu_parts(mul_nn(low[at, :], w_expand[...]))
-        active_out[at, :] = active.astype(BF)
+    spans = [slice(part * size, (part + 1) * size) for part in range(2)]
+    values = [mul_nn(low[at, :], w_expand[...]) for at in spans]
+    for at, value in zip(spans, values):
+        active, slope = gelu_parts(value)
+        active = active.astype(BF)
+        active_out[at, :] = active
         slope_out[at, :] = slope.astype(BF)
-    total[...] += mul_nn(active_out[...], w_contract[...])
+        total[at, :] += mul_nn(active, w_contract[...])
 
     @pl.when(step == pl.num_programs(0) - 1)
     def _():
@@ -303,7 +291,7 @@
             keep_grad[at, :] = jnp.where(is_low, left, right).astype(BF)
             send_grad[at, :] = jnp.where(is_low, right, left).astype(BF)
 
-        by_rows(rows, 32, block)
+        by_rows(rows, 128, block)
 
 
 def feed_forward(core, low, normal, w_expand, w_contract, norms, out_grad):
@@ -339,8 +327,7 @@
         out_specs,
         out_shape,
         [pltpu.VMEM((rows, width), F32)],
-        4 * rows * width * wide,
-        36e6,
+        34,
         scalars=1,
     )
     return call(core, low, normal, w_expand, w_contract, norms, out_grad)
@@ -352,32 +339,32 @@
     return jnp.where(later == 0, 1 - core[0], core[0]) * half + step % half
 
 
-def contract_back_body(
-    core, low_grad, w_contract, slope, w_expand, grad_in, normal_in, inverse_in, norms,
-    send_wide, keep_wide, grad_out, low_out, send_low, keep_low, norm_out,
-    total,
-):
+def contract_back_body(last, core, *refs):
+    low_grad, w_contract, slope, w_expand = refs[:4]
+    if last:
+        (total_in, grad_in, normal_in, inverse_in, norms) = refs[4:9]
+        (wide_out, grad_out, low_out, send_low, keep_low, norm_out, total) = refs[9:]
+    else:
+        wide_out, total = refs[4:]
     step = pl.program_id(0)
-    steps = pl.num_programs(0)
     rows, width = low_grad.shape
 
     @pl.when(step == 0)
     def _():
-        total[...] = jnp.zeros_like(total)
-
-    wide_grad = (mul_nt(low_grad[...], w_contract[...]) * slope[...].astype(F32)).astype(BF)
-
-    @pl.when(step < steps // 2)
-    def _():
-        send_wide[...] = wide_grad
-
-    @pl.when(step >= steps // 2)
-    def _():
-        keep_wide[...] = wide_grad
-
-    total[...] += mul_nt(wide_grad, w_expand[...])
-
-    @pl.when(step == steps - 1)
+        total[...] = total_in[...] if last else jnp.zeros_like(total)
+
+    size = rows // 2
+    spans = [slice(part * size, (part + 1) * size) for part in range(2)]
+    values = [mul_nt(low_grad[at, :], w_contract[...]) for at in spans]
+    for at, value in zip(spans, values):
+        wide_grad = (value * slope[at, :].astype(F32)).astype(BF)
+        wide_out[at, :] = wide_grad
+        total[at, :] += mul_nt(wide_grad, w_expand[...])
+
+    if not last:
+        return
+
+    @pl.when(step == pl.num_programs(0) - 1)
     def _():
         norm_out[...] = jnp.zeros_like(norm_out)
         half = width // 2
@@ -398,55 +385,55 @@
             keep_low[at, :] = jnp.where(is_low, left, right).astype(BF)
             send_low[at, :] = jnp.where(is_low, right, left).astype(BF)
 
-        by_rows(rows, 32, block)
-
-
-def feed_backward(core, low_grad, w_contract, slope, w_expand, grad, normal, inverse, norms):
+        by_rows(rows, 128, block)
+
+
+def feed_backward(last, core, low_grad, w_contract, slope, w_expand, *rest):
     rows, width = low_grad.shape
     wide = w_expand.shape[1]
     chunk = 512
-    steps = wide // chunk
-    half = steps // 2
+    steps = wide // chunk // 2
+
+    def at(s, core):
+        return (core[0] if last else 1 - core[0]) * steps + s
+
     in_specs = [
         whole((rows, width)),
-        pl.BlockSpec((chunk, width), lambda s, core: (send_first(s, steps, core), 0)),
-        pl.BlockSpec((rows, chunk), lambda s, core: (0, send_first(s, steps, core))),
-        pl.BlockSpec((width, chunk), lambda s, core: (0, send_first(s, steps, core))),
-        whole((rows, width)),
-        whole((rows, width)),
-        whole((rows, 1)),
-        whole(norms.shape),
-    ]
-    out_specs = [
-        pl.BlockSpec((rows, chunk), lambda s, _: (0, jnp.minimum(s, half - 1))),
-        pl.BlockSpec((rows, chunk), lambda s, _: (0, jnp.maximum(s - half, 0))),
-        whole((rows, width)),
-        whole((rows, width)),
-        whole((rows, width // 2)),
-        whole((rows, width // 2)),
-        whole((2, width)),
-    ]
-    out_shape = [
-        shape_of((rows, wide // 2), BF),
-        shape_of((rows, wide // 2), BF),
-        shape_of((rows, width), F32),
-        shape_of((rows, width), BF),
-        shape_of((rows, width // 2), BF),
-        shape_of((rows, width // 2), BF),
-        shape_of((2, width), F32),
-    ]
+        pl.BlockSpec((chunk, width), lambda s, core: (at(s, core), 0)),
+        pl.BlockSpec((rows, chunk), lambda s, core: (0, at(s, core))),
+        pl.BlockSpec((width, chunk), lambda s, core: (0, at(s, core))),
+    ] + [whole(item.shape) for item in rest]
+    out_specs = [pl.BlockSpec((rows, chunk), lambda s, _: (0, s)), whole((rows, width))]
+    out_shape = [shape_of((rows, wide // 2), BF), shape_of((rows, width), F32)]
+    scratch = []
+    if last:
+        out_specs += [whole((rows, width))] + [whole((rows, width // 2))] * 2 + [whole((2, width))]
+        out_shape += [
+            shape_of((rows, width), BF),
+            shape_of((rows, width // 2), BF),
+            shape_of((rows, width // 2), BF),
+            shape_of((2, width), F32),
+        ]
+        scratch = [pltpu.VMEM((rows, width), F32)]
     call = kernel_call(
-        contract_back_body,
+        partial(contract_back_body, last),
         (steps,),
         in_specs,
         out_specs,
         out_shape,
-        [pltpu.VMEM((rows, width), F32)],
-        4 * rows * width * wide,
-        32e6,
+        scratch,
+        18,
         scalars=1,
     )
-    return call(core, low_grad, w_contract, slope, w_expand, grad, normal, inverse, norms)
+    return call(core, low_grad, w_contract, slope, w_expand, *rest)
+
+
+def add_rows(parts):
+    first, last = parts
+    rows = first.shape[0]
+    if rows == last.shape[0]:
+        return first + last
+    return jnp.concatenate([first + last[:rows], last[rows:]])
 
 
 def backward_body(causal, core, *refs):
@@ -478,40 +465,40 @@
     query_grads, key_grads, value_grads = [], [], []
     for pair in range(GROUP // PAIR):
         lanes = slice(pair * PAIR, (pair + 1) * PAIR)
-        key_all = key_in[:, lanes]
-        value_all = value_in[:, lanes]
-        key_grad = value_grad = None
-        query_parts = []
+        started = []
         for begin, size, seen in row_parts(rows, keys, causal):
             rows_at = slice(begin, begin + size)
             query = query_in[rows_at, lanes]
             grad = o_grad[rows_at, lanes]
+            key = key_in[:seen, lanes]
+            value = value_in[:seen, lanes]
             product = grad.astype(F32) * o_in[rows_at, lanes].astype(F32)
-            key = key_all[:seen]
-            value = value_all[:seen]
-            query_part = None
+            head_queries = [query * scaled[head] for head in range(2)]
+            head_grads = [grad * plain[head] for head in range(2)]
+            scores = [mul_nt(item, key) for item in head_queries]
+            prob_grads = [mul_nt(item, value) for item in head_grads]
+            started.append(
+                (rows_at, seen, key, product, head_queries, head_grads, scores, prob_grads)
+            )
+        query_parts, key_parts, value_parts = [], [], []
+        for rows_at, seen, key, product, head_queries, head_grads, scores, prob_grads in started:
+            probs, score_grads = [], []
             for head in range(2):
                 mine = first_lanes if head == 0 else jnp.logical_not(first_lanes)
                 delta = jnp.sum(jnp.where(mine, product, 0.0), -1, keepdims=True)
-                head_query = query * scaled[head]
-                head_grad = grad * plain[head]
                 lse = lse_in[rows_at, pair * 2 + head : pair * 2 + head + 1]
-                prob = jnp.exp(mul_nt(head_query, key) + bias[rows_at, :seen] - lse)
-                score_grad = (prob * (mul_nt(head_grad, value) - delta)).astype(BF)
-                value_term = mul_tn(prob.astype(BF), head_grad)
-                key_term = mul_tn(score_grad, head_query)
-                query_term = mul_nn(score_grad, key * scaled[head])
-                query_part = query_term if query_part is None else query_part + query_term
-                if seen < keys:
-                    zeros = jnp.zeros((keys - seen, PAIR), F32)
-                    value_term = jnp.concatenate([value_term, zeros])
-                    key_term = jnp.concatenate([key_term, zeros])
-                value_grad = value_term if value_grad is None else value_grad + value_term
-                key_grad = key_term if key_grad is None else key_grad + key_term
-            query_parts.append(query_part)
+                prob = jnp.exp(scores[head] + bias[rows_at, :seen] - lse)
+                score_grads.append((prob * (prob_grads[head] - delta)).astype(BF))
+                probs.append(prob.astype(BF))
+            value_parts.append(mul_tn(jnp.concatenate(probs), jnp.concatenate(head_grads)))
+            stacked = jnp.concatenate(score_grads)
+            key_parts.append(mul_tn(stacked, jnp.concatenate(head_queries)))
+            wide = jnp.concatenate(score_grads, axis=1)
+            head_keys = jnp.concatenate([key * scaled[0], key * scaled[1]])
+            query_parts.append(mul_nn(wide, head_keys))
         query_grads.append(jnp.concatenate(query_parts).astype(BF))
-        key_grads.append(key_grad.astype(BF))
-        value_grads.append(value_grad.astype(BF))
+        key_grads.append(add_rows(key_parts).astype(BF))
+        value_grads.append(add_rows(value_parts).astype(BF))
     query_grad = jnp.concatenate(query_grads, axis=1)
     key_grad = jnp.concatenate(key_grads, axis=1)
     value_grad = jnp.concatenate(value_grads, axis=1)
@@ -565,7 +552,7 @@
                 keep_low[at, :] = jnp.where(is_low, left, right).astype(BF)
                 send_low[at, :] = jnp.where(is_low, right, left).astype(BF)
 
-            by_rows(rows, 32, block)
+            by_rows(rows, 128, block)
 
 
 def attention_backward(causal, core, row_seg, key_seg, low_grad, w_out, saved, weights, grad, extra):
@@ -622,7 +609,6 @@
             shape_of((keys // 2, width), BF),
         ]
         scratch += [pltpu.VMEM((keys, width), F32)]
-    flops = 2 * rows * width * width * 4 + 10 * rows * keys * width
     call = kernel_call(
         partial(backward_body, causal),
         (steps,),
@@ -630,8 +616,7 @@
         out_specs,
         out_shape,
         scratch,
-        flops,
-        24e6,
+        44,
         scalars=1,
     )
     return call(
@@ -655,12 +640,22 @@
     return lax.optimization_barrier((value, after))[0]
 
 
+def beside(outputs, arrays):
+    return lax.optimization_barrier((outputs, arrays))
+
+
+def during(outputs, *chains):
+    outputs, terms = lax.optimization_barrier((outputs, [chain.terms for chain in chains]))
+    for chain, items in zip(chains, terms):
+        chain.terms = items
+    return outputs
+
+
 class Plan:
     def __init__(self, steps, row_count):
         self.steps = steps
         self.row_count = row_count
-        bit_count = row_count.bit_length() - 1
-        sizes = [2 ** (bit_count - 2) if step == "group" else 2 for step in steps]
+        sizes = [self.pieces(step) for step in steps]
         self.relative, self.fixed = [], []
         for k in range(row_count):
             mask = fixed = 0
@@ -670,19 +665,28 @@
                 digit = k // rest % size
                 if step == "group":
                     fixed = digit << 2
+                elif step == "plane":
+                    mask |= digit
                 else:
                     mask |= digit << step
             self.relative.append(mask)
             self.fixed.append(fixed)
-        self.own_bits = sum(1 << step for step in steps if step != "group")
         self.groups = [list(range(low, row_count, 4)) for low in range(4)]
 
+    def pieces(self, step):
+        if step == "group":
+            return self.row_count // 4
+        return 4 if step == "plane" else 2
+
+    def first_pieces(self):
+        return 1 if self.steps[0] == "group" else self.pieces(self.steps[0])
+
     def at_places(self, chip):
-        own = chip & self.own_bits
+        own = (chip & 3) if "group" in self.steps else chip
         return (own ^ jnp.asarray(self.relative, jnp.int32)) | jnp.asarray(self.fixed, jnp.int32)
 
-    def permute(self, tensor, bit):
-        pairs = [(i, i ^ (1 << bit)) for i in range(self.row_count)]
+    def permute(self, tensor, mask):
+        pairs = [(i, i ^ mask) for i in range(self.row_count)]
         return lax.ppermute(tensor, "row", pairs)
 
     def group_sum(self, tensor):
@@ -715,71 +719,76 @@
     def __init__(self, plan, blocks):
         self.plan = plan
         self.left = list(plan.steps)
-        self.got = None
-        self.total = None
-        if self.left[0] == "group":
-            self.sent = blocks[0]
-            self.left.pop(0)
-            self.total = plan.group_sum(self.sent)
-        else:
-            self.keep, self.sent = blocks
-            self.got = plan.permute(self.sent, self.left.pop(0))
+        self.launch(list(blocks))
+
+    def launch(self, pieces):
+        step = self.left.pop(0)
+        if step == "group":
+            self.sent = pieces
+            self.terms = [self.plan.group_sum(pieces[0])]
+            return
+        self.sent = pieces[1:]
+        masks = [1, 2, 3] if step == "plane" else [1 << step]
+        got = [self.plan.permute(piece, mask) for piece, mask in zip(self.sent, masks)]
+        self.terms = [pieces[0]] + got
+
+    def hold(self, *after):
+        got = self.terms[1:] if len(self.terms) > 1 else self.terms
+        self.terms[-len(got) :] = tie(got, *after)
 
     def sum_rows(self, rows):
-        if self.got is None:
-            return self.total[rows]
-        return self.keep[rows].astype(F32) + self.got[rows].astype(F32)
+        total = self.terms[0][rows].astype(F32)
+        for term in self.terms[1:]:
+            total = total + term[rows].astype(F32)
+        return total
 
     def merged(self):
         assert self.left.pop(0) == "group"
         return self.sum_rows(slice(None)).astype(BF)
 
     def advance(self):
-        if self.left[0] == "group":
-            self.sent = self.merged()
-            self.total, self.got = self.plan.group_sum(self.sent), None
-            return
-        rows = (self.keep if self.got is not None else self.total).shape[0]
-        sent = self.sum_rows(slice(rows // 2, None)).astype(BF)
-        self.keep = self.sum_rows(slice(None, rows // 2)).astype(BF)
-        self.sent = sent
-        self.got = self.plan.permute(sent, self.left.pop(0))
+        step = self.left[0]
+        count = 1 if step == "group" else self.plan.pieces(step)
+        rows = self.terms[0].shape[0] // count
+        self.launch(
+            [self.sum_rows(slice(k * rows, (k + 1) * rows)).astype(BF) for k in range(count)]
+        )
 
     def result(self):
         assert not self.left
-        return self.sum_rows(slice(None)).astype(F32)
+        return self.sum_rows(slice(None))
 
 
 def swap_mem(tensor):
     return lax.ppermute(tensor, "mem", [(0, 1), (1, 0)])
 
 
-def weight_grads_body(spans, item_of_step, count, at_place, *refs):
-    items = len(set(item_of_step))
-    sources = refs[: 2 * items]
-    own_grad, other_grad = refs[2 * items : 2 * items + 2]
-    outs = refs[2 * items + 2 : -1]
+def weight_grads_body(spans, sources_count, grads_count, step_table, count, at_place, *refs):
+    sources = refs[: 2 * sources_count]
+    grads = refs[2 * sources_count : 2 * (sources_count + grads_count)]
+    outs = refs[2 * (sources_count + grads_count) : -1]
     whole_grad = refs[-1]
     step = pl.program_id(0)
     _, block_rows, lanes = whole_grad.shape
     joined = max(16 // block_rows, 1)
-    for item in range(items):
-        steps = [at for at, which in enumerate(item_of_step) if which == item]
+    for entry in sorted(set(step_table)):
+        steps = [at for at, which in enumerate(step_table) if which == entry]
 
         @pl.when((step >= steps[0]) & (step <= steps[-1]))
         def _():
-            own, other = sources[2 * item : 2 * item + 2]
+            own, other = sources[2 * entry[0] : 2 * entry[0] + 2]
+            own_grad, other_grad = grads[2 * entry[1] : 2 * entry[1] + 2]
             grad = mul_tn(own[...], own_grad[0]) + mul_tn(other[...], other_grad[0])
             whole_grad[...] = grad.reshape(count, block_rows, lanes)
 
     at_out = 0
-    for number, (begin, chunks, halves) in enumerate(spans):
-        targets = outs[at_out : at_out + (2 if halves else 1)]
-        at_out += len(targets)
+    for number, (begin, chunks, pieces) in enumerate(spans):
+        targets = outs[at_out : at_out + pieces]
+        at_out += pieces
 
         @pl.when((step >= begin) & (step < begin + chunks))
         def _():
-            size = count // len(targets)
+            size = count // pieces
             for part, out in enumerate(targets):
                 for k in range(0, size, joined):
                     base = number * count + part * size + k
@@ -788,20 +797,27 @@
                     out[rows, :] = jnp.concatenate(blocks).astype(BF)
 
 
-def weight_grads(chip, sources, item_of_step, own_grads, other_grads, chunk, outs):
-    if own_grads.ndim == 2:
-        own_grads, other_grads = own_grads[None], other_grads[None]
+def weight_grads(chip, sources, grads, step_table, chunk, outs, travelling=()):
     tokens, width = sources[0][0].shape
-    across = own_grads.shape[2] // chunk
     count = outs[0][1].row_count
-    steps = len(item_of_step)
-    grads_block = pl.BlockSpec((1, tokens, chunk), lambda i, _: (i // across, 0, i % across))
-    in_specs = [whole((tokens, width))] * (2 * len(sources)) + [grads_block] * 2
-    out_specs, out_shape, spans, parts = [], [], [], []
+    steps = len(step_table)
+    in_specs = [whole((tokens, width))] * (2 * len(sources))
+    flat = [item for pair in sources for item in pair]
+    for number, pair in enumerate(grads):
+        pair = [item if item.ndim == 3 else item[None] for item in pair]
+        flat += pair
+        across = pair[0].shape[2] // chunk
+        mine = [at for at, which in enumerate(step_table) if which[1] == number]
+
+        def index(i, _, first=mine[0], last=mine[-1], across=across):
+            at = jnp.clip(i, first, last) - first
+            return (at // across, 0, at % across)
+
+        in_specs += [pl.BlockSpec((1, tokens, chunk), index)] * 2
+    out_specs, out_shape, spans = [], [], []
     begin = 0
     for chunks, plan in outs:
-        halves = plan.steps[0] != "group"
-        pieces = 2 if halves else 1
+        pieces = plan.first_pieces()
 
         def index(i, _, begin=begin, chunks=chunks):
             return (0, jnp.clip(i - begin, 0, chunks - 1))
@@ -809,28 +825,68 @@
         for _ in range(pieces):
             out_specs.append(pl.BlockSpec((width // pieces, chunk), index))
             out_shape.append(shape_of((width // pieces, chunk * chunks), BF))
-        spans.append((begin, chunks, halves))
-        parts.append(pieces)
+        spans.append((begin, chunks, pieces))
         begin += chunks
     call = kernel_call(
-        partial(weight_grads_body, spans, item_of_step, count),
+        partial(weight_grads_body, spans, len(sources), len(grads), step_table, count),
         (steps,),
         in_specs,
         out_specs,
         out_shape,
         [pltpu.VMEM((count, width // count, chunk), F32)],
-        4 * tokens * width * chunk * steps,
-        4 * tokens * (width * len(sources) + chunk * steps) + 2 * width * chunk * steps,
+        16,
         scalars=1,
     )
     at_place = jnp.concatenate([plan.at_places(chip) for _, plan in outs])
-    flat = [item for pair in sources for item in pair]
-    results = call(at_place, *flat, own_grads, other_grads)
-    blocks, at = [], 0
-    for pieces in parts:
-        blocks.append(results[at : at + pieces])
+    results = during(call(at_place, *flat), *travelling)
+    chains, at = [], 0
+    for (_, plan), (_, _, pieces) in zip(outs, spans):
+        chains.append(Chain(plan, results[at : at + pieces]))
         at += pieces
-    return blocks
+    return chains
+
+
+def wide_grads_body(at_chunk, own, other, own_grad, other_grad, *outs):
+    step = pl.program_id(0)
+    chains = len(outs) // 2
+    lanes = outs[0].shape[1]
+    block_rows = outs[0].shape[0] * 2 * chains // at_chunk.shape[0]
+    blocks = own.shape[1] // block_rows
+    size = outs[0].shape[0] // block_rows
+    grad = mul_tn(own[...], own_grad[...]) + mul_tn(other[...], other_grad[...])
+    grad = grad.astype(BF)
+    for block in range(blocks):
+        for chain in range(chains):
+            part = grad[block * block_rows : (block + 1) * block_rows]
+            part = part[:, chain * lanes : (chain + 1) * lanes]
+            place = at_chunk[2 * size * chain + step * blocks + block]
+            for half in range(2):
+
+                @pl.when((place >= half * size) & (place < (half + 1) * size))
+                def _():
+                    row = pl.multiple_of((place - half * size) * block_rows, block_rows)
+                    outs[2 * chain + half][pl.ds(row, block_rows), :] = part
+
+
+def wide_grads(chip, own, other, own_grad, other_grad, plans):
+    tokens, width = own.shape
+    lanes = own_grad.shape[1]
+    chunk = 512
+    source = pl.BlockSpec((tokens, chunk), lambda i, _: (0, i))
+    out = (width // 2, lanes // len(plans))
+    call = kernel_call(
+        wide_grads_body,
+        (width // chunk,),
+        [source] * 2 + [whole((tokens, lanes))] * 2,
+        [whole(out)] * (2 * len(plans)),
+        [shape_of(out, BF)] * (2 * len(plans)),
+        [],
+        20,
+        scalars=1,
+    )
+    place = jnp.concatenate([jnp.argsort(plan.at_places(chip)) for plan in plans])
+    results = call(place.astype(jnp.int32), own, other, own_grad, other_grad)
+    return [Chain(plan, results[2 * at : 2 * at + 2]) for at, plan in enumerate(plans)]
 
 
 def shards(
@@ -857,10 +913,9 @@
     upper = list(range(2, row_count.bit_length() - 1))
     plan_x = Plan([0, 1, "group"], row_count)
     plan_y = Plan([1, 0, "group"], row_count)
-    plan_z = Plan(["group", 0, 1], row_count)
+    group_first = Plan(["group", 0, 1], row_count)
     last_x = Plan([0, 1] + upper, row_count)
-    last_y = Plan([1] + upper + [0], row_count)
-    last_z = Plan(upper + [0, 1], row_count)
+    last_y = Plan([1, 0] + upper, row_count)
 
     other_inputs = swap_mem(inputs)
     other_memory = swap_mem(memory)
@@ -885,60 +940,50 @@
         (cross_query, cross_key, cross_value, cross_out),
         norm_params,
     )
+    cross_saved, (other_inputs, other_self_o, other_one) = beside(
+        cross_saved, (other_inputs, swap_mem(self_o), swap_mem(low_one))
+    )
     cross_o, normal_two, inverse_two, low_two = cross_saved[3], *cross_saved[5:]
-    (active, slope, layer_out, grad_three, low_three, send_three, keep_three, norm_three) = (
-        feed_forward(core, low_two, normal_two, expand_weight, contract_weight, norm_params, out_grad)
-    )
-    other_active = swap_mem(active)
-    got_three = swap_mem(send_three)
-    other_self_o = swap_mem(self_o)
-    other_one = swap_mem(low_one)
-    other_cross_o = swap_mem(cross_o)
-    other_two = swap_mem(low_two)
-    (send_wide, keep_wide, grad_two, low_grad_two, send_two, keep_two, norm_two) = feed_backward(
+    outputs = feed_forward(
+        core, low_two, normal_two, expand_weight, contract_weight, norm_params, out_grad
+    )
+    outputs, (other_cross_o, other_two) = beside(outputs, (swap_mem(cross_o), swap_mem(low_two)))
+    (active, slope, layer_out, grad_three, low_three, send_three, keep_three, norm_three) = outputs
+    outputs = feed_backward(False, core, low_three, contract_weight, slope, expand_weight)
+    (send_wide, part_two), (other_active, got_three) = beside(
+        outputs, (swap_mem(active), swap_mem(send_three))
+    )
+
+    contract_x, contract_y = wide_grads(
+        chip, active, other_active, keep_three, got_three, [plan_x, plan_y]
+    )
+    outputs = feed_backward(
+        True,
         core,
-        low_three,
+        tie(low_three, contract_x.sent, contract_y.sent),
         contract_weight,
         slope,
         expand_weight,
+        part_two,
         grad_three,
         normal_two,
         inverse_two,
         norm_params,
     )
-    got_wide = swap_mem(send_wide)
+    outputs, got_wide = beside(outputs, swap_mem(send_wide))
+    (keep_wide, grad_two, low_grad_two, send_two, keep_two, norm_two) = outputs
+    expand, expand_x = weight_grads(
+        chip,
+        [(low_two, other_two)],
+        [(keep_wide, got_wide)],
+        [(0, 0)] * 4,
+        512,
+        [(2, group_first), (2, plan_x)],
+        (contract_x, contract_y),
+    )
+    contract_x.advance()
+    contract_y.advance()
     got_two = swap_mem(send_two)
-
-    blocks = weight_grads(
-        chip,
-        [(tie(active, low_grad_two), other_active)],
-        [0, 0],
-        keep_three,
-        got_three,
-        256,
-        [(1, plan_x), (1, plan_y)],
-    )
-    contract_x, contract_y = Chain(plan_x, blocks[0]), Chain(plan_y, blocks[1])
-    blocks = weight_grads(
-        chip,
-        [(tie(low_two, contract_x.sent, contract_y.sent), other_two)],
-        [0, 0, 0, 0],
-        keep_wide,
-        got_wide,
-        512,
-        [(2, plan_z), (2, plan_x)],
-    )
-    expand_z, expand_x = Chain(plan_z, blocks[0]), Chain(plan_x, blocks[1])
-    blocks = weight_grads(
-        chip,
-        [(tie(cross_o, expand_z.sent, expand_x.sent), other_cross_o)],
-        [0],
-        keep_two,
-        got_two,
-        512,
-        [(1, plan_y)],
-    )
-    cross_out_y = Chain(plan_y, blocks[0])
 
     (send_c, keep_c, grad_one, low_grad_one, send_one, keep_one, norm_one, mem_own, mem_send) = (
         attention_backward(
@@ -946,7 +991,7 @@
             core,
             target_seg,
             pair_seg,
-            tie(low_grad_two, cross_out_y.sent),
+            tie(low_grad_two, expand.sent, expand_x.sent, contract_x.sent, contract_y.sent),
             cross_out,
             (cross_saved[0], cross_saved[1], cross_saved[2], cross_o, cross_saved[4]),
             (cross_query, cross_key, cross_value),
@@ -954,118 +999,106 @@
             (normal_one, inverse_one, norm_params),
         )
     )
-    memory_grad = (mem_own.astype(F32) + swap_mem(mem_send).astype(F32)).astype(BF)
-    got_c = swap_mem(send_c)
-    got_one = swap_mem(send_one)
-
-    contract_x.got, contract_y.got, expand_x.got = tie(
-        (contract_x.got, contract_y.got, expand_x.got), low_grad_one
-    )
-    for chain in (contract_x, contract_y, expand_x):
-        chain.advance()
+    (send_c, keep_c, grad_one, low_grad_one, send_one, keep_one, norm_one, mem_own, mem_send) = during(
+        (send_c, keep_c, grad_one, low_grad_one, send_one, keep_one, norm_one, mem_own, mem_send),
+        contract_x,
+        contract_y,
+        expand_x,
+    )
     norm_grad = jnp.concatenate([norm_one, norm_two, norm_three])
     norm_grad = norm_grad.reshape(2, 3, norm_grad.shape[1])
     norm_half = norm_grad[core[0]] + swap_mem(norm_grad[1 - core[0]])
+    got_c = swap_mem(send_c)
+    got_one = swap_mem(send_one)
+    merged = [chain.merged() for chain in (contract_x, contract_y)]
+    contract_sums = group_sum_joined(plan_x, merged)
+    expand_x.advance()
+    memory_grad = (mem_own.astype(F32) + swap_mem(mem_send).astype(F32)).astype(BF)
+    block_rows = inputs.shape[1] // row_count
+    norm_blocks = norm_half.reshape(3, row_count, block_rows).transpose(1, 0, 2)
+    norm_blocks = jnp.take(norm_blocks, last_y.at_places(chip), axis=0)
+    norm_chain = Chain(last_y, norm_blocks.reshape((2, -1) + norm_blocks.shape[1:]).astype(BF))
     pair_memory = jnp.concatenate([memory, other_memory])
     turned_memory = jnp.concatenate([other_memory, memory])
-    blocks = weight_grads(
+    cross_x, cross_y = weight_grads(
         chip,
         [
-            (tie(low_one, contract_x.sent, contract_y.sent, expand_x.sent), other_one),
+            (tie(cross_o, merged, expand_x.sent, norm_chain.sent, memory_grad), other_cross_o),
+            (low_one, other_one),
             (pair_memory, turned_memory),
+            (self_o, other_self_o),
         ],
-        [0, 0, 1, 1, 1, 1],
-        keep_c,
-        got_c,
+        [(keep_two, got_two), (keep_c, got_c), (keep_one, got_one)],
+        [(0, 0)] * 2 + [(1, 1)] * 2 + [(2, 1)] * 4 + [(3, 2)] * 2,
         256,
-        [(3, plan_x), (3, plan_y)],
-    )
-    cross_x, cross_y = Chain(plan_x, blocks[0]), Chain(plan_y, blocks[1])
-    blocks = weight_grads(
-        chip,
-        [(tie(self_o, cross_x.sent, cross_y.sent), other_self_o)],
-        [0],
-        keep_one,
-        got_one,
-        512,
-        [(1, last_z)],
-    )
-    block_rows = self_o.shape[1] // row_count
-    norm_blocks = norm_half.reshape(3, row_count, block_rows).transpose(1, 0, 2)
-    norm_blocks = jnp.pad(norm_blocks, ((0, 0), (0, block_rows - 3), (0, PAIR - block_rows)))
-    norm_blocks = jnp.take(norm_blocks, last_z.at_places(chip), axis=0).astype(BF)
-    norm_blocks = norm_blocks.reshape(2, -1, PAIR)
-    self_out_z = Chain(
-        last_z, [jnp.concatenate([blocks[0][i], norm_blocks[i]], axis=1) for i in range(2)]
-    )
-    contract_x.got, contract_y.got, expand_x.got, cross_out_y.got = tie(
-        (contract_x.got, contract_y.got, expand_x.got, cross_out_y.got), self_out_z.sent
-    )
-    cross_out_y.advance()
-    merging = (contract_x, contract_y, expand_x)
-    merged = [chain.merged() for chain in merging]
-    merged_sums = group_sum_joined(plan_x, merged)
+        [(5, plan_x), (5, plan_y)],
+        (expand_x, expand, norm_chain),
+    )
+    expand_x.advance()
+    expand.advance()
+    norm_chain.advance()
 
     send_s, keep_s, input_grad = attention_backward(
         True,
         core,
         target_seg,
         target_seg,
-        tie(low_grad_one, cross_out_y.sent, merged),
+        tie(
+            low_grad_one, cross_x.sent, cross_y.sent, expand.sent, expand_x.sent, norm_chain.sent
+        ),
         self_out,
         (self_saved[0], self_saved[1], self_saved[2], self_o, self_saved[4]),
         (self_query, self_key, self_value),
         grad_one,
         (),
     )
+    send_s, keep_s, input_grad = during(
+        (send_s, keep_s, input_grad), cross_x, cross_y, expand, norm_chain
+    )
     got_s = swap_mem(send_s)
-    cross_x.got, cross_y.got, self_out_z.got, cross_out_y.got = tie(
-        (cross_x.got, cross_y.got, self_out_z.got, cross_out_y.got), input_grad
-    )
-    for chain in (cross_x, cross_y, self_out_z):
-        chain.advance()
-    blocks = weight_grads(
+    cross_x.advance()
+    cross_y.advance()
+    expand.advance()
+    norm_chain.advance()
+    self_chains = weight_grads(
         chip,
-        [(tie(inputs, cross_x.sent, cross_y.sent, self_out_z.sent), other_inputs)],
-        [0, 0, 0],
-        keep_s,
-        got_s,
-        512,
-        [(1, last_x), (1, last_y), (1, last_z)],
-    )
-    self_x, self_y = Chain(last_x, blocks[0]), Chain(last_y, blocks[1])
-    self_z = Chain(last_z, blocks[2])
-    expand_z.total = tie(expand_z.total, self_x.sent, self_y.sent, self_z.sent)
-    expand_z.advance()
-    cross_out_merged = cross_out_y.merged()
-    cross_merged = [cross_x.merged(), cross_y.merged(), cross_out_merged]
-    cross_sums = group_sum_joined(plan_x, cross_merged)
-    self_out_z.advance()
-    self_x.advance(), self_y.advance(), self_z.advance()
-    expand_z.advance()
-    while self_x.left:
-        for chain in (self_x, self_y, self_z, self_out_z):
+        [(tie(inputs, cross_x.sent, cross_y.sent, expand.sent, norm_chain.sent), other_inputs)],
+        [(keep_s, got_s)],
+        [(0, 0)] * 6,
+        256,
+        [(3, last_x), (3, last_y)],
+        (cross_x, cross_y, expand, norm_chain),
+    )
+    started = [chain.sent for chain in self_chains]
+    merged = [chain.merged() for chain in (cross_x, cross_y)]
+    cross_sums = group_sum_joined(plan_x, merged)
+    norm_chain.hold(merged)
+    norm_chain.advance()
+    for chain in self_chains:
+        chain.hold(merged, norm_chain.sent)
+    while self_chains[0].left:
+        for chain in self_chains + [norm_chain]:
             if chain.left:
                 chain.advance()
-    self_out_sum = self_out_z.result()
     own_lanes = self_out.shape[1] // 2
-    cross_first, cross_second = cross_sums[0].astype(F32), cross_sums[1].astype(F32)
-    chunk = 256
+    self_sum = jnp.concatenate([chain.result() for chain in self_chains], axis=1)
+    cross_sum = jnp.concatenate(cross_sums, axis=1).astype(F32)
+    cross_parts = [cross_sum[:, at * own_lanes : (at + 1) * own_lanes] for at in range(5)]
     return (
         layer_out,
         input_grad,
         memory_grad,
-        self_x.result(),
-        self_y.result(),
-        self_z.result(),
-        self_out_sum[:, :own_lanes],
-        cross_first[:, : 2 * chunk],
-        jnp.concatenate([cross_first[:, 2 * chunk :], cross_second[:, :chunk]], axis=1),
-        cross_second[:, chunk:],
-        cross_sums[2].astype(F32),
-        jnp.concatenate([expand_z.result(), merged_sums[2].astype(F32)], axis=1),
-        jnp.concatenate([merged_sums[0], merged_sums[1]], axis=1).astype(F32),
-        self_out_sum[:3, own_lanes : own_lanes + block_rows],
+        self_sum[:, :own_lanes],
+        self_sum[:, own_lanes : 2 * own_lanes],
+        self_sum[:, 2 * own_lanes :],
+        cross_parts[4],
+        cross_parts[1],
+        cross_parts[2],
+        cross_parts[3],
+        cross_parts[0],
+        jnp.concatenate([expand.result(), expand_x.result()], axis=1),
+        jnp.concatenate(contract_sums, axis=1).astype(F32),
+        norm_chain.result()[0],
     )
 
 

time: 398 us -> 342 us (0.86)
  waiting for transfers between devices: 66.3 us -> 40.3 us
  starting transfers between devices: 59.2 us -> 37.2 us
  Pallas kernels: 213 us -> 197 us
    ppermute x30 -> x24, waiting for transfers between devices: 57.2 us -> 35.2 us  [permute(): return lax.ppermute(tensor, 'row', pairs)]
    reduce_scatter x3 -> x4, starting transfers between devices: 11.6 us -> 0.16 us  [group_sum(): lax.psum_scatter(tensor, 'row', scatter_dimension=0, tiled=True, axis_ind...]
    pallas_call x2, Pallas kernels: 49.4 us -> 38.1 us  [attention_forward(): return call(*operands, *weights, norms)]
    ppermute x30 -> x24, starting transfers between devices: 43.6 us -> 32.8 us  [permute(): return lax.ppermute(tensor, 'row', pairs)]
    pallas_call x1, Pallas kernels: 29.5 us -> 20.7 us  [feed_forward(): return call(core, low, normal, w_expand, w_contract, norms, out_grad)]
    pallas_call x7 -> x6, Pallas kernels: 73 us -> 81.1 us  [the longest x3 45.2 us: weight_grads(): results = during(call(at_place, *flat), *travelling)]
    unnamed x84 -> x74, local copies, waits for them, and re-layouts: 4.57 us -> 8.9 us
    convert_element_type x25 -> x20, other arithmetic: 10.7 us -> 15 us  [the longest x16 13.1 us: advance(): self.sum_rows(slice(k * rows, (k + 1) * rows)).astype(BF)]
  transfers between devices with their start and end apart: 49 -> 44, of which waited for: 14 -> 10; matrix products, arithmetic and copies ran while one was open for 8% -> 10% of each run, Pallas kernels for 40% -> 53%
where the time goes in v3:
time: 342 us; the launch traced here: 336 us
  Pallas kernels  197 us (58%)
  waiting for transfers between devices  40.3 us (12%)
  starting transfers between devices  37.2 us (11%)
  other arithmetic  31.5 us (9%)
  local copies, waits for them, and re-layouts  15.8 us (5%)
  between operations  14.6 us (4%)
    pallas_call x2, Pallas kernels, attention_backward(): call(core, row_seg.reshape(rows, 1), key_seg.reshape(1, keys), low_grad,...  56.9 us
    pallas_call x3, Pallas kernels, weight_grads(): results = during(call(at_place, *flat), *travelling)  45.2 us
    pallas_call x2, Pallas kernels, attention_forward(): return call(*operands, *weights, norms)  38.1 us
    ppermute x24, waiting for transfers between devices, permute(): return lax.ppermute(tensor, 'row', pairs)  35.2 us
    ppermute x24, starting transfers between devices, permute(): return lax.ppermute(tensor, 'row', pairs)  32.8 us
    pallas_call x2, Pallas kernels, feed_backward(): return call(core, low_grad, w_contract, slope, w_expand, *rest)  23.6 us
    pallas_call x1, Pallas kernels, feed_forward(): return call(core, low, normal, w_expand, w_contract, norms, out_grad)  20.7 us
    convert_element_type x16, other arithmetic, advance(): self.sum_rows(slice(k * rows, (k + 1) * rows)).astype(BF)  13.1 us
  transfers between devices with their start and end apart: 44, of which 10 were waited for; matrix products, arithmetic and copies ran while one was open for 10% of the time, Pallas kernels for 53%

profile of v3, /device:TPU:0, one launch (start us, length us, event | category | flops | bytes accessed | tf_op | source)
XLA Modules:
  0.0 336.2 jit_solution(10764376081194400998)
XLA Ops:
  8.8 18.2 %shard_map.425 = (bf16[512,1024]{1,0:T(8,128)(2,1)}, bf16[512,1024]{1,0:T(8,128)(2,1)}, bf16[512,1024]{1,0:T(8,128)(2,1)}, bf16[512,1024]{1,0:T(8,128)(2,1)}, f3...) custom-call(s32[512,1]{1,0:T(8,128)} %copy.53.refs_0_, ...), custom_call_target="tpu_custom_call" | custom-call | flops 1 | bytes 31457280 | tf_op jit(solution)/shard_map/pallas_call | solution.py:242
  28.5 5.0 %collective-permute-done = s32[256]{0:T(256)S(1)} collective-permute-done((s32[256]{0:T(256)S(1)}, s32[256]{0:T(256)S(1)}, u32[]{:S(2)}, u32[]{:S(2)}) %collective-permute-start) | collective-permute-done | bytes 1056 | tf_op jit(solution)/shard_map/ppermute | solution.py:763
  34.9 19.9 %shard_map.426 = (bf16[512,1024]{1,0:T(8,128)(2,1)}, bf16[512,1024]{1,0:T(8,128)(2,1)}, bf16[512,1024]{1,0:T(8,128)(2,1)}, bf16[512,1024]{1,0:T(8,128)(2,1)}, f3...) custom-call(s32[512,1]{1,0:T(8,128)} %copy.53.refs_0_, ...), custom_call_target="tpu_custom_call" | custom-call | flops 1 | bytes 31457280 | tf_op jit(solution)/shard_map/pallas_call | solution.py:242
  56.5 20.7 %shard_map.427 = (bf16[512,4096]{1,0:T(8,128)(2,1)}, bf16[512,4096]{1,0:T(8,128)(2,1)}, bf16[512,1024]{1,0:T(8,128)(2,1)}, f32[512,1024]{1,0:T(8,128)}, bf16[512...) custom-call(s32[1]{0:T(128)} %bitcast.core, ...), custom_call_target="tpu_custom_call" | custom-call | flops 1 | bytes 35651584 | tf_op jit(solution)/shard_map/pallas_call | solution.py:333
  77.9 9.5 %shard_map.428 = (bf16[512,2048]{1,0:T(8,128)(2,1)}, f32[512,1024]{1,0:T(8,128)}) custom-call(s32[1]{0:T(128)} %bitcast.core, bf16[512,1024]{1,0:T(8,128)(2,1)} %get-tuple-element.205.refs_0_, bf16[4096,1024]{1,0:T(8,128)(2,1)} %refs_1_.3, bf16[512,4096]{1,0:T(8,128)(2,1)} %get-tuple-element.196.refs_2_, bf16[1024,4096]{1,0:T(8,128)(2,1)} %refs_3_.7), custom_call_target="tpu_custom_call" | custom-call | flops 1 | bytes 18874368 | tf_op jit(solution)/shard_map/pallas_call | solution.py:428
  91.7 12.2 %shard_map.429 = (bf16[2048,256]{1,0:T(8,128)(2,1)}, bf16[2048,256]{1,0:T(8,128)(2,1)}, bf16[2048,256]{1,0:T(8,128)(2,1)}, bf16[2048,256]{1,0:T(8,128)(2,1)}) custom-call(s32[32]{0:T(128)} %pad_add_fusion.1.at_chunk, bf16[512,4096]{1,0:T(8,128)(2,1)} %get-tuple-element.195.own, bf16[512,4096]{1,0:T(8,128)(2,1)} %collective-permute-done.7.other, ...), custom_call_target="tpu_custom_call" | custom-call | flops 1 | bytes 20971520 | tf_op jit(solution)/shard_map/pallas_call | solution.py:888
  104.0 2.6 collective-permute-start.10
  108.7 14.1 %shard_map.430 = (bf16[512,2048]{1,0:T(8,128)(2,1)}, f32[512,1024]{1,0:T(8,128)}, bf16[512,1024]{1,0:T(8,128)(2,1)}, bf16[512,512]{1,0:T(8,128)(2,1)}, bf16[512,512]{1,0:T(8,128)(2,1)}, /*index=5*/f32[2,1024]{1,0:T(2,128)}) custom-call(s32[1]{0:T(128)} %bitcast.core, bf16[512,1024]{1,0:T(8,128)(2,1)} %get-tuple-element.205.refs_0_, ...), custom_call_target="tpu_custom_call" | custom-call | flops 1 | bytes 18874368 | tf_op jit(solution)/shard_map/pallas_call | solution.py:428
  124.2 9.8 %shard_map.431 = (bf16[1024,1024]{1,0:T(8,128)(2,1)}, bf16[512,1024]{1,0:T(8,128)(2,1)}, bf16[512,1024]{1,0:T(8,128)(2,1)}) custom-call(s32[32]{0:T(128)} %get-tuple-element.369.at_place, bf16[512,1024]{1,0:T(8,128)(2,1)} %get-tuple-element.180.low.refs_0_, bf16[512,1024]{1,0:T(8,128)(2,1)} %copy-done.14, bf16[1,512,2048]{2,1,0:T(8,128)(2,1)} %bitcast.39, ...), custom_call_target="tpu_custom_call" | custom-call | flops 1 | bytes 16777216 | tf_op jit(solution)/shard_map/pallas_call | solution.py:841
  137.3 2.3 add_convert_fusion.13
  140.2 1.6 pad_maximum_fusion.2
  141.9 31.5 %shard_map.432 = (bf16[3,512,512]{2,1,0:T(8,128)(2,1)}, bf16[3,512,512]{2,1,0:T(8,128)(2,1)}, f32[512,1024]{1,0:T(8,128)}, bf16[512,1024]{1,0:T(8,128)(2,1)}, bf...) custom-call(s32[1]{0:T(128)} %bitcast.core, ...), custom_call_target="tpu_custom_call" | custom-call | flops 1 | bytes 46137344 | tf_op jit(solution)/shard_map/pallas_call | solution.py:622
  178.9 1.6 collective-permute-start.20
  181.9 2.0 add_convert_fusion.8
  185.2 25.8 %shard_map.433 = (bf16[512,1280]{1,0:T(8,128)(2,1)}, bf16[512,1280]{1,0:T(8,128)(2,1)}, bf16[512,1280]{1,0:T(8,128)(2,1)}, bf16[512,1280]{1,0:T(8,128)(2,1)}) custom-call(s32[32]{0:T(128)} %get-tuple-element.368.at_place, bf16[512,1024]{1,0:T(8,128)(2,1)} %get-tuple-element.260.refs_7_.refs_0_, bf16[512,1024]{1,0:T(8,128)(2,1)} %copy-done.20, ...), custom_call_target="tpu_custom_call" | custom-call | flops 1 | bytes 16777216 | tf_op jit(solution)/shard_map/pallas_call | solution.py:841
  215.4 1.8 fusion.1
  218.1 2.0 add_convert_fusion.6
  220.3 25.4 %shard_map.434 = (bf16[3,512,512]{2,1,0:T(8,128)(2,1)}, bf16[3,512,512]{2,1,0:T(8,128)(2,1)}, bf16[512,1024]{1,0:T(8,128)(2,1)}) custom-call(s32[1]{0:T(128)} %bitcast.core, s32[512,1]{1,0:T(8,128)} %copy.53.refs_0_, s32[1,512]{1,0:T(1,128)} %bitcast.50, bf16[512,1024]{1,0:T(8,128)(2,1)} %get-tuple-element.281.refs_2_, bf16[1024,1024]{1,0:T(8,128)(2,1)} %refs_3_.9, ...), custom_call_target="tpu_custom_call" | custom-call | flops 1 | bytes 46137344 | tf_op jit(solution)/shard_map/pallas_call | solution.py:622
  245.6 2.0 collective-permute-done.24
  249.2 2.6 add_convert_fusion.2
  256.5 1.7 add_convert_fusion.24
  263.2 9.5 %shard_map.435 = (bf16[512,768]{1,0:T(8,128)(2,1)}, bf16[512,768]{1,0:T(8,128)(2,1)}, bf16[512,768]{1,0:T(8,128)(2,1)}, bf16[512,768]{1,0:T(8,128)(2,1)}) custom-call(s32[32]{0:T(128)} %pad_add_fusion.4.at_place, bf16[512,1024]{1,0:T(8,128)(2,1)} %refs_0_, bf16[512,1024]{1,0:T(8,128)(2,1)} %copy-done.17, bf16[3,512,512]{2,1,0:T(8,128)(2,1)} %get-tuple-element.303.refs_2_, ...), custom_call_target="tpu_custom_call" | custom-call | flops 1 | bytes 16777216 | tf_op jit(solution)/shard_map/pallas_call | solution.py:841
  277.2 2.6 collective-permute-start.39
  283.4 11.7 %collective-permute-done.31 = bf16[512,768]{1,0:T(8,128)(2,1)S(1)} collective-permute-done((bf16[512,768]{1,0:T(8,128)(2,1)}, bf16[512,768]{1,0:T(8,128)(2,1)S(1)}, u32[]{:S(2)}, u32[]{:S(2)}) %collective-permute-start.31) | collective-permute-done | bytes 786464 | tf_op jit(solution)/shard_map/ppermute | solution.py:690
  296.9 3.0 collective-permute-done.35
  301.8 4.8 %collective-permute-done.32 = bf16[256,768]{1,0:T(8,128)(2,1)S(1)} collective-permute-done((bf16[256,768]{1,0:T(8,128)(2,1)S(1)}, bf16[256,768]{1,0:T(8,128)(2,1)S(1)}, u32[]{:S(2)}, u32[]{:S(2)}) %collective-permute-start.32) | collective-permute-done | bytes 393248 | tf_op jit(solution)/shard_map/ppermute | solution.py:690
  306.7 1.6 collective-permute-start.33
  309.7 5.8 %collective-permute-done.33 = bf16[128,768]{1,0:T(8,128)(2,1)S(1)} collective-permute-done((bf16[128,768]{1,0:T(8,128)(2,1)S(1)}, bf16[128,768]{1,0:T(8,128)(2,1)S(1)}, u32[]{:S(2)}, u32[]{:S(2)}) %collective-permute-start.33) | collective-permute-done | bytes 196640 | tf_op jit(solution)/shard_map/ppermute | solution.py:690
  315.5 1.9 collective-permute-start.34
  317.4 1.7 collective-permute-done.37
  319.1 2.4 collective-permute-start.38
  321.6 3.6 %collective-permute-done.34 = bf16[64,768]{1,0:T(8,128)(2,1)S(1)} collective-permute-done((bf16[64,768]{1,0:T(8,128)(2,1)S(1)}, bf16[64,768]{1,0:T(8,128)(2,1)S(1)}, u32[]{:S(2)}, u32[]{:S(2)}) %collective-permute-start.34) | collective-permute-done | bytes 98336 | tf_op jit(solution)/shard_map/ppermute | solution.py:690
  (205 shorter events, 60.4 us)
Async XLA Ops:
  7.2 203.9 %reduce-scatter.5.cloned.1.call-start = ((), (), s32[]{:S(2)}) async-start(), calls=%async_computation.4 | async-start | bytes 2621440 | tf_op jit(solution)/shard_map/reduce_scatter | solution.py:693
  26.9 27.8 %collective-permute-start.3 = (bf16[512,1024]{1,0:T(8,128)(2,1)}, bf16[512,1024]{1,0:T(8,128)(2,1)S(1)}, u32[]{:S(2)}, u32[]{:S(2)}) collective-permute-start(bf16[512,1024]{1,0:T(8,128)(2,1)} %get-tuple-element.179.refs_6_.refs_7_), channel_id=1, source_target_pairs={{0,1},{1,0},{2,3},{3,2},{4,5},{5,4},{6,7},{7,6},{8,9},{9,8},{10,11... | collective-permute-start | bytes 3145736 | tf_op jit(solution)/shard_map/ppermute | solution.py:763
  27.5 27.3 %collective-permute-start.4 = (bf16[512,1024]{1,0:T(8,128)(2,1)}, bf16[512,1024]{1,0:T(8,128)(2,1)S(1)}, u32[]{:S(2)}, u32[]{:S(2)}) collective-permute-start(bf16[512,1024]{1,0:T(8,128)(2,1)} %get-tuple-element.169.refs_2_), channel_id=1, source_target_pairs={{0,1},{1,0},{2,3},{3,2},{4,5},{5,4},{6,7},{7,6},{8,9},{9,8},{10,11... | collective-permute-start | bytes 3145736 | tf_op jit(solution)/shard_map/ppermute | solution.py:763
  27.5 27.3 %collective-permute-start.2 = (bf16[512,1024]{1,0:T(8,128)(2,1)S(1)}, bf16[512,1024]{1,0:T(8,128)(2,1)S(1)}, u32[]{:S(2)}, u32[]{:S(2)}) collective-permute-start(bf16[512,1024]{1,0:T(8,128)(2,1)S(1)} %copy-done), channel_id=1, source_target_pairs={{0,1},{1,0},{2,3},{3,2},{4,5},{5,4},{6,7},{7,6},{8,9},{9,8},{10,11... | collective-permute-start | bytes 3145736 | tf_op jit(solution)/shard_map/ppermute | solution.py:763
  55.9 21.2 %collective-permute-start.5 = (bf16[512,1024]{1,0:T(8,128)(2,1)}, bf16[512,1024]{1,0:T(8,128)(2,1)S(1)}, u32[]{:S(2)}, u32[]{:S(2)}) collective-permute-start(bf16[512,1024]{1,0:T(8,128)(2,1)} %get-tuple-element.260.refs_7_.refs_0_), channel_id=1, source_target_pairs={{0,1},{1,0},{2,3},{3,2},{4,5},{5,4},{6,7},{7,6},{8,9},{9,8},{10,11... | collective-permute-start | bytes 3145736 | tf_op jit(solution)/shard_map/ppermute | solution.py:763
  56.3 20.9 %collective-permute-start.6 = (bf16[512,1024]{1,0:T(8,128)(2,1)}, bf16[512,1024]{1,0:T(8,128)(2,1)S(1)}, u32[]{:S(2)}, u32[]{:S(2)}) collective-permute-start(bf16[512,1024]{1,0:T(8,128)(2,1)} %get-tuple-element.180.low.refs_0_), channel_id=1, source_target_pairs={{0,1},{1,0},{2,3},{3,2},{4,5},{5,4},{6,7},{7,6},{8,9},{9,8},{10,11... | collective-permute-start | bytes 3145736 | tf_op jit(solution)/shard_map/ppermute | solution.py:763
  88.2 34.6 %collective-permute-start.9 = (bf16[512,2048]{1,0:T(8,128)(2,1)}, bf16[512,2048]{1,0:T(8,128)(2,1)S(1)}, u32[]{:S(2)}, u32[]{:S(2)}) collective-permute-start(bf16[512,2048]{1,0:T(8,128)(2,1)} %get-tuple-element.215), channel_id=1, source_target_pairs={{0,1},{1,0},{2,3},{3,2},{4,5},{5,4},{6,7},{7,6},{8,9},{9,8},{10,11... | collective-permute-start | bytes 6291464 | tf_op jit(solution)/shard_map/ppermute | solution.py:763
  104.0 30.0 %collective-permute-start.10 = (bf16[2048,256]{1,0:T(8,128)(2,1)}, bf16[2048,256]{1,0:T(8,128)(2,1)}, u32[]{:S(2)}, u32[]{:S(2)}) collective-permute-start(bf16[2048,256]{1,0:T(8,128)(2,1)} %get-tuple-element.203), channel_id=1, source_target_pairs={{0,2},{2,0},{4,6},{6,4},{8,10},{10,8},{12,14},{14,12},{16,18},{18,... | collective-permute-start | bytes 3145736 | tf_op jit(solution)/shard_map/ppermute | solution.py:690
  106.6 27.4 %collective-permute-start.11 = (bf16[2048,256]{1,0:T(8,128)(2,1)}, bf16[2048,256]{1,0:T(8,128)(2,1)S(1)}, u32[]{:S(2)}, u32[]{:S(2)}) collective-permute-start(bf16[2048,256]{1,0:T(8,128)(2,1)} %get-tuple-element.204), channel_id=1, source_target_pairs={{0,4},{2,6},{4,0},{6,2},{8,12},{10,14},{12,8},{14,10},{16,20},{18,... | collective-permute-start | bytes 3145736 | tf_op jit(solution)/shard_map/ppermute | solution.py:690
  134.0 121.4 %reduce-scatter.11.cloned.1.call-start = ((), (), s32[]{:S(2)}) async-start(), calls=%async_computation.7 | async-start | bytes 1310720 | tf_op jit(solution)/shard_map/reduce_scatter | solution.py:693
  134.1 39.3 %collective-permute-start.14 = (bf16[512,1024]{1,0:T(8,128)(2,1)}, bf16[512,1024]{1,0:T(8,128)(2,1)}, u32[]{:S(2)}, u32[]{:S(2)}) collective-permute-start(bf16[512,1024]{1,0:T(8,128)(2,1)} %get-tuple-element.226), channel_id=1, source_target_pairs={{0,2},{2,0},{4,6},{6,4},{8,10},{10,8},{12,14},{14,12},{16,18},{18,... | collective-permute-start | bytes 3145736 | tf_op jit(solution)/shard_map/ppermute | solution.py:690
  136.3 37.1 %collective-permute-start.13 = (bf16[1024,256]{1,0:T(8,128)(2,1)}, bf16[1024,256]{1,0:T(8,128)(2,1)S(1)}, u32[]{:S(2)}, u32[]{:S(2)}) collective-permute-start(bf16[1024,256]{1,0:T(8,128)(2,1)} %get-tuple-element.333), channel_id=1, source_target_pairs={{0,2},{2,0},{4,6},{6,4},{8,10},{10,8},{12,14},{14,12},{16,18},{18,... | collective-permute-start | bytes 1572872 | tf_op jit(solution)/shard_map/ppermute | solution.py:690
  139.6 33.8 %collective-permute-start.12 = (bf16[1024,256]{1,0:T(8,128)(2,1)}, bf16[1024,256]{1,0:T(8,128)(2,1)S(1)}, u32[]{:S(2)}, u32[]{:S(2)}) collective-permute-start(bf16[1024,256]{1,0:T(8,128)(2,1)} %get-tuple-element.335), channel_id=1, source_target_pairs={{0,4},{2,6},{4,0},{6,2},{8,12},{10,14},{12,8},{14,10},{16,20},{18,... | collective-permute-start | bytes 1572872 | tf_op jit(solution)/shard_map/ppermute | solution.py:690
  141.9 42.1 %collective-permute-start.17 = (bf16[512,512]{1,0:T(8,128)(2,1)}, bf16[512,512]{1,0:T(8,128)(2,1)}, u32[]{:S(2)}, u32[]{:S(2)}) collective-permute-start(bf16[512,512]{1,0:T(8,128)(2,1)} %get-tuple-element.265), channel_id=1, source_target_pairs={{0,1},{1,0},{2,3},{3,2},{4,5},{5,4},{6,7},{7,6},{8,9},{9,8},{10,11... | collective-permute-start | bytes 1572872 | tf_op jit(solution)/shard_map/ppermute | solution.py:763
  178.9 82.2 %reduce-scatter.9.cloned.1.call-start = ((), (), s32[]{:S(2)}) async-start(), calls=%async_computation.6 | async-start | bytes 655360 | tf_op jit(solution)/shard_map/reduce_scatter | solution.py:693
  178.9 32.1 %collective-permute-start.20 = (bf16[256,1024]{1,0:T(8,128)(2,1)S(1)}, bf16[256,1024]{1,0:T(8,128)(2,1)}, u32[]{:S(2)}, u32[]{:S(2)}) collective-permute-start(bf16[256,1024]{1,0:T(8,128)(2,1)S(1)} %get-tuple-element.331), channel_id=1, source_target_pairs={{0,4},{2,6},{4,0},{6,2},{8,12},{10,14},{12,8},{14,10},{16,20},{18,... | collective-permute-start | bytes 1572872 | tf_op jit(solution)/shard_map/ppermute | solution.py:690
  181.4 29.6 %collective-permute-start.21 = (bf16[8,3,64]{2,1,0:T(4,128)(2,1)S(1)}, bf16[8,3,64]{2,1,0:T(4,128)(2,1)S(1)}, u32[]{:S(2)}, u32[]{:S(2)}) collective-permute-start(bf16[8,3,64]{2,1,0:T(4,128)(2,1)S(1)} %get-tuple-element.365), channel_id=1, source_target_pairs={{0,4},{2,6},{4,0},{6,2},{8,12},{10,14},{12,8},{14,10},{16,20},{18,... | collective-permute-start | bytes 9224 | tf_op jit(solution)/shard_map/ppermute | solution.py:690
  211.1 36.6 %collective-permute-start.22 = (bf16[512,1280]{1,0:T(8,128)(2,1)}, bf16[512,1280]{1,0:T(8,128)(2,1)S(1)}, u32[]{:S(2)}, u32[]{:S(2)}) collective-permute-start(bf16[512,1280]{1,0:T(8,128)(2,1)} %get-tuple-element.274), channel_id=1, source_target_pairs={{0,2},{2,0},{4,6},{6,4},{8,10},{10,8},{12,14},{14,12},{16,18},{18,... | collective-permute-start | bytes 3932168 | tf_op jit(solution)/shard_map/ppermute | solution.py:690
  212.1 35.5 %collective-permute-start.23 = (bf16[512,1280]{1,0:T(8,128)(2,1)}, bf16[512,1280]{1,0:T(8,128)(2,1)S(1)}, u32[]{:S(2)}, u32[]{:S(2)}) collective-permute-start(bf16[512,1280]{1,0:T(8,128)(2,1)} %get-tuple-element.275), channel_id=1, source_target_pairs={{0,4},{2,6},{4,0},{6,2},{8,12},{10,14},{12,8},{14,10},{16,20},{18,... | collective-permute-start | bytes 3932168 | tf_op jit(solution)/shard_map/ppermute | solution.py:690
  214.3 31.3 %collective-permute-start.25 = (bf16[4,3,64]{2,1,0:T(4,128)(2,1)S(1)}, bf16[4,3,64]{2,1,0:T(4,128)(2,1)S(1)}, u32[]{:S(2)}, u32[]{:S(2)}) collective-permute-start(bf16[4,3,64]{2,1,0:T(4,128)(2,1)S(1)} %get-tuple-element.363), channel_id=1, source_target_pairs={{0,2},{2,0},{4,6},{6,4},{8,10},{10,8},{12,14},{14,12},{16,18},{18,... | collective-permute-start | bytes 4616 | tf_op jit(solution)/shard_map/ppermute | solution.py:690
  217.1 30.5 %collective-permute-start.24 = (bf16[128,1024]{1,0:T(8,128)(2,1)}, bf16[128,1024]{1,0:T(8,128)(2,1)}, u32[]{:S(2)}, u32[]{:S(2)}) collective-permute-start(bf16[128,1024]{1,0:T(8,128)(2,1)} %get-tuple-element.354), channel_id=1, source_target_pairs={{0,2},{2,0},{4,6},{6,4},{8,10},{10,8},{12,14},{14,12},{16,18},{18,... | collective-permute-start | bytes 786440 | tf_op jit(solution)/shard_map/ppermute | solution.py:690
  220.2 107.4 %reduce-scatter.7.cloned.1.call-start = ((), (), s32[]{:S(2)}) async-start(), calls=%async_computation.5 | async-start | bytes 1638400 | tf_op jit(solution)/shard_map/reduce_scatter | solution.py:693
  249.1 12.9 %collective-permute-start.26 = (bf16[3,512,512]{2,1,0:T(8,128)(2,1)}, bf16[3,512,512]{2,1,0:T(8,128)(2,1)S(1)}, u32[]{:S(2)}, u32[]{:S(2)}) collective-permute-start(bf16[3,512,512]{2,1,0:T(8,128)(2,1)} %get-tuple-element.304), channel_id=1, source_target_pairs={{0,1},{1,0},{2,3},{3,2},{4,5},{5,4},{6,7},{7,6},{8,9},{9,8},{10,11... | collective-permute-start | bytes 4718600 | tf_op jit(solution)/shard_map/ppermute | solution.py:763
  251.8 21.9 %collective-permute-start.28 = (bf16[256,1280]{1,0:T(8,128)(2,1)}, bf16[256,1280]{1,0:T(8,128)(2,1)}, u32[]{:S(2)}, u32[]{:S(2)}) collective-permute-start(bf16[256,1280]{1,0:T(8,128)(2,1)} %get-tuple-element.327), channel_id=1, source_target_pairs={{0,2},{2,0},{4,6},{6,4},{8,10},{10,8},{12,14},{14,12},{16,18},{18,... | collective-permute-start | bytes 1966088 | tf_op jit(solution)/shard_map/ppermute | solution.py:690
  253.9 19.7 %collective-permute-start.27 = (bf16[256,1280]{1,0:T(8,128)(2,1)}, bf16[256,1280]{1,0:T(8,128)(2,1)}, u32[]{:S(2)}, u32[]{:S(2)}) collective-permute-start(bf16[256,1280]{1,0:T(8,128)(2,1)} %get-tuple-element.329), channel_id=1, source_target_pairs={{0,4},{2,6},{4,0},{6,2},{8,12},{10,14},{12,8},{14,10},{16,20},{18,... | collective-permute-start | bytes 1966088 | tf_op jit(solution)/shard_map/ppermute | solution.py:690
  258.2 15.5 %collective-permute-start.29 = (bf16[64,1024]{1,0:T(8,128)(2,1)}, bf16[64,1024]{1,0:T(8,128)(2,1)S(1)}, u32[]{:S(2)}, u32[]{:S(2)}) collective-permute-start(bf16[64,1024]{1,0:T(8,128)(2,1)} %get-tuple-element.352), channel_id=1, source_target_pairs={{0,4},{2,6},{4,0},{6,2},{8,12},{10,14},{12,8},{14,10},{16,20},{18,... | collective-permute-start | bytes 393224 | tf_op jit(solution)/shard_map/ppermute | solution.py:690
  258.7 14.0 %collective-permute-start.30 = (bf16[2,3,64]{2,1,0:T(4,128)(2,1)S(1)}, bf16[2,3,64]{2,1,0:T(4,128)(2,1)S(1)}, u32[]{:S(2)}, u32[]{:S(2)}) collective-permute-start(bf16[2,3,64]{2,1,0:T(4,128)(2,1)S(1)} %get-tuple-element.367), channel_id=1, source_target_pairs={{0,8},{2,10},{4,12},{6,14},{8,0},{10,2},{12,4},{14,6},{16,24},{18,... | collective-permute-start | bytes 2312 | tf_op jit(solution)/shard_map/ppermute | solution.py:690
  276.2 19.0 %collective-permute-start.31 = (bf16[512,768]{1,0:T(8,128)(2,1)}, bf16[512,768]{1,0:T(8,128)(2,1)S(1)}, u32[]{:S(2)}, u32[]{:S(2)}) collective-permute-start(bf16[512,768]{1,0:T(8,128)(2,1)} %get-tuple-element.310), channel_id=1, source_target_pairs={{0,2},{2,0},{4,6},{6,4},{8,10},{10,8},{12,14},{14,12},{16,18},{18,... | collective-permute-start | bytes 2359304 | tf_op jit(solution)/shard_map/ppermute | solution.py:690
  277.2 24.0 %collective-permute-start.39 = (bf16[1,3,64]{2,1,0:T(4,128)(2,1)S(1)}, bf16[1,3,64]{2,1,0:T(4,128)(2,1)S(1)}, u32[]{:S(2)}, u32[]{:S(2)}) collective-permute-start(bf16[1,3,64]{2,1,0:T(4,128)(2,1)S(1)} %add_convert_fusion.35), channel_id=1, source_target_pairs={{0,16},{2,18},{4,20},{6,22},{8,24},{10,26},{12,28},{14,30},{16,0},... | collective-permute-start | bytes 1160 | tf_op jit(solution)/shard_map/ppermute | solution.py:690
  279.9 20.1 %collective-permute-start.35 = (bf16[512,768]{1,0:T(8,128)(2,1)}, bf16[512,768]{1,0:T(8,128)(2,1)S(1)}, u32[]{:S(2)}, u32[]{:S(2)}) collective-permute-start(bf16[512,768]{1,0:T(8,128)(2,1)} %get-tuple-element.320), channel_id=1, source_target_pairs={{0,4},{2,6},{4,0},{6,2},{8,12},{10,14},{12,8},{14,10},{16,20},{18,... | collective-permute-start | bytes 2359304 | tf_op jit(solution)/shard_map/ppermute | solution.py:690
  295.3 11.3 %collective-permute-start.32 = (bf16[256,768]{1,0:T(8,128)(2,1)S(1)}, bf16[256,768]{1,0:T(8,128)(2,1)S(1)}, u32[]{:S(2)}, u32[]{:S(2)}) collective-permute-start(bf16[256,768]{1,0:T(8,128)(2,1)S(1)} %get-tuple-element.339), channel_id=1, source_target_pairs={{0,4},{2,6},{4,0},{6,2},{8,12},{10,14},{12,8},{14,10},{16,20},{18,... | collective-permute-start | bytes 1179656 | tf_op jit(solution)/shard_map/ppermute | solution.py:690
  308.4 10.6 %collective-permute-start.37 = (bf16[128,768]{1,0:T(8,128)(2,1)S(1)}, bf16[128,768]{1,0:T(8,128)(2,1)S(1)}, u32[]{:S(2)}, u32[]{:S(2)}) collective-permute-start(bf16[128,768]{1,0:T(8,128)(2,1)S(1)} %get-tuple-element.343), channel_id=1, source_target_pairs={{0,8},{2,10},{4,12},{6,14},{8,0},{10,2},{12,4},{14,6},{16,24},{18,... | collective-permute-start | bytes 589832 | tf_op jit(solution)/shard_map/ppermute | solution.py:690
  (49 other events, 425.0 us)
Sparse Core Ops, SparseCore 0:
  134.2 43.2 reduce-scatter.4
  179.8 27.1 reduce-scatter.10
  220.3 21.4 reduce-scatter.8
  282.7 31.2 reduce-scatter.6
